TPU v7x, 32 devices: a whole 2x2x4 slice. The times are simulated.
32 devices in a mesh: gy: 2 (over x), gz: 16 (over z, y, core).
Axes of the slice: x: 2, y: 2, z: 4, core: 2. Of those that a mesh axis runs over, the one named last changes fastest.
Arguments:
- residual: float32 [128, 2, 8, 1024], P('gz', None, None, 'gy'), may hold values from -130 to 130
- direction_prev: float32 [128, 2, 8, 1024], P('gz', None, None, 'gy'), may hold values from -12 to 12
- phase_labels: int32 [128, 1024], P('gz', 'gy'), may hold values from 0 to 2
- phase_diffusivity: float32 [3], replicated, may hold values from 0.1 to 1
- x_eigen: float32 [8], replicated, may hold values from 0.00390625 to 2
- rz_prev: float32 [1], replicated, may hold values from 4194304 to 62914560
Outputs:
- preconditioned: float32 [128, 2, 8, 1024], P('gz', None, None, 'gy')
- direction: float32 [128, 2, 8, 1024], P('gz', None, None, 'gy')
- rz_total: float32 [1], replicated
All inputs are finite; a program needn't handle non-finite values.
Results may differ from a plain program's by a relative error of at most 0.0003.
Values sent between devices are 32-bit elements; how exact they have to be, the bound alone decides.
No kernel may reach another device: no remote copies, remote signals or barrier semaphores. Data moves between devices by JAX's collectives and lax.ppermute only.
A program may use at most 64 MiB of HBM per device.

v0:
```python
import functools

import jax
import jax.numpy as jnp
import numpy as np
from jax import lax
from jax.experimental import pallas as pl
from jax.experimental.pallas import tpu as pltpu
from jax.sharding import PartitionSpec as P

LANES = 128
SUBS = 8
HALF = 4
VMEM = pl.BlockSpec(memory_space=pltpu.VMEM)
SMEM = pl.BlockSpec(memory_space=pltpu.SMEM)


def split_bf16(table):
    high = table.astype(jnp.bfloat16)
    low = (table - np.asarray(high, np.float64)).astype(jnp.bfloat16)
    return np.stack([np.asarray(high), np.asarray(low)])


def lane_transform(sign):
    ids = np.arange(LANES)
    angle = 2.0 * np.pi * (ids[:, None] * ids[None, :] % LANES) / LANES
    cosine, sine = np.cos(angle), sign * np.sin(angle)
    return split_bf16(np.block([[cosine, sine], [-sine, cosine]]))


def twiddles(radix):
    angle = 2.0 * np.pi * np.arange(radix)[:, None] * np.arange(LANES)[None, :] / (radix * LANES)
    return np.stack([np.cos(angle), np.sin(angle)]).astype(np.float32)


def y_eigen(radix):
    wave = np.arange(radix)[:, None] + radix * np.arange(LANES)[None, :]
    return (4.0 * np.sin(np.pi * wave / (radix * LANES)) ** 2).astype(np.float32)


def power(base, exponent):
    result = None
    while exponent:
        if exponent & 1:
            result = base if result is None else result * base
        exponent >>= 1
        if exponent:
            base = base * base
    return result


def small_dft(re, im, sign):
    count = len(re)
    if count == 1:
        return re, im
    even_re, even_im = small_dft(re[0::2], im[0::2], sign)
    odd_re, odd_im = small_dft(re[1::2], im[1::2], sign)
    out_re, out_im = [None] * count, [None] * count
    for i in range(count // 2):
        angle = 2.0 * np.pi * i / count
        c, s = float(np.cos(angle)), float(sign * np.sin(angle))
        if i == 0:
            a, b = odd_re[i], odd_im[i]
        elif 4 * i == count:
            a, b = (odd_im[i], -odd_re[i]) if sign < 0 else (-odd_im[i], odd_re[i])
        else:
            a = odd_re[i] * c - odd_im[i] * s
            b = odd_re[i] * s + odd_im[i] * c
        out_re[i], out_im[i] = even_re[i] + a, even_im[i] + b
        out_re[i + count // 2], out_im[i + count // 2] = even_re[i] - a, even_im[i] - b
    return out_re, out_im


def lane_product(re, im, table_ref):
    count, shape = len(re), re[0].shape
    rows = int(np.prod(shape[:-1]))
    flat = jnp.concatenate(
        [jnp.concatenate([a.reshape(rows, LANES), b.reshape(rows, LANES)], axis=1) for a, b in zip(re, im)],
        axis=0,
    )
    high = flat.astype(jnp.bfloat16)
    low = (flat - high.astype(jnp.float32)).astype(jnp.bfloat16)
    dot = functools.partial(jnp.dot, preferred_element_type=jnp.float32)
    out = dot(high, table_ref[0]) + (dot(low, table_ref[0]) + dot(high, table_ref[1]))
    out_re = [out[i * rows : (i + 1) * rows, :LANES].reshape(shape) for i in range(count)]
    out_im = [out[i * rows : (i + 1) * rows, LANES:].reshape(shape) for i in range(count)]
    return out_re, out_im


def sub_ids(shape):
    return lax.broadcasted_iota(jnp.int32, shape, len(shape) - 2)


def turn(value, shift):
    shift = shift % SUBS
    return value if shift == 0 else pltpu.roll(value, shift, value.ndim - 2)


def for_targets(pieces, me):
    peers = len(pieces)
    out = []
    for s in range(peers):
        chosen = pieces[0]
        for t in range(1, peers):
            chosen = jnp.where(lax.rem(me + s, peers) == t, pieces[t], chosen)
        out.append(chosen)
    return out


def by_source(held, me):
    peers = len(held)
    out = []
    for t in range(peers):
        chosen = held[0]
        for s in range(1, peers):
            chosen = jnp.where(lax.rem(me + (peers - t), peers) == s, held[s], chosen)
        out.append(chosen)
    return out


def cell_weight(labels, diffusivity_ref):
    weight = jnp.zeros(labels.shape, jnp.float32)
    for i in range(diffusivity_ref.shape[0]):
        value = lax.rsqrt(jnp.full(labels.shape, diffusivity_ref[i], jnp.float32))
        weight = jnp.where(labels == i, value, weight)
    return weight


def mode_roots(eigen_ref, y_eigen_ref, me, kept, length):
    radix = y_eigen_ref.shape[0]
    subs = sub_ids((SUBS, LANES))
    x_part = jnp.zeros((SUBS, LANES), jnp.float32)
    for i in range(kept):
        x_part = jnp.where(lax.rem(subs, kept) == i, eigen_ref[me * kept + i], x_part)
    half_shift = 0.5 * jnp.stack([x_part + y_eigen_ref[a : a + 1, :] for a in range(radix)])
    root = jnp.sqrt(half_shift * (half_shift + 2.0))
    return 1.0 / (1.0 + half_shift + root), (0.5 / length) / root


def group_powers(decay, cells, groups, kept):
    group = sub_ids((SUBS, LANES)) // kept
    ahead = jnp.ones_like(decay)
    behind = jnp.ones_like(decay)
    bit = 1
    while bit < groups:
        factor = power(decay, cells * bit)
        ahead = ahead * jnp.where((group & bit) != 0, factor, 1.0)
        behind = behind * jnp.where((group & bit) != 0, 1.0, factor)
        bit *= 2
    return ahead, behind


def pack_kernel(groups, residual_ref, labels_ref, diffusivity_ref, *out_refs):
    cells, _, waves, planes = residual_ref.shape
    kept, inner = waves // groups, cells // groups
    me = lax.axis_index("gy")
    group = sub_ids((SUBS, LANES)) // kept
    weight = cell_weight(labels_ref[...], diffusivity_ref)
    for part in range(2):
        for a in range(planes // LANES):
            lanes = slice(a * LANES, (a + 1) * LANES)
            rows = [residual_ref[z, part, :, lanes] * weight[z : z + 1, lanes] for z in range(cells)]
            for zp in range(inner):
                pieces = []
                for t in range(groups):
                    piece = turn(rows[zp], -t * kept)
                    for zg in range(1, groups):
                        piece = jnp.where(group == zg, turn(rows[zg * inner + zp], (zg - t) * kept), piece)
                    pieces.append(piece)
                for ref, value in zip(out_refs, for_targets(pieces, me)):
                    ref[part, a, zp] = value


def forward_kernel(groups, *refs):
    held = refs[:groups]
    lane_ref, twiddle_ref, y_eigen_ref, eigen_ref = refs[groups : groups + 4]
    message_ref, local_ref, decay_ref, scale_ref = refs[groups + 4 :]
    _, block_rows, inner, _, _ = held[0].shape
    radix = block_rows * groups
    length = radix * LANES
    kept = SUBS // groups
    me = lax.axis_index("gy")
    re, im = [], []
    blocks = [by_source([ref[part] for ref in held], me) for part in range(2)]
    for t in range(groups):
        for a in range(block_rows):
            re.append(blocks[0][t][a])
            im.append(blocks[1][t][a])
    re, im = small_dft(re, im, -1.0)
    turned_re, turned_im = [], []
    for a in range(radix):
        c, s = twiddle_ref[0, a : a + 1, :], twiddle_ref[1, a : a + 1, :]
        turned_re.append(re[a] * c + im[a] * s)
        turned_im.append(im[a] * c - re[a] * s)
    re, im = lane_product(turned_re, turned_im, lane_ref)
    decay, scale = mode_roots(eigen_ref, y_eigen_ref, me, kept, length)
    decay_ref[...] = decay
    scale_ref[...] = scale
    group = sub_ids((SUBS, LANES)) // kept
    subs = sub_ids((SUBS, LANES))
    energy = jnp.zeros((SUBS, LANES), jnp.float32)
    for part, field in enumerate((re, im)):
        for a in range(radix):
            d, g = decay[a], scale[a]
            cell = [field[a][i] for i in range(inner)]
            ahead, behind = [cell[0]], [cell[-1]]
            for i in range(1, inner):
                ahead.append(cell[i] + d * ahead[-1])
                behind.append(cell[inner - 1 - i] + d * behind[-1])
            behind = behind[::-1]
            value = [ahead[i] + behind[i] - cell[i] for i in range(inner)]
            total = sum(cell[i] * value[i] for i in range(inner))
            last, first = ahead[-1], behind[0]
            from_low = jnp.zeros_like(last)
            from_high = jnp.zeros_like(first)
            low_weight, high_weight = jnp.ones_like(last), jnp.ones_like(first)
            bit = 1
            while bit < groups:
                upper = (group & bit) != 0
                step = bit * kept
                if 2 * step == SUBS:
                    other_last, other_first = turn(last, step), turn(first, step)
                else:
                    other_last = jnp.where(upper, turn(last, step), turn(last, -step))
                    other_first = jnp.where(upper, turn(first, step), turn(first, -step))
                span = power(d, inner * bit)
                joined = 2.0 * d * other_last * first
                total = total + jnp.where(upper & ((group & (bit - 1)) == 0), joined, 0.0)
                from_low = from_low + jnp.where(upper, low_weight * other_last, 0.0)
                from_high = from_high + jnp.where(upper, 0.0, high_weight * other_first)
                low_weight = low_weight * jnp.where(upper, span, 1.0)
                high_weight = high_weight * jnp.where(upper, 1.0, span)
                last = jnp.where(upper, last + span * other_last, other_last + span * last)
                first = jnp.where(upper, other_first + span * first, first + span * other_first)
                bit *= 2
            energy = energy + g * total
            message_ref[part * radix + a] = jnp.where(subs < HALF, last, first)
            for i in range(inner):
                spread = power(d, i + 1) * from_low + power(d, inner - i) * from_high
                local_ref[part, a, i] = value[i] + spread
    message_ref[2 * radix] = energy


def join(level, cells, groups, own, other, decay, scale, slab):
    radix = decay.shape[0]
    kept = SUBS // groups
    subs = sub_ids((SUBS, LANES))
    right = lax.rem(lax.shift_right_logical(slab, level), 2)
    mine = jnp.where(subs < HALF, 1, 0) != right
    energy = own[2 * radix] + other[2 * radix]
    joined, couple = [], jnp.zeros((SUBS, LANES), jnp.float32)
    for i in range(2 * radix):
        d, g = decay[i % radix], scale[i % radix]
        span = power(d, cells << level)
        mate = other[i]
        joined.append(jnp.where(mine, mate + span * own[i], own[i] + span * mate))
        couple = couple + (2.0 * g * d) * jnp.where(mine, own[i] * turn(mate, HALF), 0.0)
    couple = couple + turn(couple, HALF)
    energy = energy + jnp.where(subs < kept, couple, 0.0)
    return joined, energy


def join_kernel(level, cells, groups, own_ref, other_ref, decay_ref, scale_ref, out_ref):
    joined, energy = join(
        level, cells, groups, own_ref, other_ref, decay_ref[...], scale_ref[...], lax.axis_index("gz")
    )
    for i, value in enumerate(joined):
        out_ref[i] = value
    out_ref[len(joined)] = energy


def backward_kernel(groups, slabs, *refs):
    levels = slabs.bit_length() - 1
    own_ref, received = refs[0], refs[1 : 1 + levels]
    local_ref, decay_ref, scale_ref, lane_ref, twiddle_ref = refs[1 + levels : 6 + levels]
    out_refs, energy_refs = refs[6 + levels : 6 + levels + groups], refs[6 + levels + groups :]
    _, radix, inner, _, _ = local_ref.shape
    kept, cells = SUBS // groups, inner * groups
    me, slab = lax.axis_index("gy"), lax.axis_index("gz")
    decay, scale = decay_ref[...], scale_ref[...]
    subs = sub_ids((SUBS, LANES))
    totals, energy = join(levels - 1, cells, groups, own_ref, received[-1], decay, scale, slab)
    low = subs < HALF
    fields, walls = ([], []), jnp.zeros((SUBS, LANES), jnp.float32)
    ahead, behind = group_powers(decay, inner, groups, kept)
    for part in range(2):
        for a in range(radix):
            i, d = part * radix + a, decay[a]
            span, weight = power(d, cells), jnp.ones_like(d)
            incoming = jnp.zeros_like(d)
            for level in range(levels):
                right = lax.rem(lax.shift_right_logical(slab, level), 2)
                mine = jnp.where(low, 1, 0) != right
                incoming = incoming + jnp.where(mine, 0.0, weight * received[level][i])
                weight = weight * jnp.where(mine, 1.0, span)
                span = span * span
            far = span * d
            turned = turn(totals[i], HALF)
            image = d * (turned - far * totals[i]) / (1.0 - far * far)
            walls = walls + (scale[a] * d) * (turned * image)
            incoming = incoming - weight * image
            turned = turn(incoming, HALF)
            from_low = ahead[a] * jnp.where(low, incoming, turned)
            from_high = behind[a] * jnp.where(low, turned, incoming)
            fields[part].append(
                jnp.stack(
                    [
                        scale[a] * (local_ref[part, a, z] + power(d, z + 1) * from_low + power(d, inner - z) * from_high)
                        for z in range(inner)
                    ]
                )
            )
    energy = energy - jnp.where(lax.rem(subs, HALF) < kept, walls, 0.0)
    re, im = lane_product(fields[0], fields[1], lane_ref)
    turned_re, turned_im = [], []
    for a in range(radix):
        c, s = twiddle_ref[0, a : a + 1, :], twiddle_ref[1, a : a + 1, :]
        turned_re.append(re[a] * c - im[a] * s)
        turned_im.append(im[a] * c + re[a] * s)
    re, im = small_dft(turned_re, turned_im, 1.0)
    rows = radix // groups
    for part, field in enumerate((re, im)):
        for a in range(rows):
            pieces = [field[t * rows + a] for t in range(groups)]
            for ref, value in zip(out_refs, for_targets(pieces, me)):
                ref[part * rows + a] = value
    for ref in out_refs:
        ref[2 * rows] = jnp.stack([energy] * inner)


def unpack_kernel(groups, *refs):
    held = refs[:groups]
    labels_ref, diffusivity_ref, previous_ref, rz_prev_ref = refs[groups : groups + 4]
    out_ref, direction_ref, total_ref = refs[groups + 4 :]
    cells, _, waves, planes = out_ref.shape
    kept, inner, rows = waves // groups, cells // groups, planes // LANES
    me = lax.axis_index("gy")
    block = sub_ids((SUBS, LANES)) // kept
    weight = cell_weight(labels_ref[...], diffusivity_ref)
    energies = by_source([ref[2 * rows, 0] for ref in held], me)
    total = jnp.sum(sum(energies[1:], energies[0]), axis=(0, 1), keepdims=True)
    total_ref[...] = total
    ratio = total / rz_prev_ref[0]
    for part in range(2):
        for a in range(rows):
            lanes = slice(a * LANES, (a + 1) * LANES)
            for zp in range(inner):
                sources = by_source([ref[part * rows + a, zp] for ref in held], me)
                for zg in range(groups):
                    z = zg * inner + zp
                    value = turn(sources[0], -zg * kept)
                    for t in range(1, groups):
                        value = jnp.where(block == t, turn(sources[t], (t - zg) * kept), value)
                    value = value * weight[z : z + 1, lanes]
                    out_ref[z, part, :, lanes] = value
                    direction_ref[z, part, :, lanes] = value + ratio * previous_ref[z, part, :, lanes]


def float_array(*shape):
    return jax.ShapeDtypeStruct(shape, jnp.float32)


def on_device(residual, direction_prev, phase_labels, phase_diffusivity, x_eigen, rz_prev):
    cells, parts, waves, planes = residual.shape
    groups, slabs = lax.axis_size("gy"), lax.axis_size("gz")
    levels = slabs.bit_length() - 1
    inner, rows = cells // groups, planes // LANES
    radix = rows * groups
    distances = [[(i, (i + s) % groups) for i in range(groups)] for s in range(1, groups)]

    pieces = pl.pallas_call(
        functools.partial(pack_kernel, groups),
        out_shape=[float_array(parts, rows, inner, SUBS, LANES)] * groups,
        in_specs=[VMEM, VMEM, SMEM],
        out_specs=[VMEM] * groups,
        name="pack",
    )(residual, phase_labels, phase_diffusivity)
    held = [pieces[0]] + [lax.ppermute(x, "gy", d) for x, d in zip(pieces[1:], distances)]

    message, local, decay, scale = pl.pallas_call(
        functools.partial(forward_kernel, groups),
        out_shape=[
            float_array(parts * radix + 1, SUBS, LANES),
            float_array(parts, radix, inner, SUBS, LANES),
            float_array(radix, SUBS, LANES),
            float_array(radix, SUBS, LANES),
        ],
        in_specs=[VMEM] * (groups + 3) + [SMEM],
        out_specs=[VMEM] * 4,
        name="forward",
    )(*held, lane_transform(-1.0), twiddles(radix), y_eigen(radix), x_eigen)

    received = []
    for level in range(levels):
        swap = [(i, i ^ (1 << level)) for i in range(slabs)]
        received.append(lax.ppermute(message, "gz", swap))
        if level < levels - 1:
            message = pl.pallas_call(
                functools.partial(join_kernel, level, cells, groups),
                out_shape=float_array(*message.shape),
                in_specs=[VMEM] * 4,
                out_specs=VMEM,
                name=f"join{level}",
            )(message, received[-1], decay, scale)

    pieces = pl.pallas_call(
        functools.partial(backward_kernel, groups, slabs),
        out_shape=[float_array(parts * rows + 1, inner, SUBS, LANES)] * groups,
        in_specs=[VMEM] * (6 + levels),
        out_specs=[VMEM] * groups,
        name="backward",
    )(message, *received, local, decay, scale, lane_transform(1.0), twiddles(radix))
    held = [pieces[0]] + [lax.ppermute(x, "gy", d) for x, d in zip(pieces[1:], distances)]

    preconditioned, direction, total = pl.pallas_call(
        functools.partial(unpack_kernel, groups),
        out_shape=[float_array(*residual.shape), float_array(*residual.shape), float_array(1, 1)],
        in_specs=[VMEM] * (groups + 1) + [SMEM, VMEM, SMEM],
        out_specs=[VMEM] * 3,
        name="unpack",
    )(*held, phase_labels, phase_diffusivity, direction_prev, rz_prev)
    return preconditioned, direction, jnp.reshape(total, (1,))


def solution(mesh):
    placed = (P("gz", None, None, "gy"), P("gz", None, None, "gy"), P("gz", "gy"), P(), P(), P())
    return jax.shard_map(
        on_device,
        mesh=mesh,
        in_specs=placed,
        out_specs=(P("gz", None, None, "gy"), P("gz", None, None, "gy"), P()),
        check_vma=False,
    )
```

profile of v0, /device:TPU:0, one launch (start us, length us, event | category | flops | bytes accessed | tf_op | source)
XLA Modules:
  0.0 45.4 jit_solution(3119868485008964807)
XLA Ops:
  0.6 1.7 %pack.1 = (f32[2,4,4,8,128]{4,3,2,1,0:T(8,128)}, f32[2,4,4,8,128]{4,3,2,1,0:T(8,128)}) custom-call(f32[8,2,8,512]{3,2,1,0:T(8,128)} %residual_ref.1, s32[8,512]{1,0:T(8,128)} %refs_2_.2, f32[3]{0:T(128)} %refs_3_.2), custom_call_target="tpu_custom_call" | custom-call | tf_op jit(solution)/shard_map/pack/pallas_call | solution.py:371
  2.3 2.9 %collective-permute-start = (f32[2,4,4,8,128]{4,3,2,1,0:T(8,128)}, f32[2,4,4,8,128]{4,3,2,1,0:T(8,128)S(1)}, u32[]{:S(2)}, u32[]{:S(2)}) collective-permute-start(f32[2,4,4,8,128]{4,3,2,1,0:T(8,128)} %get-tuple-element.15), channel_id=1, source_target_pairs={{0,16},{16,0},{1,17},{17,1},{2,18},{18,2},{3,19},{19,3},{4,20},{20... | collective-permute-start | bytes 393224 | tf_op jit(solution)/shard_map/ppermute | solution.py:378
  5.3 3.7 %collective-permute-done.refs_1_ = f32[2,4,4,8,128]{4,3,2,1,0:T(8,128)S(1)} collective-permute-done((f32[2,4,4,8,128]{4,3,2,1,0:T(8,128)}, f32[2,4,4,8,128]{4,3,2,1,0:T(8,128)S(1)}, u32[]{:S(2)}, u32[]{:S(2)}) %collective-permute-start) | collective-permute-done | bytes 131104 | tf_op jit(solution)/shard_map/ppermute | solution.py:378
  9.0 0.0 copy-start.4
  9.0 0.6 %copy-done.4 = f32[2,4,4,8,128]{4,3,2,1,0:T(8,128)} copy-done((f32[2,4,4,8,128]{4,3,2,1,0:T(8,128)}, f32[2,4,4,8,128]{4,3,2,1,0:T(8,128)S(1)}, u32[]{:S(2)}) %copy-start.4) | copy-done | bytes 131096
  9.6 2.2 %forward.1 = (f32[17,8,128]{2,1,0:T(8,128)}, f32[2,8,4,8,128]{4,3,2,1,0:T(8,128)}, f32[8,8,128]{2,1,0:T(8,128)}, f32[8,8,128]{2,1,0:T(8,128)}) custom-call(f32[2,4,4,8,128]{4,3,2,1,0:T(8,128)} %get-tuple-element.14.refs_0_, f32[2,4,4,8,128]{4,3,2,1,0:T(8,128)} %copy-done.4, bf16[2,256,256]{2,1,0:T(8,128)(2,1)} %constant.8.clone.refs_2_, ...), custom_call_target="tpu_custom_call" | custom-call | tf_op jit(solution)/shard_map/forward/pallas_call | solution.py:380
  11.9 0.0 collective-permute-start.1
  11.9 1.5 %collective-permute-done.1.other_ref.refs_1_ = f32[17,8,128]{2,1,0:T(8,128)S(1)} collective-permute-done((f32[17,8,128]{2,1,0:T(8,128)}, f32[17,8,128]{2,1,0:T(8,128)S(1)}, u32[]{:S(2)}, u32[]{:S(2)}) %collective-permute-start.1) | collective-permute-done | bytes 69664 | tf_op jit(solution)/shard_map/ppermute | solution.py:396
  13.3 0.0 copy-start
  13.3 0.6 %copy-done = f32[17,8,128]{2,1,0:T(8,128)} copy-done((f32[17,8,128]{2,1,0:T(8,128)}, f32[17,8,128]{2,1,0:T(8,128)S(1)}, u32[]{:S(2)}) %copy-start) | copy-done | bytes 69656
  14.0 1.6 %join0.1.own_ref = f32[17,8,128]{2,1,0:T(8,128)} custom-call(f32[17,8,128]{2,1,0:T(8,128)} %get-tuple-element.16.own_ref, f32[17,8,128]{2,1,0:T(8,128)} %copy-done, f32[8,8,128]{2,1,0:T(8,128)} %get-tuple-element.17.decay_ref.refs_6_, f32[8,8,128]{2,1,0:T(8,128)} %get-tuple-element.18.scale_ref.refs_7_), custom_call_target="tpu_custom_call" | custom-call | tf_op jit(solution)/shard_map/join0/pallas_call | solution.py:398
  15.5 1.8 %collective-permute-start.2 = (f32[17,8,128]{2,1,0:T(8,128)}, f32[17,8,128]{2,1,0:T(8,128)S(1)}, u32[]{:S(2)}, u32[]{:S(2)}) collective-permute-start(f32[17,8,128]{2,1,0:T(8,128)} %join0.1.own_ref), channel_id=1, source_target_pairs={{0,2},{1,3},{2,0},{3,1},{4,6},{5,7},{6,4},{7,5},{8,10},{9,11},{10,... | collective-permute-start | bytes 208904 | tf_op jit(solution)/shard_map/ppermute | solution.py:396
  17.3 2.7 %collective-permute-done.2.other_ref.refs_2_ = f32[17,8,128]{2,1,0:T(8,128)S(1)} collective-permute-done((f32[17,8,128]{2,1,0:T(8,128)}, f32[17,8,128]{2,1,0:T(8,128)S(1)}, u32[]{:S(2)}, u32[]{:S(2)}) %collective-permute-start.2) | collective-permute-done | bytes 69664 | tf_op jit(solution)/shard_map/ppermute | solution.py:396
  20.1 0.0 copy-start.1
  20.1 0.6 %copy-done.1 = f32[17,8,128]{2,1,0:T(8,128)} copy-done((f32[17,8,128]{2,1,0:T(8,128)}, f32[17,8,128]{2,1,0:T(8,128)S(1)}, u32[]{:S(2)}) %copy-start.1) | copy-done | bytes 69656
  20.7 1.6 %join1.1.own_ref = f32[17,8,128]{2,1,0:T(8,128)} custom-call(f32[17,8,128]{2,1,0:T(8,128)} %join0.1.own_ref, f32[17,8,128]{2,1,0:T(8,128)} %copy-done.1, f32[8,8,128]{2,1,0:T(8,128)} %get-tuple-element.17.decay_ref.refs_6_, f32[8,8,128]{2,1,0:T(8,128)} %get-tuple-element.18.scale_ref.refs_7_), custom_call_target="tpu_custom_call" | custom-call | tf_op jit(solution)/shard_map/join1/pallas_call | solution.py:398
  22.3 1.8 %collective-permute-start.3 = (f32[17,8,128]{2,1,0:T(8,128)}, f32[17,8,128]{2,1,0:T(8,128)S(1)}, u32[]{:S(2)}, u32[]{:S(2)}) collective-permute-start(f32[17,8,128]{2,1,0:T(8,128)} %join1.1.own_ref), channel_id=1, source_target_pairs={{0,4},{1,5},{2,6},{3,7},{4,0},{5,1},{6,2},{7,3},{8,12},{9,13},{10,... | collective-permute-start | bytes 208904 | tf_op jit(solution)/shard_map/ppermute | solution.py:396
  24.1 2.7 %collective-permute-done.3.other_ref.refs_3_ = f32[17,8,128]{2,1,0:T(8,128)S(1)} collective-permute-done((f32[17,8,128]{2,1,0:T(8,128)}, f32[17,8,128]{2,1,0:T(8,128)S(1)}, u32[]{:S(2)}, u32[]{:S(2)}) %collective-permute-start.3) | collective-permute-done | bytes 69664 | tf_op jit(solution)/shard_map/ppermute | solution.py:396
  26.8 0.0 copy-start.2
  26.8 0.6 %copy-done.2 = f32[17,8,128]{2,1,0:T(8,128)} copy-done((f32[17,8,128]{2,1,0:T(8,128)}, f32[17,8,128]{2,1,0:T(8,128)S(1)}, u32[]{:S(2)}) %copy-start.2) | copy-done | bytes 69656
  27.4 1.6 %join2.1.refs_0_ = f32[17,8,128]{2,1,0:T(8,128)} custom-call(f32[17,8,128]{2,1,0:T(8,128)} %join1.1.own_ref, f32[17,8,128]{2,1,0:T(8,128)} %copy-done.2, f32[8,8,128]{2,1,0:T(8,128)} %get-tuple-element.17.decay_ref.refs_6_, f32[8,8,128]{2,1,0:T(8,128)} %get-tuple-element.18.scale_ref.refs_7_), custom_call_target="tpu_custom_call" | custom-call | tf_op jit(solution)/shard_map/join2/pallas_call | solution.py:398
  29.0 2.8 %collective-permute-start.4 = (f32[17,8,128]{2,1,0:T(8,128)}, f32[17,8,128]{2,1,0:T(8,128)S(1)}, u32[]{:S(2)}, u32[]{:S(2)}) collective-permute-start(f32[17,8,128]{2,1,0:T(8,128)} %join2.1.refs_0_), channel_id=1, source_target_pairs={{0,8},{1,9},{2,10},{3,11},{4,12},{5,13},{6,14},{7,15},{8,0},{9,1},... | collective-permute-start | bytes 208904 | tf_op jit(solution)/shard_map/ppermute | solution.py:396
  31.8 2.6 %collective-permute-done.4.refs_4_ = f32[17,8,128]{2,1,0:T(8,128)S(1)} collective-permute-done((f32[17,8,128]{2,1,0:T(8,128)}, f32[17,8,128]{2,1,0:T(8,128)S(1)}, u32[]{:S(2)}, u32[]{:S(2)}) %collective-permute-start.4) | collective-permute-done | bytes 69664 | tf_op jit(solution)/shard_map/ppermute | solution.py:396
  34.4 0.0 copy-start.5
  34.4 0.6 %copy-done.5 = f32[17,8,128]{2,1,0:T(8,128)} copy-done((f32[17,8,128]{2,1,0:T(8,128)}, f32[17,8,128]{2,1,0:T(8,128)S(1)}, u32[]{:S(2)}) %copy-start.5) | copy-done | bytes 69656
  35.1 2.3 %backward.1 = (f32[9,4,8,128]{3,2,1,0:T(8,128)}, f32[9,4,8,128]{3,2,1,0:T(8,128)}) custom-call(f32[17,8,128]{2,1,0:T(8,128)} %join2.1.refs_0_, f32[17,8,128]{2,1,0:T(8,128)} %copy-done, f32[17,8,128]{2,1,0:T(8,128)} %copy-done.1, f32[17,8,128]{2,1,0:T(8,128)} %copy-done.2, f32[17,8,128]{2,1,0:T(8,128)} %copy-done.5, ...), custom_call_target="tpu_custom_call" | custom-call | tf_op jit(solution)/shard_map/backward/pallas_call | solution.py:406
  37.4 1.7 %collective-permute-start.5 = (f32[9,4,8,128]{3,2,1,0:T(8,128)}, f32[9,4,8,128]{3,2,1,0:T(8,128)S(1)}, u32[]{:S(2)}, u32[]{:S(2)}) collective-permute-start(f32[9,4,8,128]{3,2,1,0:T(8,128)} %get-tuple-element.21), channel_id=1, source_target_pairs={{0,16},{16,0},{1,17},{17,1},{2,18},{18,2},{3,19},{19,3},{4,20},{20... | collective-permute-start | bytes 442376 | tf_op jit(solution)/shard_map/ppermute | solution.py:413
  39.8 3.0 %collective-permute-done.5.refs_1_ = f32[9,4,8,128]{3,2,1,0:T(8,128)S(1)} collective-permute-done((f32[9,4,8,128]{3,2,1,0:T(8,128)}, f32[9,4,8,128]{3,2,1,0:T(8,128)S(1)}, u32[]{:S(2)}, u32[]{:S(2)}) %collective-permute-start.5) | collective-permute-done | bytes 147488 | tf_op jit(solution)/shard_map/ppermute | solution.py:413
  42.7 0.0 copy-start.3
  42.7 0.7 %copy-done.3 = f32[9,4,8,128]{3,2,1,0:T(8,128)} copy-done((f32[9,4,8,128]{3,2,1,0:T(8,128)}, f32[9,4,8,128]{3,2,1,0:T(8,128)S(1)}, u32[]{:S(2)}) %copy-start.3) | copy-done | bytes 147480
  43.4 2.0 %unpack.1 = (f32[8,2,8,512]{3,2,1,0:T(8,128)}, f32[8,2,8,512]{3,2,1,0:T(8,128)}, f32[1,1]{1,0:T(1,128)}) custom-call(f32[9,4,8,128]{3,2,1,0:T(8,128)} %get-tuple-element.20.refs_0_, f32[9,4,8,128]{3,2,1,0:T(8,128)} %copy-done.3, s32[8,512]{1,0:T(8,128)} %refs_2_.2, f32[3]{0:T(128)} %refs_3_.2, f32[8,2,8,512]{3,2,1,0:T(8,128)} %refs_4_.2, f32[1]{0:T(128)S(6)} %copy.14.refs_5_), custom_call_target="tpu_custom_call" | custom-call | tf_op jit(solution)/shard_map/unpack/pallas_call | solution.py:415
Async XLA Ops:
  2.3 6.6 %collective-permute-start = (f32[2,4,4,8,128]{4,3,2,1,0:T(8,128)}, f32[2,4,4,8,128]{4,3,2,1,0:T(8,128)S(1)}, u32[]{:S(2)}, u32[]{:S(2)}) collective-permute-start(f32[2,4,4,8,128]{4,3,2,1,0:T(8,128)} %get-tuple-element.15), channel_id=1, source_target_pairs={{0,16},{16,0},{1,17},{17,1},{2,18},{18,2},{3,19},{19,3},{4,20},{20... | collective-permute-start | bytes 393224 | tf_op jit(solution)/shard_map/ppermute | solution.py:378
  9.0 0.7 %copy-start.4 = (f32[2,4,4,8,128]{4,3,2,1,0:T(8,128)}, f32[2,4,4,8,128]{4,3,2,1,0:T(8,128)S(1)}, u32[]{:S(2)}) copy-start(f32[2,4,4,8,128]{4,3,2,1,0:T(8,128)S(1)} %collective-permute-done.refs_1_) | copy-start | bytes 393220
  11.9 1.5 %collective-permute-start.1 = (f32[17,8,128]{2,1,0:T(8,128)}, f32[17,8,128]{2,1,0:T(8,128)S(1)}, u32[]{:S(2)}, u32[]{:S(2)}) collective-permute-start(f32[17,8,128]{2,1,0:T(8,128)} %get-tuple-element.16.own_ref), channel_id=1, source_target_pairs={{0,1},{1,0},{2,3},{3,2},{4,5},{5,4},{6,7},{7,6},{8,9},{9,8},{10,11... | collective-permute-start | bytes 208904 | tf_op jit(solution)/shard_map/ppermute | solution.py:396
  13.3 0.6 %copy-start = (f32[17,8,128]{2,1,0:T(8,128)}, f32[17,8,128]{2,1,0:T(8,128)S(1)}, u32[]{:S(2)}) copy-start(f32[17,8,128]{2,1,0:T(8,128)S(1)} %collective-permute-done.1.other_ref.refs_1_) | copy-start | bytes 208900
  15.5 4.5 %collective-permute-start.2 = (f32[17,8,128]{2,1,0:T(8,128)}, f32[17,8,128]{2,1,0:T(8,128)S(1)}, u32[]{:S(2)}, u32[]{:S(2)}) collective-permute-start(f32[17,8,128]{2,1,0:T(8,128)} %join0.1.own_ref), channel_id=1, source_target_pairs={{0,2},{1,3},{2,0},{3,1},{4,6},{5,7},{6,4},{7,5},{8,10},{9,11},{10,... | collective-permute-start | bytes 208904 | tf_op jit(solution)/shard_map/ppermute | solution.py:396
  20.1 0.6 %copy-start.1 = (f32[17,8,128]{2,1,0:T(8,128)}, f32[17,8,128]{2,1,0:T(8,128)S(1)}, u32[]{:S(2)}) copy-start(f32[17,8,128]{2,1,0:T(8,128)S(1)} %collective-permute-done.2.other_ref.refs_2_) | copy-start | bytes 208900
  22.3 4.5 %collective-permute-start.3 = (f32[17,8,128]{2,1,0:T(8,128)}, f32[17,8,128]{2,1,0:T(8,128)S(1)}, u32[]{:S(2)}, u32[]{:S(2)}) collective-permute-start(f32[17,8,128]{2,1,0:T(8,128)} %join1.1.own_ref), channel_id=1, source_target_pairs={{0,4},{1,5},{2,6},{3,7},{4,0},{5,1},{6,2},{7,3},{8,12},{9,13},{10,... | collective-permute-start | bytes 208904 | tf_op jit(solution)/shard_map/ppermute | solution.py:396
  26.8 0.6 %copy-start.2 = (f32[17,8,128]{2,1,0:T(8,128)}, f32[17,8,128]{2,1,0:T(8,128)S(1)}, u32[]{:S(2)}) copy-start(f32[17,8,128]{2,1,0:T(8,128)S(1)} %collective-permute-done.3.other_ref.refs_3_) | copy-start | bytes 208900
  29.0 5.4 %collective-permute-start.4 = (f32[17,8,128]{2,1,0:T(8,128)}, f32[17,8,128]{2,1,0:T(8,128)S(1)}, u32[]{:S(2)}, u32[]{:S(2)}) collective-permute-start(f32[17,8,128]{2,1,0:T(8,128)} %join2.1.refs_0_), channel_id=1, source_target_pairs={{0,8},{1,9},{2,10},{3,11},{4,12},{5,13},{6,14},{7,15},{8,0},{9,1},... | collective-permute-start | bytes 208904 | tf_op jit(solution)/shard_map/ppermute | solution.py:396
  34.4 0.6 %copy-start.5 = (f32[17,8,128]{2,1,0:T(8,128)}, f32[17,8,128]{2,1,0:T(8,128)S(1)}, u32[]{:S(2)}) copy-start(f32[17,8,128]{2,1,0:T(8,128)S(1)} %collective-permute-done.4.refs_4_) | copy-start | bytes 208900
  37.4 5.4 %collective-permute-start.5 = (f32[9,4,8,128]{3,2,1,0:T(8,128)}, f32[9,4,8,128]{3,2,1,0:T(8,128)S(1)}, u32[]{:S(2)}, u32[]{:S(2)}) collective-permute-start(f32[9,4,8,128]{3,2,1,0:T(8,128)} %get-tuple-element.21), channel_id=1, source_target_pairs={{0,16},{16,0},{1,17},{17,1},{2,18},{18,2},{3,19},{19,3},{4,20},{20... | collective-permute-start | bytes 442376 | tf_op jit(solution)/shard_map/ppermute | solution.py:413
  42.7 0.7 %copy-start.3 = (f32[9,4,8,128]{3,2,1,0:T(8,128)}, f32[9,4,8,128]{3,2,1,0:T(8,128)S(1)}, u32[]{:S(2)}) copy-start(f32[9,4,8,128]{3,2,1,0:T(8,128)S(1)} %collective-permute-done.5.refs_1_) | copy-start | bytes 442372
where the time goes:
time: 45.8 us; the launch traced here: 45.4 us
  waiting for transfers between devices  16.1 us (35%)
  Pallas kernels  13 us (28%)
  starting transfers between devices  11.1 us (24%)
  local copies, waits for them, and re-layouts  3.81 us (8%)
  between operations  1.3 us (3%)
    ppermute x4, waiting for transfers between devices, on_device(): received.append(lax.ppermute(message, 'gz', swap))  9.48 us
    ppermute x2, waiting for transfers between devices, on_device(): lax.ppermute(x, 'gy', d)  6.66 us
    ppermute x4, starting transfers between devices, on_device(): received.append(lax.ppermute(message, 'gz', swap))  6.44 us
    pallas_call x3, Pallas kernels, on_device(): pl.pallas_call(functools.partial(join_kernel, level, cells, groups), out_...  4.75 us
    ppermute x2, starting transfers between devices, on_device(): lax.ppermute(x, 'gy', d)  4.68 us
    unnamed x12, local copies, waits for them, and re-layouts  3.81 us
    pallas_call x1, Pallas kernels, on_device(): pl.pallas_call(functools.partial(backward_kernel, groups, slabs), out_sha...  2.33 us
    pallas_call x1, Pallas kernels, on_device(): pl.pallas_call(functools.partial(forward_kernel, groups), out_shape=[floa...  2.22 us
  transfers between devices with their start and end apart: 6, of which 6 were waited for; matrix products, arithmetic and copies ran while one was open for 0% of the time, Pallas kernels for 0%

commit v1 on v0

--- a/solution.py
+++ b/solution.py
@@ -360,6 +360,14 @@
     return jax.ShapeDtypeStruct(shape, jnp.float32)
 
 
+def held_array(*shape):
+    return pltpu.VMEM(shape, jnp.float32)
+
+
+def inside(value):
+    return pltpu.with_memory_space_constraint(value, pltpu.VMEM)
+
+
 def on_device(residual, direction_prev, phase_labels, phase_diffusivity, x_eigen, rz_prev):
     cells, parts, waves, planes = residual.shape
     groups, slabs = lax.axis_size("gy"), lax.axis_size("gz")
@@ -370,7 +378,7 @@
 
     pieces = pl.pallas_call(
         functools.partial(pack_kernel, groups),
-        out_shape=[float_array(parts, rows, inner, SUBS, LANES)] * groups,
+        out_shape=[held_array(parts, rows, inner, SUBS, LANES)] * groups,
         in_specs=[VMEM, VMEM, SMEM],
         out_specs=[VMEM] * groups,
         name="pack",
@@ -380,15 +388,15 @@
     message, local, decay, scale = pl.pallas_call(
         functools.partial(forward_kernel, groups),
         out_shape=[
-            float_array(parts * radix + 1, SUBS, LANES),
-            float_array(parts, radix, inner, SUBS, LANES),
-            float_array(radix, SUBS, LANES),
-            float_array(radix, SUBS, LANES),
+            held_array(parts * radix + 1, SUBS, LANES),
+            held_array(parts, radix, inner, SUBS, LANES),
+            held_array(radix, SUBS, LANES),
+            held_array(radix, SUBS, LANES),
         ],
         in_specs=[VMEM] * (groups + 3) + [SMEM],
         out_specs=[VMEM] * 4,
         name="forward",
-    )(*held, lane_transform(-1.0), twiddles(radix), y_eigen(radix), x_eigen)
+    )(*map(inside, held), lane_transform(-1.0), twiddles(radix), y_eigen(radix), x_eigen)
 
     received = []
     for level in range(levels):
@@ -397,19 +405,19 @@
         if level < levels - 1:
             message = pl.pallas_call(
                 functools.partial(join_kernel, level, cells, groups),
-                out_shape=float_array(*message.shape),
+                out_shape=held_array(*message.shape),
                 in_specs=[VMEM] * 4,
                 out_specs=VMEM,
                 name=f"join{level}",
-            )(message, received[-1], decay, scale)
+            )(*map(inside, (message, received[-1], decay, scale)))
 
     pieces = pl.pallas_call(
         functools.partial(backward_kernel, groups, slabs),
-        out_shape=[float_array(parts * rows + 1, inner, SUBS, LANES)] * groups,
+        out_shape=[held_array(parts * rows + 1, inner, SUBS, LANES)] * groups,
         in_specs=[VMEM] * (6 + levels),
         out_specs=[VMEM] * groups,
         name="backward",
-    )(message, *received, local, decay, scale, lane_transform(1.0), twiddles(radix))
+    )(*map(inside, (message, *received, local, decay, scale)), lane_transform(1.0), twiddles(radix))
     held = [pieces[0]] + [lax.ppermute(x, "gy", d) for x, d in zip(pieces[1:], distances)]
 
     preconditioned, direction, total = pl.pallas_call(
@@ -418,7 +426,7 @@
         in_specs=[VMEM] * (groups + 1) + [SMEM, VMEM, SMEM],
         out_specs=[VMEM] * 3,
         name="unpack",
-    )(*held, phase_labels, phase_diffusivity, direction_prev, rz_prev)
+    )(*map(inside, held), phase_labels, phase_diffusivity, direction_prev, rz_prev)
     return preconditioned, direction, jnp.reshape(total, (1,))
 
 

time: 45.8 us -> 33.7 us (0.74)
  Pallas kernels: 13 us -> 5.71 us
  local copies, waits for them, and re-layouts: 3.81 us -> 0 us
  waiting for transfers between devices: 16.1 us -> 14.9 us
    pallas_call x3, Pallas kernels: 4.75 us -> 0.13 us  [on_device(): pl.pallas_call(functools.partial(join_kernel, level, cells, groups), out_...]
    unnamed x12 -> x0, local copies, waits for them, and re-layouts: 3.81 us -> none
    pallas_call x2, Pallas kernels: 3.93 us -> 2.38 us  [the longest x1 1.37 us: on_device(): pl.pallas_call(functools.partial(forward_kernel, groups), out_shape=[held...]
    pallas_call x1, Pallas kernels: 2.33 us -> 1.34 us  [on_device(): pl.pallas_call(functools.partial(backward_kernel, groups, slabs), out_sha...]
    ppermute x4, waiting for transfers between devices: 9.48 us -> 8.64 us  [on_device(): received.append(lax.ppermute(message, 'gz', swap))]
where the time goes in v1:
time: 33.7 us; the launch traced here: 33.4 us
  waiting for transfers between devices  14.9 us (44%)
  starting transfers between devices  11.5 us (34%)
  Pallas kernels  5.71 us (17%)
  between operations  1.32 us (4%)
    ppermute x4, waiting for transfers between devices, on_device(): received.append(lax.ppermute(message, 'gz', swap))  8.64 us
    ppermute x4, starting transfers between devices, on_device(): received.append(lax.ppermute(message, 'gz', swap))  6.69 us
    ppermute x2, waiting for transfers between devices, on_device(): lax.ppermute(x, 'gy', d)  6.25 us
    ppermute x2, starting transfers between devices, on_device(): lax.ppermute(x, 'gy', d)  4.81 us
    pallas_call x1, Pallas kernels, on_device(): pl.pallas_call(functools.partial(unpack_kernel, groups), out_shape=[float...  1.86 us
    pallas_call x1, Pallas kernels, on_device(): pl.pallas_call(functools.partial(forward_kernel, groups), out_shape=[held...  1.37 us
    pallas_call x1, Pallas kernels, on_device(): pl.pallas_call(functools.partial(backward_kernel, groups, slabs), out_sha...  1.34 us
    pallas_call x1, Pallas kernels, on_device(): pl.pallas_call(functools.partial(pack_kernel, groups), out_shape=[held_ar...  1.02 us
  transfers between devices with their start and end apart: 6, of which 6 were waited for; matrix products, arithmetic and copies ran while one was open for 0% of the time, Pallas kernels for 0%

profile of v1, /device:TPU:0, one launch (start us, length us, event | category | flops | bytes accessed | tf_op | source)
XLA Modules:
  0.0 33.4 jit_solution(9117910858276358180)
XLA Ops:
  0.6 1.0 %pack.1 = (f32[2,4,4,8,128]{4,3,2,1,0:T(8,128)S(1)}, f32[2,4,4,8,128]{4,3,2,1,0:T(8,128)S(1)}) custom-call(f32[8,2,8,512]{3,2,1,0:T(8,128)} %residual_ref.1, s32[8,512]{1,0:T(8,128)} %refs_2_.2, f32[3]{0:T(128)} %refs_3_.2), custom_call_target="tpu_custom_call" | custom-call | tf_op jit(solution)/shard_map/pack/pallas_call | solution.py:379
  1.7 3.0 %collective-permute-start = (f32[2,4,4,8,128]{4,3,2,1,0:T(8,128)S(1)}, f32[2,4,4,8,128]{4,3,2,1,0:T(8,128)S(1)}, u32[]{:S(2)}, u32[]{:S(2)}) collective-permute-start(f32[2,4,4,8,128]{4,3,2,1,0:T(8,128)S(1)} %get-tuple-element.15), channel_id=1, source_target_pairs={{0,16},{16,0},{1,17},{17,1},{2,18},{18,2},{3,19},{19,3},{4,20},{20... | collective-permute-start | bytes 393224 | tf_op jit(solution)/shard_map/ppermute | solution.py:386
  4.7 3.5 %collective-permute-done.refs_1_ = f32[2,4,4,8,128]{4,3,2,1,0:T(8,128)S(1)} collective-permute-done((f32[2,4,4,8,128]{4,3,2,1,0:T(8,128)S(1)}, f32[2,4,4,8,128]{4,3,2,1,0:T(8,128)S(1)}, u32[]{:S(2)}, u32[]{:S(2)}) %collective-permute-start) | collective-permute-done | bytes 131104 | tf_op jit(solution)/shard_map/ppermute | solution.py:386
  8.2 1.4 %forward.1 = (f32[17,8,128]{2,1,0:T(8,128)S(1)}, f32[2,8,4,8,128]{4,3,2,1,0:T(8,128)S(1)}, f32[8,8,128]{2,1,0:T(8,128)S(1)}, f32[8,8,128]{2,1,0:T(8,128)S(1)}) custom-call(f32[2,4,4,8,128]{4,3,2,1,0:T(8,128)S(1)} %get-tuple-element.14.refs_0_, f32[2,4,4,8,128]{4,3,2,1,0:T(8,128)S(1)} %collective-permute-done.refs_1_, ...), custom_call_target="tpu_custom_call" | custom-call | tf_op jit(solution)/shard_map/forward/pallas_call | solution.py:388
  9.5 0.1 collective-permute-start.1
  9.6 1.2 %collective-permute-done.1.other_ref.refs_1_ = f32[17,8,128]{2,1,0:T(8,128)S(1)} collective-permute-done((f32[17,8,128]{2,1,0:T(8,128)S(1)}, f32[17,8,128]{2,1,0:T(8,128)S(1)}, u32[]{:S(2)}, u32[]{:S(2)}) %collective-permute-start.1) | collective-permute-done | bytes 69664 | tf_op jit(solution)/shard_map/ppermute | solution.py:404
  10.9 1.8 %collective-permute-start.2 = (f32[17,8,128]{2,1,0:T(8,128)S(1)}, f32[17,8,128]{2,1,0:T(8,128)S(1)}, u32[]{:S(2)}, u32[]{:S(2)}) collective-permute-start(f32[17,8,128]{2,1,0:T(8,128)S(1)} %join0.1.own_ref), channel_id=1, source_target_pairs={{0,2},{1,3},{2,0},{3,1},{4,6},{5,7},{6,4},{7,5},{8,10},{9,11},{10,... | collective-permute-start | bytes 208904 | tf_op jit(solution)/shard_map/ppermute | solution.py:404
  12.7 2.5 %collective-permute-done.2.other_ref.refs_2_ = f32[17,8,128]{2,1,0:T(8,128)S(1)} collective-permute-done((f32[17,8,128]{2,1,0:T(8,128)S(1)}, f32[17,8,128]{2,1,0:T(8,128)S(1)}, u32[]{:S(2)}, u32[]{:S(2)}) %collective-permute-start.2) | collective-permute-done | bytes 69664 | tf_op jit(solution)/shard_map/ppermute | solution.py:404
  15.3 1.9 %collective-permute-start.3 = (f32[17,8,128]{2,1,0:T(8,128)S(1)}, f32[17,8,128]{2,1,0:T(8,128)S(1)}, u32[]{:S(2)}, u32[]{:S(2)}) collective-permute-start(f32[17,8,128]{2,1,0:T(8,128)S(1)} %join1.1.own_ref), channel_id=1, source_target_pairs={{0,4},{1,5},{2,6},{3,7},{4,0},{5,1},{6,2},{7,3},{8,12},{9,13},{10,... | collective-permute-start | bytes 208904 | tf_op jit(solution)/shard_map/ppermute | solution.py:404
  17.2 2.5 %collective-permute-done.3.other_ref.refs_3_ = f32[17,8,128]{2,1,0:T(8,128)S(1)} collective-permute-done((f32[17,8,128]{2,1,0:T(8,128)S(1)}, f32[17,8,128]{2,1,0:T(8,128)S(1)}, u32[]{:S(2)}, u32[]{:S(2)}) %collective-permute-start.3) | collective-permute-done | bytes 69664 | tf_op jit(solution)/shard_map/ppermute | solution.py:404
  19.7 2.9 %collective-permute-start.4 = (f32[17,8,128]{2,1,0:T(8,128)S(1)}, f32[17,8,128]{2,1,0:T(8,128)S(1)}, u32[]{:S(2)}, u32[]{:S(2)}) collective-permute-start(f32[17,8,128]{2,1,0:T(8,128)S(1)} %join2.1.refs_0_), channel_id=1, source_target_pairs={{0,8},{1,9},{2,10},{3,11},{4,12},{5,13},{6,14},{7,15},{8,0},{9,1},... | collective-permute-start | bytes 208904 | tf_op jit(solution)/shard_map/ppermute | solution.py:404
  22.6 2.4 %collective-permute-done.4.refs_4_ = f32[17,8,128]{2,1,0:T(8,128)S(1)} collective-permute-done((f32[17,8,128]{2,1,0:T(8,128)S(1)}, f32[17,8,128]{2,1,0:T(8,128)S(1)}, u32[]{:S(2)}, u32[]{:S(2)}) %collective-permute-start.4) | collective-permute-done | bytes 69664 | tf_op jit(solution)/shard_map/ppermute | solution.py:404
  25.0 1.3 %backward.1 = (f32[9,4,8,128]{3,2,1,0:T(8,128)S(1)}, f32[9,4,8,128]{3,2,1,0:T(8,128)S(1)}) custom-call(f32[17,8,128]{2,1,0:T(8,128)S(1)} %join2.1.refs_0_, f32[17,8,128]{2,1,0:T(8,128)S(1)} %collective-permute-done.1.other_ref.refs_1_, f32[17,8,128]{2,1,0:T(8,128)S(1)} %collective-permute-done.2.other_ref.refs_2_, ...), custom_call_target="tpu_custom_call" | custom-call | tf_op jit(solution)/shard_map/backward/pallas_call | solution.py:414
  26.3 1.8 %collective-permute-start.5 = (f32[9,4,8,128]{3,2,1,0:T(8,128)S(1)}, f32[9,4,8,128]{3,2,1,0:T(8,128)S(1)}, u32[]{:S(2)}, u32[]{:S(2)}) collective-permute-start(f32[9,4,8,128]{3,2,1,0:T(8,128)S(1)} %get-tuple-element.21), channel_id=1, source_target_pairs={{0,16},{16,0},{1,17},{17,1},{2,18},{18,2},{3,19},{19,3},{4,20},{20... | collective-permute-start | bytes 442376 | tf_op jit(solution)/shard_map/ppermute | solution.py:421
  28.8 2.8 %collective-permute-done.5.refs_1_ = f32[9,4,8,128]{3,2,1,0:T(8,128)S(1)} collective-permute-done((f32[9,4,8,128]{3,2,1,0:T(8,128)S(1)}, f32[9,4,8,128]{3,2,1,0:T(8,128)S(1)}, u32[]{:S(2)}, u32[]{:S(2)}) %collective-permute-start.5) | collective-permute-done | bytes 147488 | tf_op jit(solution)/shard_map/ppermute | solution.py:421
  31.6 1.9 %unpack.1 = (f32[8,2,8,512]{3,2,1,0:T(8,128)}, f32[8,2,8,512]{3,2,1,0:T(8,128)}, f32[1,1]{1,0:T(1,128)}) custom-call(f32[9,4,8,128]{3,2,1,0:T(8,128)S(1)} %get-tuple-element.20.refs_0_, f32[9,4,8,128]{3,2,1,0:T(8,128)S(1)} %collective-permute-done.5.refs_1_, s32[8,512]{1,0:T(8,128)} %refs_2_.2, f32[3]{0:T(128)} %refs_3_.2, f32[8,2,8,512]{3,2,1,0:T(8,128)} %refs_4_.2, ...), custom_call_target="tpu_custom_call" | custom-call | tf_op jit(solution)/shard_map/unpack/pallas_call | solution.py:423
  (3 shorter events, 0.1 us)
Async XLA Ops:
  1.7 6.5 %collective-permute-start = (f32[2,4,4,8,128]{4,3,2,1,0:T(8,128)S(1)}, f32[2,4,4,8,128]{4,3,2,1,0:T(8,128)S(1)}, u32[]{:S(2)}, u32[]{:S(2)}) collective-permute-start(f32[2,4,4,8,128]{4,3,2,1,0:T(8,128)S(1)} %get-tuple-element.15), channel_id=1, source_target_pairs={{0,16},{16,0},{1,17},{17,1},{2,18},{18,2},{3,19},{19,3},{4,20},{20... | collective-permute-start | bytes 393224 | tf_op jit(solution)/shard_map/ppermute | solution.py:386
  9.5 1.3 %collective-permute-start.1 = (f32[17,8,128]{2,1,0:T(8,128)S(1)}, f32[17,8,128]{2,1,0:T(8,128)S(1)}, u32[]{:S(2)}, u32[]{:S(2)}) collective-permute-start(f32[17,8,128]{2,1,0:T(8,128)S(1)} %get-tuple-element.16.own_ref), channel_id=1, source_target_pairs={{0,1},{1,0},{2,3},{3,2},{4,5},{5,4},{6,7},{7,6},{8,9},{9,8},{10,11... | collective-permute-start | bytes 208904 | tf_op jit(solution)/shard_map/ppermute | solution.py:404
  10.9 4.4 %collective-permute-start.2 = (f32[17,8,128]{2,1,0:T(8,128)S(1)}, f32[17,8,128]{2,1,0:T(8,128)S(1)}, u32[]{:S(2)}, u32[]{:S(2)}) collective-permute-start(f32[17,8,128]{2,1,0:T(8,128)S(1)} %join0.1.own_ref), channel_id=1, source_target_pairs={{0,2},{1,3},{2,0},{3,1},{4,6},{5,7},{6,4},{7,5},{8,10},{9,11},{10,... | collective-permute-start | bytes 208904 | tf_op jit(solution)/shard_map/ppermute | solution.py:404
  15.3 4.4 %collective-permute-start.3 = (f32[17,8,128]{2,1,0:T(8,128)S(1)}, f32[17,8,128]{2,1,0:T(8,128)S(1)}, u32[]{:S(2)}, u32[]{:S(2)}) collective-permute-start(f32[17,8,128]{2,1,0:T(8,128)S(1)} %join1.1.own_ref), channel_id=1, source_target_pairs={{0,4},{1,5},{2,6},{3,7},{4,0},{5,1},{6,2},{7,3},{8,12},{9,13},{10,... | collective-permute-start | bytes 208904 | tf_op jit(solution)/shard_map/ppermute | solution.py:404
  19.7 5.3 %collective-permute-start.4 = (f32[17,8,128]{2,1,0:T(8,128)S(1)}, f32[17,8,128]{2,1,0:T(8,128)S(1)}, u32[]{:S(2)}, u32[]{:S(2)}) collective-permute-start(f32[17,8,128]{2,1,0:T(8,128)S(1)} %join2.1.refs_0_), channel_id=1, source_target_pairs={{0,8},{1,9},{2,10},{3,11},{4,12},{5,13},{6,14},{7,15},{8,0},{9,1},... | collective-permute-start | bytes 208904 | tf_op jit(solution)/shard_map/ppermute | solution.py:404
  26.3 5.2 %collective-permute-start.5 = (f32[9,4,8,128]{3,2,1,0:T(8,128)S(1)}, f32[9,4,8,128]{3,2,1,0:T(8,128)S(1)}, u32[]{:S(2)}, u32[]{:S(2)}) collective-permute-start(f32[9,4,8,128]{3,2,1,0:T(8,128)S(1)} %get-tuple-element.21), channel_id=1, source_target_pairs={{0,16},{16,0},{1,17},{17,1},{2,18},{18,2},{3,19},{19,3},{4,20},{20... | collective-permute-start | bytes 442376 | tf_op jit(solution)/shard_map/ppermute | solution.py:421

commit v2 on v1

--- a/solution.py
+++ b/solution.py
@@ -13,6 +13,7 @@
 HALF = 4
 VMEM = pl.BlockSpec(memory_space=pltpu.VMEM)
 SMEM = pl.BlockSpec(memory_space=pltpu.SMEM)
+ANY = pl.BlockSpec(memory_space=pl.ANY)
 
 
 def split_bf16(table):
@@ -150,34 +151,56 @@
     return ahead, behind
 
 
-def pack_kernel(groups, residual_ref, labels_ref, diffusivity_ref, *out_refs):
+def pack_kernel(groups, residual_any, labels_any, diffusivity_any, weight_ref, *refs):
+    out_refs, (residual_ref, labels_ref, diffusivity_ref, cell_sems, label_sem, value_sem) = refs[:groups], refs[groups:]
+    values = pltpu.make_async_copy(diffusivity_any, diffusivity_ref, value_sem)
+    labels = pltpu.make_async_copy(labels_any, labels_ref, label_sem)
+    values.start()
+    labels.start()
+    arriving = [
+        pltpu.make_async_copy(residual_any.at[z], residual_ref.at[z], cell_sems.at[z]) for z in range(residual_ref.shape[0])
+    ]
+    order = [zg * (len(arriving) // groups) + zp for zp in range(len(arriving) // groups) for zg in range(groups)]
+    for z in order:
+        arriving[z].start()
+    values.wait()
+    labels.wait()
     cells, _, waves, planes = residual_ref.shape
     kept, inner = waves // groups, cells // groups
     me = lax.axis_index("gy")
     group = sub_ids((SUBS, LANES)) // kept
     weight = cell_weight(labels_ref[...], diffusivity_ref)
-    for part in range(2):
-        for a in range(planes // LANES):
-            lanes = slice(a * LANES, (a + 1) * LANES)
-            rows = [residual_ref[z, part, :, lanes] * weight[z : z + 1, lanes] for z in range(cells)]
-            for zp in range(inner):
+    weight_ref[...] = weight
+    for zp in range(inner):
+        for zg in range(groups):
+            arriving[zg * inner + zp].wait()
+        for part in range(2):
+            for a in range(planes // LANES):
+                lanes = slice(a * LANES, (a + 1) * LANES)
+                rows = [residual_ref[z, part, :, lanes] * weight[z : z + 1, lanes] for z in range(zp, cells, inner)]
                 pieces = []
                 for t in range(groups):
-                    piece = turn(rows[zp], -t * kept)
+                    piece = turn(rows[0], -t * kept)
                     for zg in range(1, groups):
-                        piece = jnp.where(group == zg, turn(rows[zg * inner + zp], (zg - t) * kept), piece)
+                        piece = jnp.where(group == zg, turn(rows[zg], (zg - t) * kept), piece)
                     pieces.append(piece)
                 for ref, value in zip(out_refs, for_targets(pieces, me)):
                     ref[part, a, zp] = value
 
 
+def roots_kernel(groups, y_eigen_ref, eigen_ref, decay_ref, scale_ref):
+    length = y_eigen_ref.shape[0] * LANES
+    decay, scale = mode_roots(eigen_ref, y_eigen_ref, lax.axis_index("gy"), SUBS // groups, length)
+    decay_ref[...] = decay
+    scale_ref[...] = scale
+
+
 def forward_kernel(groups, *refs):
     held = refs[:groups]
-    lane_ref, twiddle_ref, y_eigen_ref, eigen_ref = refs[groups : groups + 4]
-    message_ref, local_ref, decay_ref, scale_ref = refs[groups + 4 :]
+    lane_ref, twiddle_ref, decay_ref, scale_ref = refs[groups : groups + 4]
+    message_ref, local_ref = refs[groups + 4 :]
     _, block_rows, inner, _, _ = held[0].shape
     radix = block_rows * groups
-    length = radix * LANES
     kept = SUBS // groups
     me = lax.axis_index("gy")
     re, im = [], []
@@ -193,9 +216,7 @@
         turned_re.append(re[a] * c + im[a] * s)
         turned_im.append(im[a] * c - re[a] * s)
     re, im = lane_product(turned_re, turned_im, lane_ref)
-    decay, scale = mode_roots(eigen_ref, y_eigen_ref, me, kept, length)
-    decay_ref[...] = decay
-    scale_ref[...] = scale
+    decay, scale = decay_ref[...], scale_ref[...]
     group = sub_ids((SUBS, LANES)) // kept
     subs = sub_ids((SUBS, LANES))
     energy = jnp.zeros((SUBS, LANES), jnp.float32)
@@ -241,64 +262,113 @@
     message_ref[2 * radix] = energy
 
 
-def join(level, cells, groups, own, other, decay, scale, slab):
+def facing(level):
+    low = sub_ids((SUBS, LANES)) < HALF
+    right = lax.rem(lax.shift_right_logical(lax.axis_index("gz"), level), 2)
+    return jnp.where(low, 1, 0) != right, right
+
+
+def join(level, cells, groups, own, other, decay, scale):
     radix = decay.shape[0]
     kept = SUBS // groups
-    subs = sub_ids((SUBS, LANES))
-    right = lax.rem(lax.shift_right_logical(slab, level), 2)
-    mine = jnp.where(subs < HALF, 1, 0) != right
-    energy = own[2 * radix] + other[2 * radix]
+    outer, _ = facing(level)
     joined, couple = [], jnp.zeros((SUBS, LANES), jnp.float32)
     for i in range(2 * radix):
         d, g = decay[i % radix], scale[i % radix]
         span = power(d, cells << level)
-        mate = other[i]
-        joined.append(jnp.where(mine, mate + span * own[i], own[i] + span * mate))
-        couple = couple + (2.0 * g * d) * jnp.where(mine, own[i] * turn(mate, HALF), 0.0)
+        joined.append(jnp.where(outer, other[i] + span * own[i], own[i] + span * other[i]))
+        couple = couple + (2.0 * g * d) * jnp.where(outer, own[i] * turn(other[i], HALF), 0.0)
     couple = couple + turn(couple, HALF)
-    energy = energy + jnp.where(subs < kept, couple, 0.0)
-    return joined, energy
+    joined.append(own[-1] + other[-1] + jnp.where(sub_ids((SUBS, LANES)) < kept, couple, 0.0))
+    return joined
+
+
+def rows_of(ref):
+    return [ref[i] for i in range(ref.shape[0])]
 
 
 def join_kernel(level, cells, groups, own_ref, other_ref, decay_ref, scale_ref, out_ref):
-    joined, energy = join(
-        level, cells, groups, own_ref, other_ref, decay_ref[...], scale_ref[...], lax.axis_index("gz")
-    )
+    joined = join(level, cells, groups, rows_of(own_ref), rows_of(other_ref), decay_ref[...], scale_ref[...])
     for i, value in enumerate(joined):
         out_ref[i] = value
-    out_ref[len(joined)] = energy
+
+
+def join_two_kernel(
+    level, cells, groups, own_ref, one_ref, two_ref, cross_ref, decay_ref, scale_ref, out_ref, near_ref, pair_ref
+):
+    decay, scale = decay_ref[...], scale_ref[...]
+    odd = lax.rem(lax.axis_index("gz"), 2) == 1
+    near = [jnp.where(odd, b, a) for a, b in zip(rows_of(one_ref), rows_of(two_ref))]
+    far = [jnp.where(odd, a, b) for a, b in zip(rows_of(one_ref), rows_of(two_ref))]
+    own = join(level, cells, groups, rows_of(own_ref), near, decay, scale)
+    other = join(level, cells, groups, far, rows_of(cross_ref), decay, scale)
+    joined = join(level + 1, cells, groups, own, other, decay, scale)
+    for i in range(len(joined)):
+        out_ref[i] = joined[i]
+        near_ref[i] = near[i]
+        pair_ref[i] = other[i]
+
+
+def edge_kernel(level, cells, groups, own_ref, decay_ref, scale_ref, out_ref):
+    radix = decay_ref.shape[0]
+    kept = SUBS // groups
+    subs = sub_ids((SUBS, LANES))
+    outer, _ = facing(level)
+    walls = jnp.zeros((SUBS, LANES), jnp.float32)
+    for a in range(radix):
+        d = decay_ref[a]
+        image = power(d, (cells << level) + 1)
+        both = []
+        for part in range(2):
+            own = own_ref[part * radix + a]
+            near = jnp.where(outer, 0.0, own)
+            walls = walls + (scale_ref[a] * d * d) * (near * near)
+            sent = own - image * turn(own, HALF)
+            both.append(jnp.where(outer, sent, turn(sent, HALF)))
+        out_ref[a] = jnp.where(subs < HALF, both[0], both[1])
+    out_ref[radix] = own_ref[2 * radix] - jnp.where(lax.rem(subs, HALF) < kept, walls, 0.0)
 
 
 def backward_kernel(groups, slabs, *refs):
     levels = slabs.bit_length() - 1
-    own_ref, received = refs[0], refs[1 : 1 + levels]
-    local_ref, decay_ref, scale_ref, lane_ref, twiddle_ref = refs[1 + levels : 6 + levels]
-    out_refs, energy_refs = refs[6 + levels : 6 + levels + groups], refs[6 + levels + groups :]
+    own_ref, received = refs[0], refs[1:levels]
+    edge_ref, other_ref, local_ref, decay_ref, scale_ref, lane_ref, twiddle_ref = refs[levels : levels + 7]
+    out_refs = refs[levels + 7 :]
     _, radix, inner, _, _ = local_ref.shape
     kept, cells = SUBS // groups, inner * groups
-    me, slab = lax.axis_index("gy"), lax.axis_index("gz")
+    me = lax.axis_index("gy")
     decay, scale = decay_ref[...], scale_ref[...]
     subs = sub_ids((SUBS, LANES))
-    totals, energy = join(levels - 1, cells, groups, own_ref, received[-1], decay, scale, slab)
     low = subs < HALF
-    fields, walls = ([], []), jnp.zeros((SUBS, LANES), jnp.float32)
+    outers = [facing(level)[0] for level in range(levels)]
+    right = facing(levels - 1)[1] == 1
+    couple = jnp.zeros((SUBS, LANES), jnp.float32)
+    fields = ([], [])
     ahead, behind = group_powers(decay, inner, groups, kept)
-    for part in range(2):
-        for a in range(radix):
-            i, d = part * radix + a, decay[a]
-            span, weight = power(d, cells), jnp.ones_like(d)
-            incoming = jnp.zeros_like(d)
-            for level in range(levels):
-                right = lax.rem(lax.shift_right_logical(slab, level), 2)
-                mine = jnp.where(low, 1, 0) != right
-                incoming = incoming + jnp.where(mine, 0.0, weight * received[level][i])
-                weight = weight * jnp.where(mine, 1.0, span)
-                span = span * span
-            far = span * d
-            turned = turn(totals[i], HALF)
-            image = d * (turned - far * totals[i]) / (1.0 - far * far)
-            walls = walls + (scale[a] * d) * (turned * image)
-            incoming = incoming - weight * image
+    for a in range(radix):
+        d = decay[a]
+        spans = [power(d, cells)]
+        for level in range(1, levels + 1):
+            spans.append(spans[-1] * spans[-1])
+        far = spans[levels] * d
+        image = spans[levels - 1] * d
+        rest = 1.0 / (1.0 - far * far)
+        edge, other = edge_ref[a], other_ref[a]
+        edge_turned, other_turned = turn(edge, HALF), turn(other, HALF)
+        for part in range(2):
+            i = part * radix + a
+            weight, incoming = jnp.ones_like(d), jnp.zeros_like(d)
+            for level in range(levels - 1):
+                incoming = incoming + jnp.where(outers[level], 0.0, weight * received[level][i])
+                weight = weight * jnp.where(outers[level], 1.0, spans[level])
+            mine = jnp.where(low, edge, edge_turned) if part == 0 else jnp.where(low, edge_turned, edge)
+            theirs = jnp.where(low, other, other_turned) if part == 0 else jnp.where(low, other_turned, other)
+            entering = rest * (theirs - far * mine)
+            leaving = rest * (mine - far * theirs)
+            here, there = mine * entering, theirs * leaving
+            couple = couple + (scale[a] * d) * (jnp.where(right, there, here) + jnp.where(right, here, there))
+            wall = d * turn(own_ref[i], HALF) + image * entering
+            incoming = incoming + weight * jnp.where(outers[levels - 1], -wall, entering)
             turned = turn(incoming, HALF)
             from_low = ahead[a] * jnp.where(low, incoming, turned)
             from_high = behind[a] * jnp.where(low, turned, incoming)
@@ -310,7 +380,7 @@
                     ]
                 )
             )
-    energy = energy - jnp.where(lax.rem(subs, HALF) < kept, walls, 0.0)
+    energy = edge_ref[radix] + other_ref[radix] + jnp.where(subs < kept, couple, 0.0)
     re, im = lane_product(fields[0], fields[1], lane_ref)
     turned_re, turned_im = [], []
     for a in range(radix):
@@ -330,30 +400,38 @@
 
 def unpack_kernel(groups, *refs):
     held = refs[:groups]
-    labels_ref, diffusivity_ref, previous_ref, rz_prev_ref = refs[groups : groups + 4]
-    out_ref, direction_ref, total_ref = refs[groups + 4 :]
-    cells, _, waves, planes = out_ref.shape
+    weight_ref, previous_ref, rz_prev_ref = refs[groups : groups + 3]
+    out_ref, direction_ref, total_ref, out_buffer, direction_buffer, total_buffer, sems, total_sem = refs[groups + 3 :]
+    cells, _, waves, planes = out_buffer.shape
     kept, inner, rows = waves // groups, cells // groups, planes // LANES
     me = lax.axis_index("gy")
     block = sub_ids((SUBS, LANES)) // kept
-    weight = cell_weight(labels_ref[...], diffusivity_ref)
     energies = by_source([ref[2 * rows, 0] for ref in held], me)
     total = jnp.sum(sum(energies[1:], energies[0]), axis=(0, 1), keepdims=True)
-    total_ref[...] = total
+    total_buffer[...] = total
+    copies = [pltpu.make_async_copy(total_buffer, total_ref, total_sem)]
+    copies[0].start()
     ratio = total / rz_prev_ref[0]
-    for part in range(2):
-        for a in range(rows):
-            lanes = slice(a * LANES, (a + 1) * LANES)
-            for zp in range(inner):
+    for zp in range(inner):
+        for part in range(2):
+            for a in range(rows):
+                lanes = slice(a * LANES, (a + 1) * LANES)
                 sources = by_source([ref[part * rows + a, zp] for ref in held], me)
                 for zg in range(groups):
                     z = zg * inner + zp
                     value = turn(sources[0], -zg * kept)
                     for t in range(1, groups):
                         value = jnp.where(block == t, turn(sources[t], (t - zg) * kept), value)
-                    value = value * weight[z : z + 1, lanes]
-                    out_ref[z, part, :, lanes] = value
-                    direction_ref[z, part, :, lanes] = value + ratio * previous_ref[z, part, :, lanes]
+                    value = value * weight_ref[z : z + 1, lanes]
+                    out_buffer[z, part, :, lanes] = value
+                    direction_buffer[z, part, :, lanes] = value + ratio * previous_ref[z, part, :, lanes]
+        for zg in range(groups):
+            z = zg * inner + zp
+            for i, (source, target) in enumerate(((out_buffer, out_ref), (direction_buffer, direction_ref))):
+                copies.append(pltpu.make_async_copy(source.at[z], target.at[z], sems.at[i, z]))
+                copies[-1].start()
+    for copy in copies:
+        copy.wait()
 
 
 def float_array(*shape):
@@ -365,7 +443,7 @@
 
 
 def inside(value):
-    return pltpu.with_memory_space_constraint(value, pltpu.VMEM)
+    return pltpu.with_memory_space_constraint(jnp.asarray(value), pltpu.VMEM)
 
 
 def on_device(residual, direction_prev, phase_labels, phase_diffusivity, x_eigen, rz_prev):
@@ -376,33 +454,49 @@
     radix = rows * groups
     distances = [[(i, (i + s) % groups) for i in range(groups)] for s in range(1, groups)]
 
-    pieces = pl.pallas_call(
+    weight, *pieces = pl.pallas_call(
         functools.partial(pack_kernel, groups),
-        out_shape=[held_array(parts, rows, inner, SUBS, LANES)] * groups,
-        in_specs=[VMEM, VMEM, SMEM],
-        out_specs=[VMEM] * groups,
+        out_shape=[held_array(cells, planes)] + [held_array(parts, rows, inner, SUBS, LANES)] * groups,
+        in_specs=[ANY] * 3,
+        out_specs=[VMEM] * (groups + 1),
+        scratch_shapes=[
+            pltpu.VMEM(residual.shape, jnp.float32),
+            pltpu.VMEM(phase_labels.shape, jnp.int32),
+            pltpu.SMEM(phase_diffusivity.shape, jnp.float32),
+            pltpu.SemaphoreType.DMA((cells,)),
+            pltpu.SemaphoreType.DMA,
+            pltpu.SemaphoreType.DMA,
+        ],
         name="pack",
     )(residual, phase_labels, phase_diffusivity)
     held = [pieces[0]] + [lax.ppermute(x, "gy", d) for x, d in zip(pieces[1:], distances)]
-
-    message, local, decay, scale = pl.pallas_call(
+    decay, scale = pl.pallas_call(
+        functools.partial(roots_kernel, groups),
+        out_shape=[held_array(radix, SUBS, LANES)] * 2,
+        in_specs=[VMEM, SMEM],
+        out_specs=[VMEM] * 2,
+        name="roots",
+    )(inside(y_eigen(radix)), x_eigen)
+
+    message, local = pl.pallas_call(
         functools.partial(forward_kernel, groups),
         out_shape=[
             held_array(parts * radix + 1, SUBS, LANES),
             held_array(parts, radix, inner, SUBS, LANES),
-            held_array(radix, SUBS, LANES),
-            held_array(radix, SUBS, LANES),
         ],
-        in_specs=[VMEM] * (groups + 3) + [SMEM],
-        out_specs=[VMEM] * 4,
+        in_specs=[VMEM] * (groups + 4),
+        out_specs=[VMEM] * 2,
         name="forward",
-    )(*map(inside, held), lane_transform(-1.0), twiddles(radix), y_eigen(radix), x_eigen)
-
-    received = []
-    for level in range(levels):
-        swap = [(i, i ^ (1 << level)) for i in range(slabs)]
-        received.append(lax.ppermute(message, "gz", swap))
-        if level < levels - 1:
+    )(*map(inside, (*held, lane_transform(-1.0), twiddles(radix), decay, scale)))
+
+    def swapped(value, even, odd):
+        return lax.ppermute(value, "gz", [(i, i ^ (odd if i & 1 else even)) for i in range(slabs)])
+
+    received, level = [], 0
+    while level < levels - 1:
+        one_bit, next_bit = 1 << level, 2 << level
+        if level == 0 or level == levels - 2:
+            received.append(swapped(message, one_bit, one_bit))
             message = pl.pallas_call(
                 functools.partial(join_kernel, level, cells, groups),
                 out_shape=held_array(*message.shape),
@@ -410,23 +504,52 @@
                 out_specs=VMEM,
                 name=f"join{level}",
             )(*map(inside, (message, received[-1], decay, scale)))
+            level += 1
+        else:
+            one = swapped(message, one_bit, next_bit)
+            two = swapped(message, next_bit, one_bit)
+            cross = swapped(message, one_bit | next_bit, one_bit | next_bit)
+            message, near, pair = pl.pallas_call(
+                functools.partial(join_two_kernel, level, cells, groups),
+                out_shape=[held_array(*message.shape)] * 3,
+                in_specs=[VMEM] * 6,
+                out_specs=[VMEM] * 3,
+                name=f"join{level}",
+            )(*map(inside, (message, one, two, cross, decay, scale)))
+            received += [near, pair]
+            level += 2
+    edge = pl.pallas_call(
+        functools.partial(edge_kernel, level, cells, groups),
+        out_shape=held_array(radix + 1, SUBS, LANES),
+        in_specs=[VMEM] * 3,
+        out_specs=VMEM,
+        name="edge",
+    )(*map(inside, (message, decay, scale)))
+    other = swapped(edge, 1 << level, 1 << level)
 
     pieces = pl.pallas_call(
         functools.partial(backward_kernel, groups, slabs),
         out_shape=[held_array(parts * rows + 1, inner, SUBS, LANES)] * groups,
-        in_specs=[VMEM] * (6 + levels),
+        in_specs=[VMEM] * (levels + 7),
         out_specs=[VMEM] * groups,
         name="backward",
-    )(*map(inside, (message, *received, local, decay, scale)), lane_transform(1.0), twiddles(radix))
+    )(*map(inside, (message, *received, edge, other, local, decay, scale, lane_transform(1.0), twiddles(radix))))
     held = [pieces[0]] + [lax.ppermute(x, "gy", d) for x, d in zip(pieces[1:], distances)]
 
     preconditioned, direction, total = pl.pallas_call(
         functools.partial(unpack_kernel, groups),
         out_shape=[float_array(*residual.shape), float_array(*residual.shape), float_array(1, 1)],
-        in_specs=[VMEM] * (groups + 1) + [SMEM, VMEM, SMEM],
-        out_specs=[VMEM] * 3,
+        in_specs=[VMEM] * (groups + 2) + [SMEM],
+        out_specs=[ANY] * 3,
+        scratch_shapes=[
+            pltpu.VMEM(residual.shape, jnp.float32),
+            pltpu.VMEM(residual.shape, jnp.float32),
+            pltpu.VMEM((1, 1), jnp.float32),
+            pltpu.SemaphoreType.DMA((2, cells)),
+            pltpu.SemaphoreType.DMA,
+        ],
         name="unpack",
-    )(*map(inside, held), phase_labels, phase_diffusivity, direction_prev, rz_prev)
+    )(*map(inside, (*held, weight, direction_prev)), rz_prev)
     return preconditioned, direction, jnp.reshape(total, (1,))
 
 

time: 33.7 us -> 30.9 us (0.917)
  Pallas kernels: 5.71 us -> 3.73 us
  starting transfers between devices: 11.5 us -> 10.8 us
    pallas_call x1, Pallas kernels: 1.37 us -> 0.37 us  [on_device(): pl.pallas_call(functools.partial(forward_kernel, groups), out_shape=[held...]
    pallas_call x1, Pallas kernels: 1.34 us -> 0.4 us  [on_device(): pl.pallas_call(functools.partial(backward_kernel, groups, slabs), out_sha...]
    pallas_call x0 -> x3, Pallas kernels: none -> 0.83 us  [the longest x1 0.7 us: on_device(): pl.pallas_call(functools.partial(roots_kernel, groups), out_shape=[held_a...]
    pallas_call x1, Pallas kernels: 1.86 us -> 1.05 us  [on_device(): pl.pallas_call(functools.partial(unpack_kernel, groups), out_shape=[float...]
    ppermute x2, waiting for transfers between devices: 6.25 us -> 5.78 us  [on_device(): lax.ppermute(x, 'gy', d)]
    ppermute x4 -> x5, starting transfers between devices: 6.69 us -> 6.28 us  [swapped(): lax.ppermute(value, 'gz', [(i, i ^ (odd if i & 1 else even)) for i in ran...]
    ppermute x4 -> x5, waiting for transfers between devices: 8.64 us -> 8.95 us  [swapped(): lax.ppermute(value, 'gz', [(i, i ^ (odd if i & 1 else even)) for i in ran...]
  transfers between devices with their start and end apart: 6 -> 7, of which waited for: 6 -> 7; matrix products, arithmetic and copies ran while one was open for 0% -> 0% of each run, Pallas kernels for 0% -> 2%
where the time goes in v2:
time: 30.9 us; the launch traced here: 30.7 us
  waiting for transfers between devices  14.7 us (48%)
  starting transfers between devices  10.8 us (35%)
  Pallas kernels  3.73 us (12%)
  between operations  1.37 us (4%)
    ppermute x5, waiting for transfers between devices, swapped(): lax.ppermute(value, 'gz', [(i, i ^ (odd if i & 1 else even)) for i in ran...  8.95 us
    ppermute x5, starting transfers between devices, swapped(): lax.ppermute(value, 'gz', [(i, i ^ (odd if i & 1 else even)) for i in ran...  6.28 us
    ppermute x2, waiting for transfers between devices, on_device(): lax.ppermute(x, 'gy', d)  5.78 us
    ppermute x2, starting transfers between devices, on_device(): lax.ppermute(x, 'gy', d)  4.56 us
    pallas_call x1, Pallas kernels, on_device(): pl.pallas_call(functools.partial(unpack_kernel, groups), out_shape=[float...  1.05 us
    pallas_call x1, Pallas kernels, on_device(): pl.pallas_call(functools.partial(pack_kernel, groups), out_shape=[held_ar...  1.04 us
    pallas_call x1, Pallas kernels, on_device(): pl.pallas_call(functools.partial(roots_kernel, groups), out_shape=[held_a...  0.7 us
  transfers between devices with their start and end apart: 7, of which 7 were waited for; matrix products, arithmetic and copies ran while one was open for 0% of the time, Pallas kernels for 2%

profile of v2, /device:TPU:0, one launch (start us, length us, event | category | flops | bytes accessed | tf_op | source)
XLA Modules:
  0.0 30.7 jit_solution(1170382486906151385)
XLA Ops:
  0.6 0.0 copy-start
  0.6 0.0 copy-start.4
  0.7 1.0 %pack.1 = (f32[8,512]{1,0:T(8,128)S(1)}, f32[2,4,4,8,128]{4,3,2,1,0:T(8,128)S(1)}, f32[2,4,4,8,128]{4,3,2,1,0:T(8,128)S(1)}) custom-call(f32[8,2,8,512]{3,2,1,0:T(8,128)} %residual_any.1, s32[8,512]{1,0:T(8,128)} %labels_any.1, f32[3]{0:T(128)} %diffusivity_any.1), custom_call_target="tpu_custom_call" | custom-call | tf_op jit(solution)/shard_map/pack/pallas_call | solution.py:457
  1.7 0.0 copy-start.3
  1.7 3.0 %collective-permute-start = (f32[2,4,4,8,128]{4,3,2,1,0:T(8,128)S(1)}, f32[2,4,4,8,128]{4,3,2,1,0:T(8,128)S(1)}, u32[]{:S(2)}, u32[]{:S(2)}) collective-permute-start(f32[2,4,4,8,128]{4,3,2,1,0:T(8,128)S(1)} %get-tuple-element.19), channel_id=1, source_target_pairs={{0,16},{16,0},{1,17},{17,1},{2,18},{18,2},{3,19},{19,3},{4,20},{20... | collective-permute-start | bytes 393224 | tf_op jit(solution)/shard_map/ppermute | solution.py:472
  4.7 0.0 copy-done.4
  4.7 0.7 %roots.1 = (f32[8,8,128]{2,1,0:T(8,128)S(1)}, f32[8,8,128]{2,1,0:T(8,128)S(1)}) custom-call(f32[8,128]{1,0:T(8,128)S(1)} %copy-done.4, f32[8]{0:T(128)} %eigen_ref.1), custom_call_target="tpu_custom_call" | custom-call | tf_op jit(solution)/shard_map/roots/pallas_call | solution.py:473
  5.4 2.8 %collective-permute-done.refs_1_ = f32[2,4,4,8,128]{4,3,2,1,0:T(8,128)S(1)} collective-permute-done((f32[2,4,4,8,128]{4,3,2,1,0:T(8,128)S(1)}, f32[2,4,4,8,128]{4,3,2,1,0:T(8,128)S(1)}, u32[]{:S(2)}, u32[]{:S(2)}) %collective-permute-start) | collective-permute-done | bytes 131104 | tf_op jit(solution)/shard_map/ppermute | solution.py:472
  8.2 0.0 copy-done
  8.2 0.0 copy-done.3
  8.2 0.4 %forward.1 = (f32[17,8,128]{2,1,0:T(8,128)S(1)}, f32[2,8,4,8,128]{4,3,2,1,0:T(8,128)S(1)}) custom-call(f32[2,4,4,8,128]{4,3,2,1,0:T(8,128)S(1)} %get-tuple-element.18.refs_0_, f32[2,4,4,8,128]{4,3,2,1,0:T(8,128)S(1)} %collective-permute-done.refs_1_, bf16[2,256,256]{2,1,0:T(8,128)(2,1)S(1)} %copy-done, f32[2,8,128]{2,1,0:T(8,128)S(1)} %copy-done.3, ...), custom_call_target="tpu_custom_call" | custom-call | tf_op jit(solution)/shard_map/forward/pallas_call | solution.py:481
  8.6 0.1 collective-permute-start.1
  8.7 1.2 %collective-permute-done.1.other_ref.refs_1_ = f32[17,8,128]{2,1,0:T(8,128)S(1)} collective-permute-done((f32[17,8,128]{2,1,0:T(8,128)S(1)}, f32[17,8,128]{2,1,0:T(8,128)S(1)}, u32[]{:S(2)}, u32[]{:S(2)}) %collective-permute-start.1) | collective-permute-done | bytes 69664 | tf_op jit(solution)/shard_map/ppermute | solution.py:493
  10.0 0.0 copy-start.2
  10.0 1.8 %collective-permute-start.2 = (f32[17,8,128]{2,1,0:T(8,128)S(1)}, f32[17,8,128]{2,1,0:T(8,128)S(1)}, u32[]{:S(2)}, u32[]{:S(2)}) collective-permute-start(f32[17,8,128]{2,1,0:T(8,128)S(1)} %join0.1.own_ref), channel_id=1, source_target_pairs={{0,2},{1,5},{2,0},{3,7},{4,6},{5,1},{6,4},{7,3},{8,10},{9,13},{10,... | collective-permute-start | bytes 208904 | tf_op jit(solution)/shard_map/ppermute | solution.py:493
  11.8 1.6 %collective-permute-start.3 = (f32[17,8,128]{2,1,0:T(8,128)S(1)}, f32[17,8,128]{2,1,0:T(8,128)S(1)}, u32[]{:S(2)}, u32[]{:S(2)}) collective-permute-start(f32[17,8,128]{2,1,0:T(8,128)S(1)} %join0.1.own_ref), channel_id=1, source_target_pairs={{0,4},{1,3},{2,6},{3,1},{4,0},{5,7},{6,2},{7,5},{8,12},{9,11},{10,... | collective-permute-start | bytes 208904 | tf_op jit(solution)/shard_map/ppermute | solution.py:493
  13.4 0.1 collective-permute-start.4
  13.5 0.9 %collective-permute-done.2.one_ref = f32[17,8,128]{2,1,0:T(8,128)S(1)} collective-permute-done((f32[17,8,128]{2,1,0:T(8,128)S(1)}, f32[17,8,128]{2,1,0:T(8,128)S(1)}, u32[]{:S(2)}, u32[]{:S(2)}) %collective-permute-start.2) | collective-permute-done | bytes 69664 | tf_op jit(solution)/shard_map/ppermute | solution.py:493
  14.4 2.3 %collective-permute-done.3.two_ref = f32[17,8,128]{2,1,0:T(8,128)S(1)} collective-permute-done((f32[17,8,128]{2,1,0:T(8,128)S(1)}, f32[17,8,128]{2,1,0:T(8,128)S(1)}, u32[]{:S(2)}, u32[]{:S(2)}) %collective-permute-start.3) | collective-permute-done | bytes 69664 | tf_op jit(solution)/shard_map/ppermute | solution.py:493
  16.7 1.9 %collective-permute-done.4.cross_ref = f32[17,8,128]{2,1,0:T(8,128)S(1)} collective-permute-done((f32[17,8,128]{2,1,0:T(8,128)S(1)}, f32[17,8,128]{2,1,0:T(8,128)S(1)}, u32[]{:S(2)}, u32[]{:S(2)}) %collective-permute-start.4) | collective-permute-done | bytes 69664 | tf_op jit(solution)/shard_map/ppermute | solution.py:493
  18.6 0.1 join1.1
  18.7 2.7 %collective-permute-start.5 = (f32[9,8,128]{2,1,0:T(8,128)S(1)}, f32[9,8,128]{2,1,0:T(8,128)S(1)}, u32[]{:S(2)}, u32[]{:S(2)}) collective-permute-start(f32[9,8,128]{2,1,0:T(8,128)S(1)} %edge.1.refs_4_), channel_id=1, source_target_pairs={{0,8},{1,9},{2,10},{3,11},{4,12},{5,13},{6,14},{7,15},{8,0},{9,1},... | collective-permute-start | bytes 110600 | tf_op jit(solution)/shard_map/ppermute | solution.py:493
  21.4 2.6 %collective-permute-done.5.refs_5_ = f32[9,8,128]{2,1,0:T(8,128)S(1)} collective-permute-done((f32[9,8,128]{2,1,0:T(8,128)S(1)}, f32[9,8,128]{2,1,0:T(8,128)S(1)}, u32[]{:S(2)}, u32[]{:S(2)}) %collective-permute-start.5) | collective-permute-done | bytes 36896 | tf_op jit(solution)/shard_map/ppermute | solution.py:493
  24.0 0.0 copy-done.2
  24.0 0.0 copy-start.1
  24.0 0.4 %backward.1 = (f32[9,4,8,128]{3,2,1,0:T(8,128)S(1)}, f32[9,4,8,128]{3,2,1,0:T(8,128)S(1)}) custom-call(f32[17,8,128]{2,1,0:T(8,128)S(1)} %get-tuple-element.23.own_ref.refs_0_, f32[17,8,128]{2,1,0:T(8,128)S(1)} %collective-permute-done.1.other_ref.refs_1_, f32[17,8,128]{2,1,0:T(8,128)S(1)} %get-tuple-element.24.refs_2_, ...), custom_call_target="tpu_custom_call" | custom-call | tf_op jit(solution)/shard_map/backward/pallas_call | solution.py:530
  24.4 1.6 %collective-permute-start.6 = (f32[9,4,8,128]{3,2,1,0:T(8,128)S(1)}, f32[9,4,8,128]{3,2,1,0:T(8,128)S(1)}, u32[]{:S(2)}, u32[]{:S(2)}) collective-permute-start(f32[9,4,8,128]{3,2,1,0:T(8,128)S(1)} %get-tuple-element.28), channel_id=1, source_target_pairs={{0,16},{16,0},{1,17},{17,1},{2,18},{18,2},{3,19},{19,3},{4,20},{20... | collective-permute-start | bytes 442376 | tf_op jit(solution)/shard_map/ppermute | solution.py:537
  26.6 3.0 %collective-permute-done.6.refs_1_ = f32[9,4,8,128]{3,2,1,0:T(8,128)S(1)} collective-permute-done((f32[9,4,8,128]{3,2,1,0:T(8,128)S(1)}, f32[9,4,8,128]{3,2,1,0:T(8,128)S(1)}, u32[]{:S(2)}, u32[]{:S(2)}) %collective-permute-start.6) | collective-permute-done | bytes 147488 | tf_op jit(solution)/shard_map/ppermute | solution.py:537
  29.6 0.0 copy-done.1
  29.6 1.0 %unpack.1 = (f32[8,2,8,512]{3,2,1,0:T(8,128)}, f32[8,2,8,512]{3,2,1,0:T(8,128)}, f32[1,1]{1,0:T(1,128)}) custom-call(f32[9,4,8,128]{3,2,1,0:T(8,128)S(1)} %get-tuple-element.27.refs_0_, f32[9,4,8,128]{3,2,1,0:T(8,128)S(1)} %collective-permute-done.6.refs_1_, f32[8,512]{1,0:T(8,128)S(1)} %get-tuple-element.29.refs_2_, f32[8,2,8,512]{3,2,1,0:T(8,128)S(1)} %copy-done.1, ...), custom_call_target="tpu_custom_call" | custom-call | tf_op jit(solution)/shard_map/unpack/pallas_call | solution.py:539
  (2 shorter events, 0.1 us)
Async XLA Ops:
  0.6 7.6 %copy-start = (bf16[2,256,256]{2,1,0:T(8,128)(2,1)S(1)}, bf16[2,256,256]{2,1,0:T(8,128)(2,1)}, u32[]{:S(2)}) copy-start(bf16[2,256,256]{2,1,0:T(8,128)(2,1)} %constant.9.clone.refs_2_) | copy-start | bytes 786436
  0.6 4.1 %copy-start.4 = (f32[8,128]{1,0:T(8,128)S(1)}, f32[8,128]{1,0:T(8,128)}, u32[]{:S(2)}) copy-start(f32[8,128]{1,0:T(8,128)} %constant.8.clone.y_eigen_ref) | copy-start | bytes 12292
  1.7 6.5 %copy-start.3 = (f32[2,8,128]{2,1,0:T(8,128)S(1)}, f32[2,8,128]{2,1,0:T(8,128)}, u32[]{:S(2)}) copy-start(f32[2,8,128]{2,1,0:T(8,128)} %constant.10.clone.refs_3_.refs_10_) | copy-start | bytes 24580
  1.7 6.5 %collective-permute-start = (f32[2,4,4,8,128]{4,3,2,1,0:T(8,128)S(1)}, f32[2,4,4,8,128]{4,3,2,1,0:T(8,128)S(1)}, u32[]{:S(2)}, u32[]{:S(2)}) collective-permute-start(f32[2,4,4,8,128]{4,3,2,1,0:T(8,128)S(1)} %get-tuple-element.19), channel_id=1, source_target_pairs={{0,16},{16,0},{1,17},{17,1},{2,18},{18,2},{3,19},{19,3},{4,20},{20... | collective-permute-start | bytes 393224 | tf_op jit(solution)/shard_map/ppermute | solution.py:472
  8.6 1.3 %collective-permute-start.1 = (f32[17,8,128]{2,1,0:T(8,128)S(1)}, f32[17,8,128]{2,1,0:T(8,128)S(1)}, u32[]{:S(2)}, u32[]{:S(2)}) collective-permute-start(f32[17,8,128]{2,1,0:T(8,128)S(1)} %get-tuple-element.22.own_ref), channel_id=1, source_target_pairs={{0,1},{1,0},{2,3},{3,2},{4,5},{5,4},{6,7},{7,6},{8,9},{9,8},{10,11... | collective-permute-start | bytes 208904 | tf_op jit(solution)/shard_map/ppermute | solution.py:493
  10.0 14.1 %copy-start.2 = (bf16[2,256,256]{2,1,0:T(8,128)(2,1)S(1)}, bf16[2,256,256]{2,1,0:T(8,128)(2,1)}, u32[]{:S(2)}) copy-start(bf16[2,256,256]{2,1,0:T(8,128)(2,1)} %constant.11.clone.refs_9_) | copy-start | bytes 786436
  10.0 4.4 %collective-permute-start.2 = (f32[17,8,128]{2,1,0:T(8,128)S(1)}, f32[17,8,128]{2,1,0:T(8,128)S(1)}, u32[]{:S(2)}, u32[]{:S(2)}) collective-permute-start(f32[17,8,128]{2,1,0:T(8,128)S(1)} %join0.1.own_ref), channel_id=1, source_target_pairs={{0,2},{1,5},{2,0},{3,7},{4,6},{5,1},{6,4},{7,3},{8,10},{9,13},{10,... | collective-permute-start | bytes 208904 | tf_op jit(solution)/shard_map/ppermute | solution.py:493
  11.8 4.9 %collective-permute-start.3 = (f32[17,8,128]{2,1,0:T(8,128)S(1)}, f32[17,8,128]{2,1,0:T(8,128)S(1)}, u32[]{:S(2)}, u32[]{:S(2)}) collective-permute-start(f32[17,8,128]{2,1,0:T(8,128)S(1)} %join0.1.own_ref), channel_id=1, source_target_pairs={{0,4},{1,3},{2,6},{3,1},{4,0},{5,7},{6,2},{7,5},{8,12},{9,11},{10,... | collective-permute-start | bytes 208904 | tf_op jit(solution)/shard_map/ppermute | solution.py:493
  13.4 5.2 %collective-permute-start.4 = (f32[17,8,128]{2,1,0:T(8,128)S(1)}, f32[17,8,128]{2,1,0:T(8,128)S(1)}, u32[]{:S(2)}, u32[]{:S(2)}) collective-permute-start(f32[17,8,128]{2,1,0:T(8,128)S(1)} %join0.1.own_ref), channel_id=1, source_target_pairs={{0,6},{1,7},{2,4},{3,5},{4,2},{5,3},{6,0},{7,1},{8,14},{9,15},{10,... | collective-permute-start | bytes 208904 | tf_op jit(solution)/shard_map/ppermute | solution.py:493
  18.7 5.3 %collective-permute-start.5 = (f32[9,8,128]{2,1,0:T(8,128)S(1)}, f32[9,8,128]{2,1,0:T(8,128)S(1)}, u32[]{:S(2)}, u32[]{:S(2)}) collective-permute-start(f32[9,8,128]{2,1,0:T(8,128)S(1)} %edge.1.refs_4_), channel_id=1, source_target_pairs={{0,8},{1,9},{2,10},{3,11},{4,12},{5,13},{6,14},{7,15},{8,0},{9,1},... | collective-permute-start | bytes 110600 | tf_op jit(solution)/shard_map/ppermute | solution.py:493
  24.0 5.6 %copy-start.1 = (f32[8,2,8,512]{3,2,1,0:T(8,128)S(1)}, f32[8,2,8,512]{3,2,1,0:T(8,128)}, u32[]{:S(2)}) copy-start(f32[8,2,8,512]{3,2,1,0:T(8,128)} %refs_3_.2) | copy-start | bytes 786436
  24.4 5.2 %collective-permute-start.6 = (f32[9,4,8,128]{3,2,1,0:T(8,128)S(1)}, f32[9,4,8,128]{3,2,1,0:T(8,128)S(1)}, u32[]{:S(2)}, u32[]{:S(2)}) collective-permute-start(f32[9,4,8,128]{3,2,1,0:T(8,128)S(1)} %get-tuple-element.28), channel_id=1, source_target_pairs={{0,16},{16,0},{1,17},{17,1},{2,18},{18,2},{3,19},{19,3},{4,20},{20... | collective-permute-start | bytes 442376 | tf_op jit(solution)/shard_map/ppermute | solution.py:537

commit v3 on v2

--- a/solution.py
+++ b/solution.py
@@ -188,11 +188,13 @@
                     ref[part, a, zp] = value
 
 
-def roots_kernel(groups, y_eigen_ref, eigen_ref, decay_ref, scale_ref):
+def roots_kernel(groups, y_eigen_ref, eigen_ref, *out_refs):
     length = y_eigen_ref.shape[0] * LANES
-    decay, scale = mode_roots(eigen_ref, y_eigen_ref, lax.axis_index("gy"), SUBS // groups, length)
-    decay_ref[...] = decay
-    scale_ref[...] = scale
+    for s in range(groups):
+        device = lax.rem(lax.axis_index("gy") + groups - s, groups)
+        decay, scale = mode_roots(eigen_ref, y_eigen_ref, device, SUBS // groups, length)
+        out_refs[2 * s][...] = decay
+        out_refs[2 * s + 1][...] = scale
 
 
 def forward_kernel(groups, *refs):
@@ -329,24 +331,40 @@
     out_ref[radix] = own_ref[2 * radix] - jnp.where(lax.rem(subs, HALF) < kept, walls, 0.0)
 
 
-def backward_kernel(groups, slabs, *refs):
+def to_planes(re, im, lane_ref, twiddle_ref):
+    re, im = lane_product(re, im, lane_ref)
+    turned_re, turned_im = [], []
+    for a in range(len(re)):
+        c, s = twiddle_ref[0, a : a + 1, :], twiddle_ref[1, a : a + 1, :]
+        turned_re.append(re[a] * c - im[a] * s)
+        turned_im.append(im[a] * c + re[a] * s)
+    return small_dft(turned_re, turned_im, 1.0)
+
+
+def local_kernel(groups, local_ref, scale_ref, lane_ref, twiddle_ref, after_ref, *out_refs):
+    radix = scale_ref.shape[0]
+    rows = radix // groups
+    fields = [[scale_ref[a] * local_ref[part, a] for a in range(radix)] for part in range(2)]
+    for part, field in enumerate(to_planes(*fields, lane_ref, twiddle_ref)):
+        for a in range(rows):
+            pieces = [field[t * rows + a] for t in range(groups)]
+            for ref, value in zip(out_refs, for_targets(pieces, lax.axis_index("gy"))):
+                ref[part * rows + a] = value
+
+
+def entering_kernel(groups, slabs, cells, *refs):
     levels = slabs.bit_length() - 1
     own_ref, received = refs[0], refs[1:levels]
-    edge_ref, other_ref, local_ref, decay_ref, scale_ref, lane_ref, twiddle_ref = refs[levels : levels + 7]
-    out_refs = refs[levels + 7 :]
-    _, radix, inner, _, _ = local_ref.shape
-    kept, cells = SUBS // groups, inner * groups
-    me = lax.axis_index("gy")
-    decay, scale = decay_ref[...], scale_ref[...]
+    edge_ref, other_ref, decay_ref, scale_ref, out_ref = refs[levels:]
+    radix = decay_ref.shape[0]
+    kept = SUBS // groups
     subs = sub_ids((SUBS, LANES))
     low = subs < HALF
     outers = [facing(level)[0] for level in range(levels)]
     right = facing(levels - 1)[1] == 1
     couple = jnp.zeros((SUBS, LANES), jnp.float32)
-    fields = ([], [])
-    ahead, behind = group_powers(decay, inner, groups, kept)
     for a in range(radix):
-        d = decay[a]
+        d = decay_ref[a]
         spans = [power(d, cells)]
         for level in range(1, levels + 1):
             spans.append(spans[-1] * spans[-1])
@@ -366,57 +384,65 @@
             entering = rest * (theirs - far * mine)
             leaving = rest * (mine - far * theirs)
             here, there = mine * entering, theirs * leaving
-            couple = couple + (scale[a] * d) * (jnp.where(right, there, here) + jnp.where(right, here, there))
+            couple = couple + (scale_ref[a] * d) * (jnp.where(right, there, here) + jnp.where(right, here, there))
             wall = d * turn(own_ref[i], HALF) + image * entering
-            incoming = incoming + weight * jnp.where(outers[levels - 1], -wall, entering)
+            out_ref[i] = incoming + weight * jnp.where(outers[levels - 1], -wall, entering)
+    out_ref[2 * radix] = edge_ref[radix] + other_ref[radix] + jnp.where(subs < kept, couple, 0.0)
+
+
+def response(groups, inner, entering_ref, decay_ref, scale_ref, lane_ref, twiddle_ref):
+    radix = decay_ref.shape[0]
+    rows = radix // groups
+    low = sub_ids((SUBS, LANES)) < HALF
+    decay = decay_ref[...]
+    ahead, behind = group_powers(decay, inner, groups, SUBS // groups)
+    fields = ([], [])
+    for part in range(2):
+        for a in range(radix):
+            d, incoming = decay[a], entering_ref[part * radix + a]
             turned = turn(incoming, HALF)
-            from_low = ahead[a] * jnp.where(low, incoming, turned)
-            from_high = behind[a] * jnp.where(low, turned, incoming)
+            from_low = scale_ref[a] * ahead[a] * jnp.where(low, incoming, turned)
+            from_high = scale_ref[a] * behind[a] * jnp.where(low, turned, incoming)
             fields[part].append(
-                jnp.stack(
-                    [
-                        scale[a] * (local_ref[part, a, z] + power(d, z + 1) * from_low + power(d, inner - z) * from_high)
-                        for z in range(inner)
-                    ]
-                )
+                jnp.stack([power(d, z + 1) * from_low + power(d, inner - z) * from_high for z in range(inner)])
             )
-    energy = edge_ref[radix] + other_ref[radix] + jnp.where(subs < kept, couple, 0.0)
-    re, im = lane_product(fields[0], fields[1], lane_ref)
-    turned_re, turned_im = [], []
-    for a in range(radix):
-        c, s = twiddle_ref[0, a : a + 1, :], twiddle_ref[1, a : a + 1, :]
-        turned_re.append(re[a] * c - im[a] * s)
-        turned_im.append(im[a] * c + re[a] * s)
-    re, im = small_dft(turned_re, turned_im, 1.0)
-    rows = radix // groups
-    for part, field in enumerate((re, im)):
+    planes = to_planes(*fields, lane_ref, twiddle_ref)
+    me = lax.axis_index("gy")
+    return [[for_targets([field[t * rows + a] for t in range(groups)], me)[0] for a in range(rows)] for field in planes]
+
+
+def own_kernel(groups, entering_ref, decay_ref, scale_ref, lane_ref, twiddle_ref, local_ref, out_ref):
+    rows, inner = local_ref.shape[0] // 2, local_ref.shape[1]
+    field = response(groups, inner, entering_ref, decay_ref, scale_ref, lane_ref, twiddle_ref)
+    for part in range(2):
         for a in range(rows):
-            pieces = [field[t * rows + a] for t in range(groups)]
-            for ref, value in zip(out_refs, for_targets(pieces, me)):
-                ref[part * rows + a] = value
-    for ref in out_refs:
-        ref[2 * rows] = jnp.stack([energy] * inner)
-
-
-def unpack_kernel(groups, *refs):
-    held = refs[:groups]
-    weight_ref, previous_ref, rz_prev_ref = refs[groups : groups + 3]
-    out_ref, direction_ref, total_ref, out_buffer, direction_buffer, total_buffer, sems, total_sem = refs[groups + 3 :]
+            out_ref[part * rows + a] = field[part][a] + local_ref[part * rows + a]
+
+
+def finish_kernel(groups, *refs):
+    entering, parts = refs[:groups], refs[groups : 2 * groups]
+    roots = refs[2 * groups : 4 * groups]
+    lane_ref, twiddle_ref, weight_ref, previous_ref, rz_prev_ref = refs[4 * groups : 4 * groups + 5]
+    out_ref, direction_ref, total_ref, out_buffer, direction_buffer, total_buffer, sems, total_sem = refs[4 * groups + 5 :]
     cells, _, waves, planes = out_buffer.shape
     kept, inner, rows = waves // groups, cells // groups, planes // LANES
     me = lax.axis_index("gy")
     block = sub_ids((SUBS, LANES)) // kept
-    energies = by_source([ref[2 * rows, 0] for ref in held], me)
+    energies = by_source([ref[ref.shape[0] - 1] for ref in entering], me)
     total = jnp.sum(sum(energies[1:], energies[0]), axis=(0, 1), keepdims=True)
     total_buffer[...] = total
     copies = [pltpu.make_async_copy(total_buffer, total_ref, total_sem)]
     copies[0].start()
     ratio = total / rz_prev_ref[0]
+    held = [[[parts[0][part * rows + a] for a in range(rows)] for part in range(2)]]
+    for s in range(1, groups):
+        field = response(groups, inner, entering[s], roots[2 * s], roots[2 * s + 1], lane_ref, twiddle_ref)
+        held.append([[field[part][a] + parts[s][part * rows + a] for a in range(rows)] for part in range(2)])
     for zp in range(inner):
         for part in range(2):
             for a in range(rows):
                 lanes = slice(a * LANES, (a + 1) * LANES)
-                sources = by_source([ref[part * rows + a, zp] for ref in held], me)
+                sources = by_source([fields[part][a][zp] for fields in held], me)
                 for zg in range(groups):
                     z = zg * inner + zp
                     value = turn(sources[0], -zg * kept)
@@ -470,13 +496,14 @@
         name="pack",
     )(residual, phase_labels, phase_diffusivity)
     held = [pieces[0]] + [lax.ppermute(x, "gy", d) for x, d in zip(pieces[1:], distances)]
-    decay, scale = pl.pallas_call(
+    roots = pl.pallas_call(
         functools.partial(roots_kernel, groups),
-        out_shape=[held_array(radix, SUBS, LANES)] * 2,
+        out_shape=[held_array(radix, SUBS, LANES)] * (2 * groups),
         in_specs=[VMEM, SMEM],
-        out_specs=[VMEM] * 2,
+        out_specs=[VMEM] * (2 * groups),
         name="roots",
     )(inside(y_eigen(radix)), x_eigen)
+    decay, scale = roots[:2]
 
     message, local = pl.pallas_call(
         functools.partial(forward_kernel, groups),
@@ -492,7 +519,7 @@
     def swapped(value, even, odd):
         return lax.ppermute(value, "gz", [(i, i ^ (odd if i & 1 else even)) for i in range(slabs)])
 
-    received, level = [], 0
+    received, level, after = [], 0, None
     while level < levels - 1:
         one_bit, next_bit = 1 << level, 2 << level
         if level == 0 or level == levels - 2:
@@ -507,6 +534,7 @@
             level += 1
         else:
             one = swapped(message, one_bit, next_bit)
+            after = one if after is None else after
             two = swapped(message, next_bit, one_bit)
             cross = swapped(message, one_bit | next_bit, one_bit | next_bit)
             message, near, pair = pl.pallas_call(
@@ -518,6 +546,17 @@
             )(*map(inside, (message, one, two, cross, decay, scale)))
             received += [near, pair]
             level += 2
+    tables = (lane_transform(1.0), twiddles(radix))
+    piece = held_array(parts * rows, inner, SUBS, LANES)
+    pieces = pl.pallas_call(
+        functools.partial(local_kernel, groups),
+        out_shape=[piece] * groups,
+        in_specs=[VMEM] * 5,
+        out_specs=[VMEM] * groups,
+        name="local",
+    )(*map(inside, (local, scale, *tables, received[0] if after is None else after)))
+    held = [lax.ppermute(x, "gy", d) for x, d in zip(pieces[1:], distances)]
+
     edge = pl.pallas_call(
         functools.partial(edge_kernel, level, cells, groups),
         out_shape=held_array(radix + 1, SUBS, LANES),
@@ -526,20 +565,26 @@
         name="edge",
     )(*map(inside, (message, decay, scale)))
     other = swapped(edge, 1 << level, 1 << level)
-
-    pieces = pl.pallas_call(
-        functools.partial(backward_kernel, groups, slabs),
-        out_shape=[held_array(parts * rows + 1, inner, SUBS, LANES)] * groups,
-        in_specs=[VMEM] * (levels + 7),
-        out_specs=[VMEM] * groups,
-        name="backward",
-    )(*map(inside, (message, *received, edge, other, local, decay, scale, lane_transform(1.0), twiddles(radix))))
-    held = [pieces[0]] + [lax.ppermute(x, "gy", d) for x, d in zip(pieces[1:], distances)]
+    entering = pl.pallas_call(
+        functools.partial(entering_kernel, groups, slabs, cells),
+        out_shape=held_array(*message.shape),
+        in_specs=[VMEM] * (levels + 4),
+        out_specs=VMEM,
+        name="entering",
+    )(*map(inside, (message, *received, edge, other, decay, scale)))
+    entered = [entering] + [lax.ppermute(entering, "gy", d) for d in distances]
+    own = pl.pallas_call(
+        functools.partial(own_kernel, groups),
+        out_shape=piece,
+        in_specs=[VMEM] * 6,
+        out_specs=VMEM,
+        name="own",
+    )(*map(inside, (entering, decay, scale, *tables, pieces[0])))
 
     preconditioned, direction, total = pl.pallas_call(
-        functools.partial(unpack_kernel, groups),
+        functools.partial(finish_kernel, groups),
         out_shape=[float_array(*residual.shape), float_array(*residual.shape), float_array(1, 1)],
-        in_specs=[VMEM] * (groups + 2) + [SMEM],
+        in_specs=[VMEM] * (4 * groups + 4) + [SMEM],
         out_specs=[ANY] * 3,
         scratch_shapes=[
             pltpu.VMEM(residual.shape, jnp.float32),
@@ -548,8 +593,8 @@
             pltpu.SemaphoreType.DMA((2, cells)),
             pltpu.SemaphoreType.DMA,
         ],
-        name="unpack",
-    )(*map(inside, (*held, weight, direction_prev)), rz_prev)
+        name="finish",
+    )(*map(inside, (*entered, own, *held, *roots, *tables, weight, direction_prev)), rz_prev)
     return preconditioned, direction, jnp.reshape(total, (1,))
 
 

time: 30.9 us -> 28.6 us (0.926)
  waiting for transfers between devices: 14.7 us -> 10.1 us
  starting transfers between devices: 10.8 us -> 12.6 us
  Pallas kernels: 3.73 us -> 4.31 us
    ppermute x5, waiting for transfers between devices: 8.95 us -> 5.49 us  [swapped(): lax.ppermute(value, 'gz', [(i, i ^ (odd if i & 1 else even)) for i in ran...]
    ppermute x0 -> x2, starting transfers between devices: none -> 3.36 us  [the longest x1 1.81 us: on_device(): held = [lax.ppermute(x, 'gy', d) for x, d in zip(pieces[1:], distances)]]
    ppermute x2 -> x1, waiting for transfers between devices: 5.78 us -> 2.76 us  [on_device(): lax.ppermute(x, 'gy', d)]
    ppermute x0 -> x2, waiting for transfers between devices: none -> 1.84 us  [the longest x1 1.83 us: on_device(): entered = [entering] + [lax.ppermute(entering, 'gy', d) for d in distances]]
    ppermute x2 -> x1, starting transfers between devices: 4.56 us -> 3 us  [on_device(): lax.ppermute(x, 'gy', d)]
    pallas_call x2 -> x4, Pallas kernels: 1.44 us -> 2.01 us  [the longest x1 1.28 us: on_device(): pl.pallas_call(functools.partial(finish_kernel, groups), out_shape=[float...]
  transfers between devices with their start and end apart: 7 -> 8, of which waited for: 7 -> 7; matrix products, arithmetic and copies ran while one was open for 0% -> 0% of each run, Pallas kernels for 2% -> 6%
where the time goes in v3:
time: 28.6 us; the launch traced here: 28.5 us
  starting transfers between devices  12.6 us (44%)
  waiting for transfers between devices  10.1 us (35%)
  Pallas kernels  4.31 us (15%)
  between operations  1.39 us (5%)
    ppermute x5, starting transfers between devices, swapped(): lax.ppermute(value, 'gz', [(i, i ^ (odd if i & 1 else even)) for i in ran...  6.28 us
    ppermute x5, waiting for transfers between devices, swapped(): lax.ppermute(value, 'gz', [(i, i ^ (odd if i & 1 else even)) for i in ran...  5.49 us
    ppermute x1, starting transfers between devices, on_device(): lax.ppermute(x, 'gy', d)  3 us
    ppermute x1, waiting for transfers between devices, on_device(): lax.ppermute(x, 'gy', d)  2.76 us
    ppermute x1, waiting for transfers between devices, on_device(): entered = [entering] + [lax.ppermute(entering, 'gy', d) for d in distances]  1.83 us
    ppermute x1, starting transfers between devices, on_device(): held = [lax.ppermute(x, 'gy', d) for x, d in zip(pieces[1:], distances)]  1.81 us
    ppermute x1, starting transfers between devices, on_device(): entered = [entering] + [lax.ppermute(entering, 'gy', d) for d in distances]  1.56 us
    pallas_call x1, Pallas kernels, on_device(): pl.pallas_call(functools.partial(finish_kernel, groups), out_shape=[float...  1.28 us
  transfers between devices with their start and end apart: 8, of which 7 were waited for; matrix products, arithmetic and copies ran while one was open for 0% of the time, Pallas kernels for 6%

profile of v3, /device:TPU:0, one launch (start us, length us, event | category | flops | bytes accessed | tf_op | source)
XLA Modules:
  0.0 28.5 jit_solution(9673314567321728574)
XLA Ops:
  0.6 0.0 copy-start.1
  0.6 0.0 copy-start.4
  0.7 1.0 %pack.1 = (f32[8,512]{1,0:T(8,128)S(1)}, f32[2,4,4,8,128]{4,3,2,1,0:T(8,128)S(1)}, f32[2,4,4,8,128]{4,3,2,1,0:T(8,128)S(1)}) custom-call(f32[8,2,8,512]{3,2,1,0:T(8,128)} %residual_any.1, s32[8,512]{1,0:T(8,128)} %labels_any.1, f32[3]{0:T(128)} %diffusivity_any.1), custom_call_target="tpu_custom_call" | custom-call | tf_op jit(solution)/shard_map/pack/pallas_call | solution.py:483
  1.7 0.0 copy-start.3
  1.7 3.0 %collective-permute-start = (f32[2,4,4,8,128]{4,3,2,1,0:T(8,128)S(1)}, f32[2,4,4,8,128]{4,3,2,1,0:T(8,128)S(1)}, u32[]{:S(2)}, u32[]{:S(2)}) collective-permute-start(f32[2,4,4,8,128]{4,3,2,1,0:T(8,128)S(1)} %get-tuple-element.21), channel_id=1, source_target_pairs={{0,16},{16,0},{1,17},{17,1},{2,18},{18,2},{3,19},{19,3},{4,20},{20... | collective-permute-start | bytes 393224 | tf_op jit(solution)/shard_map/ppermute | solution.py:498
  4.7 0.0 copy-done.4
  4.7 0.7 %roots.1 = (f32[8,8,128]{2,1,0:T(8,128)S(1)}, f32[8,8,128]{2,1,0:T(8,128)S(1)}, f32[8,8,128]{2,1,0:T(8,128)S(1)}, f32[8,8,128]{2,1,0:T(8,128)S(1)}) custom-call(f32[8,128]{1,0:T(8,128)S(1)} %copy-done.4, f32[8]{0:T(128)} %eigen_ref.1), custom_call_target="tpu_custom_call" | custom-call | tf_op jit(solution)/shard_map/roots/pallas_call | solution.py:499
  5.5 2.8 %collective-permute-done.refs_1_ = f32[2,4,4,8,128]{4,3,2,1,0:T(8,128)S(1)} collective-permute-done((f32[2,4,4,8,128]{4,3,2,1,0:T(8,128)S(1)}, f32[2,4,4,8,128]{4,3,2,1,0:T(8,128)S(1)}, u32[]{:S(2)}, u32[]{:S(2)}) %collective-permute-start) | collective-permute-done | bytes 131104 | tf_op jit(solution)/shard_map/ppermute | solution.py:498
  8.2 0.0 copy-done.1
  8.2 0.0 copy-done.3
  8.2 0.4 %forward.1 = (f32[17,8,128]{2,1,0:T(8,128)S(1)}, f32[2,8,4,8,128]{4,3,2,1,0:T(8,128)S(1)}) custom-call(f32[2,4,4,8,128]{4,3,2,1,0:T(8,128)S(1)} %get-tuple-element.20.refs_0_, f32[2,4,4,8,128]{4,3,2,1,0:T(8,128)S(1)} %collective-permute-done.refs_1_, bf16[2,256,256]{2,1,0:T(8,128)(2,1)S(1)} %copy-done.1, f32[2,8,128]{2,1,0:T(8,128)S(1)} %copy-done.3, ...), custom_call_target="tpu_custom_call" | custom-call | tf_op jit(solution)/shard_map/forward/pallas_call | solution.py:508
  8.6 0.0 copy-start
  8.6 0.1 collective-permute-start.1
  8.7 1.2 %collective-permute-done.1.other_ref.refs_1_ = f32[17,8,128]{2,1,0:T(8,128)S(1)} collective-permute-done((f32[17,8,128]{2,1,0:T(8,128)S(1)}, f32[17,8,128]{2,1,0:T(8,128)S(1)}, u32[]{:S(2)}, u32[]{:S(2)}) %collective-permute-start.1) | collective-permute-done | bytes 69664 | tf_op jit(solution)/shard_map/ppermute | solution.py:520
  10.0 1.8 %collective-permute-start.2 = (f32[17,8,128]{2,1,0:T(8,128)S(1)}, f32[17,8,128]{2,1,0:T(8,128)S(1)}, u32[]{:S(2)}, u32[]{:S(2)}) collective-permute-start(f32[17,8,128]{2,1,0:T(8,128)S(1)} %join0.1.own_ref), channel_id=1, source_target_pairs={{0,2},{1,5},{2,0},{3,7},{4,6},{5,1},{6,4},{7,3},{8,10},{9,13},{10,... | collective-permute-start | bytes 208904 | tf_op jit(solution)/shard_map/ppermute | solution.py:520
  11.8 1.5 %collective-permute-start.4 = (f32[17,8,128]{2,1,0:T(8,128)S(1)}, f32[17,8,128]{2,1,0:T(8,128)S(1)}, u32[]{:S(2)}, u32[]{:S(2)}) collective-permute-start(f32[17,8,128]{2,1,0:T(8,128)S(1)} %join0.1.own_ref), channel_id=1, source_target_pairs={{0,6},{1,7},{2,4},{3,5},{4,2},{5,3},{6,0},{7,1},{8,14},{9,15},{10,... | collective-permute-start | bytes 208904 | tf_op jit(solution)/shard_map/ppermute | solution.py:520
  13.3 0.2 collective-permute-start.3
  13.5 0.8 %collective-permute-done.2.one_ref.after_ref = f32[17,8,128]{2,1,0:T(8,128)S(1)} collective-permute-done((f32[17,8,128]{2,1,0:T(8,128)S(1)}, f32[17,8,128]{2,1,0:T(8,128)S(1)}, u32[]{:S(2)}, u32[]{:S(2)}) %collective-permute-start.2) | collective-permute-done | bytes 69664 | tf_op jit(solution)/shard_map/ppermute | solution.py:520
  14.4 0.0 copy-done
  14.4 0.3 %local.1 = (f32[8,4,8,128]{3,2,1,0:T(8,128)S(1)}, f32[8,4,8,128]{3,2,1,0:T(8,128)S(1)}) custom-call(f32[2,8,4,8,128]{4,3,2,1,0:T(8,128)S(1)} %get-tuple-element.28.local_ref, f32[8,8,128]{2,1,0:T(8,128)S(1)} %get-tuple-element.23.refs_5_.scale_ref.refs_7_, bf16[2,256,256]{2,1,0:T(8,128)(2,1)S(1)} %copy-done, f32[2,8,128]{2,1,0:T(8,128)S(1)} %copy-done.3, ...), custom_call_target="tpu_custom_call" | custom-call | tf_op jit(solution)/shard_map/local/pallas_call | solution.py:551
  14.7 1.8 %collective-permute-start.7 = (f32[8,4,8,128]{3,2,1,0:T(8,128)S(1)}, f32[8,4,8,128]{3,2,1,0:T(8,128)S(1)}, u32[]{:S(2)}, u32[]{:S(2)}) collective-permute-start(f32[8,4,8,128]{3,2,1,0:T(8,128)S(1)} %get-tuple-element.30), channel_id=1, source_target_pairs={{0,16},{16,0},{1,17},{17,1},{2,18},{18,2},{3,19},{19,3},{4,20},{20... | collective-permute-start | bytes 393224 | tf_op jit(solution)/shard_map/ppermute | solution.py:558
  16.5 0.6 %collective-permute-done.4.cross_ref = f32[17,8,128]{2,1,0:T(8,128)S(1)} collective-permute-done((f32[17,8,128]{2,1,0:T(8,128)S(1)}, f32[17,8,128]{2,1,0:T(8,128)S(1)}, u32[]{:S(2)}, u32[]{:S(2)}) %collective-permute-start.4) | collective-permute-done | bytes 69664 | tf_op jit(solution)/shard_map/ppermute | solution.py:520
  17.1 0.6 %collective-permute-done.3.two_ref = f32[17,8,128]{2,1,0:T(8,128)S(1)} collective-permute-done((f32[17,8,128]{2,1,0:T(8,128)S(1)}, f32[17,8,128]{2,1,0:T(8,128)S(1)}, u32[]{:S(2)}, u32[]{:S(2)}) %collective-permute-start.3) | collective-permute-done | bytes 69664 | tf_op jit(solution)/shard_map/ppermute | solution.py:520
  17.6 0.1 join1.1
  17.8 2.7 %collective-permute-start.5 = (f32[9,8,128]{2,1,0:T(8,128)S(1)}, f32[9,8,128]{2,1,0:T(8,128)S(1)}, u32[]{:S(2)}, u32[]{:S(2)}) collective-permute-start(f32[9,8,128]{2,1,0:T(8,128)S(1)} %edge.1.refs_4_), channel_id=1, source_target_pairs={{0,8},{1,9},{2,10},{3,11},{4,12},{5,13},{6,14},{7,15},{8,0},{9,1},... | collective-permute-start | bytes 110600 | tf_op jit(solution)/shard_map/ppermute | solution.py:520
  20.4 2.3 %collective-permute-done.5.refs_5_ = f32[9,8,128]{2,1,0:T(8,128)S(1)} collective-permute-done((f32[9,8,128]{2,1,0:T(8,128)S(1)}, f32[9,8,128]{2,1,0:T(8,128)S(1)}, u32[]{:S(2)}, u32[]{:S(2)}) %collective-permute-start.5) | collective-permute-done | bytes 36896 | tf_op jit(solution)/shard_map/ppermute | solution.py:520
  22.7 0.1 entering.1.entering_ref.refs_0_
  22.8 1.6 %collective-permute-start.6 = (f32[17,8,128]{2,1,0:T(8,128)S(1)}, f32[17,8,128]{2,1,0:T(8,128)S(1)}, u32[]{:S(2)}, u32[]{:S(2)}) collective-permute-start(f32[17,8,128]{2,1,0:T(8,128)S(1)} %entering.1.entering_ref.refs_0_), channel_id=1, source_target_pairs={{0,16},{16,0},{1,17},{17,1},{2,18},{18,2},{3,19},{19,3},{4,20},{20... | collective-permute-start | bytes 208904 | tf_op jit(solution)/shard_map/ppermute | solution.py:575
  25.0 0.0 copy-start.2
  25.0 0.3 %own.1.refs_2_ = f32[8,4,8,128]{3,2,1,0:T(8,128)S(1)} custom-call(f32[17,8,128]{2,1,0:T(8,128)S(1)} %entering.1.entering_ref.refs_0_, f32[8,8,128]{2,1,0:T(8,128)S(1)} %get-tuple-element.22.refs_4_.decay_ref.refs_6_, f32[8,8,128]{2,1,0:T(8,128)S(1)} %get-tuple-element.23.refs_5_.scale_ref.refs_7_, bf16[2,256,256]{2,1,0:T(8,128)(2,1)S(1)} %copy-done, ...), custom_call_target="tpu_custom_call" | custom-call | tf_op jit(solution)/shard_map/own/pallas_call | solution.py:576
  25.3 1.8 %collective-permute-done.6.refs_1_ = f32[17,8,128]{2,1,0:T(8,128)S(1)} collective-permute-done((f32[17,8,128]{2,1,0:T(8,128)S(1)}, f32[17,8,128]{2,1,0:T(8,128)S(1)}, u32[]{:S(2)}, u32[]{:S(2)}) %collective-permute-start.6) | collective-permute-done | bytes 69664 | tf_op jit(solution)/shard_map/ppermute | solution.py:575
  27.2 0.0 collective-permute-done.7.refs_3_
  27.2 0.0 copy-done.2
  27.2 1.3 %finish.1 = (f32[8,2,8,512]{3,2,1,0:T(8,128)}, f32[8,2,8,512]{3,2,1,0:T(8,128)}, f32[1,1]{1,0:T(1,128)}) custom-call(f32[17,8,128]{2,1,0:T(8,128)S(1)} %entering.1.entering_ref.refs_0_, f32[17,8,128]{2,1,0:T(8,128)S(1)} %collective-permute-done.6.refs_1_, f32[8,4,8,128]{3,2,1,0:T(8,128)S(1)} %own.1.refs_2_, ...), custom_call_target="tpu_custom_call" | custom-call | tf_op jit(solution)/shard_map/finish/pallas_call | solution.py:584
  (2 shorter events, 0.1 us)
Async XLA Ops:
  0.6 7.6 %copy-start.1 = (bf16[2,256,256]{2,1,0:T(8,128)(2,1)S(1)}, bf16[2,256,256]{2,1,0:T(8,128)(2,1)}, u32[]{:S(2)}) copy-start(bf16[2,256,256]{2,1,0:T(8,128)(2,1)} %constant.9.clone.refs_2_) | copy-start | bytes 786436
  0.6 4.1 %copy-start.4 = (f32[8,128]{1,0:T(8,128)S(1)}, f32[8,128]{1,0:T(8,128)}, u32[]{:S(2)}) copy-start(f32[8,128]{1,0:T(8,128)} %constant.8.clone.y_eigen_ref) | copy-start | bytes 12292
  1.7 6.5 %copy-start.3 = (f32[2,8,128]{2,1,0:T(8,128)S(1)}, f32[2,8,128]{2,1,0:T(8,128)}, u32[]{:S(2)}) copy-start(f32[2,8,128]{2,1,0:T(8,128)} %constant.10.clone.refs_3_.twiddle_ref.refs_9_) | copy-start | bytes 24580
  1.7 6.5 %collective-permute-start = (f32[2,4,4,8,128]{4,3,2,1,0:T(8,128)S(1)}, f32[2,4,4,8,128]{4,3,2,1,0:T(8,128)S(1)}, u32[]{:S(2)}, u32[]{:S(2)}) collective-permute-start(f32[2,4,4,8,128]{4,3,2,1,0:T(8,128)S(1)} %get-tuple-element.21), channel_id=1, source_target_pairs={{0,16},{16,0},{1,17},{17,1},{2,18},{18,2},{3,19},{19,3},{4,20},{20... | collective-permute-start | bytes 393224 | tf_op jit(solution)/shard_map/ppermute | solution.py:498
  8.6 5.8 %copy-start = (bf16[2,256,256]{2,1,0:T(8,128)(2,1)S(1)}, bf16[2,256,256]{2,1,0:T(8,128)(2,1)}, u32[]{:S(2)}) copy-start(bf16[2,256,256]{2,1,0:T(8,128)(2,1)} %constant.11.clone.lane_ref.refs_8_) | copy-start | bytes 786436
  8.6 1.3 %collective-permute-start.1 = (f32[17,8,128]{2,1,0:T(8,128)S(1)}, f32[17,8,128]{2,1,0:T(8,128)S(1)}, u32[]{:S(2)}, u32[]{:S(2)}) collective-permute-start(f32[17,8,128]{2,1,0:T(8,128)S(1)} %get-tuple-element.24.own_ref), channel_id=1, source_target_pairs={{0,1},{1,0},{2,3},{3,2},{4,5},{5,4},{6,7},{7,6},{8,9},{9,8},{10,11... | collective-permute-start | bytes 208904 | tf_op jit(solution)/shard_map/ppermute | solution.py:520
  10.0 4.4 %collective-permute-start.2 = (f32[17,8,128]{2,1,0:T(8,128)S(1)}, f32[17,8,128]{2,1,0:T(8,128)S(1)}, u32[]{:S(2)}, u32[]{:S(2)}) collective-permute-start(f32[17,8,128]{2,1,0:T(8,128)S(1)} %join0.1.own_ref), channel_id=1, source_target_pairs={{0,2},{1,5},{2,0},{3,7},{4,6},{5,1},{6,4},{7,3},{8,10},{9,13},{10,... | collective-permute-start | bytes 208904 | tf_op jit(solution)/shard_map/ppermute | solution.py:520
  11.8 5.3 %collective-permute-start.4 = (f32[17,8,128]{2,1,0:T(8,128)S(1)}, f32[17,8,128]{2,1,0:T(8,128)S(1)}, u32[]{:S(2)}, u32[]{:S(2)}) collective-permute-start(f32[17,8,128]{2,1,0:T(8,128)S(1)} %join0.1.own_ref), channel_id=1, source_target_pairs={{0,6},{1,7},{2,4},{3,5},{4,2},{5,3},{6,0},{7,1},{8,14},{9,15},{10,... | collective-permute-start | bytes 208904 | tf_op jit(solution)/shard_map/ppermute | solution.py:520
  13.3 4.3 %collective-permute-start.3 = (f32[17,8,128]{2,1,0:T(8,128)S(1)}, f32[17,8,128]{2,1,0:T(8,128)S(1)}, u32[]{:S(2)}, u32[]{:S(2)}) collective-permute-start(f32[17,8,128]{2,1,0:T(8,128)S(1)} %join0.1.own_ref), channel_id=1, source_target_pairs={{0,4},{1,3},{2,6},{3,1},{4,0},{5,7},{6,2},{7,5},{8,12},{9,11},{10,... | collective-permute-start | bytes 208904 | tf_op jit(solution)/shard_map/ppermute | solution.py:520
  14.7 12.5 %collective-permute-start.7 = (f32[8,4,8,128]{3,2,1,0:T(8,128)S(1)}, f32[8,4,8,128]{3,2,1,0:T(8,128)S(1)}, u32[]{:S(2)}, u32[]{:S(2)}) collective-permute-start(f32[8,4,8,128]{3,2,1,0:T(8,128)S(1)} %get-tuple-element.30), channel_id=1, source_target_pairs={{0,16},{16,0},{1,17},{17,1},{2,18},{18,2},{3,19},{19,3},{4,20},{20... | collective-permute-start | bytes 393224 | tf_op jit(solution)/shard_map/ppermute | solution.py:558
  17.8 4.9 %collective-permute-start.5 = (f32[9,8,128]{2,1,0:T(8,128)S(1)}, f32[9,8,128]{2,1,0:T(8,128)S(1)}, u32[]{:S(2)}, u32[]{:S(2)}) collective-permute-start(f32[9,8,128]{2,1,0:T(8,128)S(1)} %edge.1.refs_4_), channel_id=1, source_target_pairs={{0,8},{1,9},{2,10},{3,11},{4,12},{5,13},{6,14},{7,15},{8,0},{9,1},... | collective-permute-start | bytes 110600 | tf_op jit(solution)/shard_map/ppermute | solution.py:520
  22.8 4.4 %collective-permute-start.6 = (f32[17,8,128]{2,1,0:T(8,128)S(1)}, f32[17,8,128]{2,1,0:T(8,128)S(1)}, u32[]{:S(2)}, u32[]{:S(2)}) collective-permute-start(f32[17,8,128]{2,1,0:T(8,128)S(1)} %entering.1.entering_ref.refs_0_), channel_id=1, source_target_pairs={{0,16},{16,0},{1,17},{17,1},{2,18},{18,2},{3,19},{19,3},{4,20},{20... | collective-permute-start | bytes 208904 | tf_op jit(solution)/shard_map/ppermute | solution.py:575
  25.0 2.2 %copy-start.2 = (f32[8,2,8,512]{3,2,1,0:T(8,128)S(1)}, f32[8,2,8,512]{3,2,1,0:T(8,128)}, u32[]{:S(2)}) copy-start(f32[8,2,8,512]{3,2,1,0:T(8,128)} %refs_11_.1) | copy-start | bytes 786436

commit v4 on v3

--- a/solution.py
+++ b/solution.py
@@ -295,19 +295,13 @@
         out_ref[i] = value
 
 
-def join_two_kernel(
-    level, cells, groups, own_ref, one_ref, two_ref, cross_ref, decay_ref, scale_ref, out_ref, near_ref, pair_ref
-):
+def join_two_kernel(level, cells, groups, own_ref, near_ref, far_ref, cross_ref, decay_ref, scale_ref, out_ref, pair_ref):
     decay, scale = decay_ref[...], scale_ref[...]
-    odd = lax.rem(lax.axis_index("gz"), 2) == 1
-    near = [jnp.where(odd, b, a) for a, b in zip(rows_of(one_ref), rows_of(two_ref))]
-    far = [jnp.where(odd, a, b) for a, b in zip(rows_of(one_ref), rows_of(two_ref))]
-    own = join(level, cells, groups, rows_of(own_ref), near, decay, scale)
-    other = join(level, cells, groups, far, rows_of(cross_ref), decay, scale)
+    own = join(level, cells, groups, rows_of(own_ref), rows_of(near_ref), decay, scale)
+    other = join(level, cells, groups, rows_of(far_ref), rows_of(cross_ref), decay, scale)
     joined = join(level + 1, cells, groups, own, other, decay, scale)
     for i in range(len(joined)):
         out_ref[i] = joined[i]
-        near_ref[i] = near[i]
         pair_ref[i] = other[i]
 
 
@@ -341,7 +335,7 @@
     return small_dft(turned_re, turned_im, 1.0)
 
 
-def local_kernel(groups, local_ref, scale_ref, lane_ref, twiddle_ref, after_ref, *out_refs):
+def local_kernel(groups, local_ref, scale_ref, lane_ref, twiddle_ref, *out_refs):
     radix = scale_ref.shape[0]
     rows = radix // groups
     fields = [[scale_ref[a] * local_ref[part, a] for a in range(radix)] for part in range(2)]
@@ -354,8 +348,8 @@
 
 def entering_kernel(groups, slabs, cells, *refs):
     levels = slabs.bit_length() - 1
-    own_ref, received = refs[0], refs[1:levels]
-    edge_ref, other_ref, decay_ref, scale_ref, out_ref = refs[levels:]
+    own_ref, first_ref, received = refs[0], refs[1], refs[2 : levels + 1]
+    edge_ref, other_ref, decay_ref, scale_ref, out_ref, mate_ref = refs[levels + 1 :]
     radix = decay_ref.shape[0]
     kept = SUBS // groups
     subs = sub_ids((SUBS, LANES))
@@ -375,10 +369,10 @@
         edge_turned, other_turned = turn(edge, HALF), turn(other, HALF)
         for part in range(2):
             i = part * radix + a
-            weight, incoming = jnp.ones_like(d), jnp.zeros_like(d)
-            for level in range(levels - 1):
-                incoming = incoming + jnp.where(outers[level], 0.0, weight * received[level][i])
-                weight = weight * jnp.where(outers[level], 1.0, spans[level])
+            sides = [
+                (jnp.where(outers[0], 0.0, received[0][i]), jnp.where(outers[0], 1.0, spans[0])),
+                (jnp.where(outers[0], first_ref[i], 0.0), jnp.where(outers[0], spans[0], 1.0)),
+            ]
             mine = jnp.where(low, edge, edge_turned) if part == 0 else jnp.where(low, edge_turned, edge)
             theirs = jnp.where(low, other, other_turned) if part == 0 else jnp.where(low, other_turned, other)
             entering = rest * (theirs - far * mine)
@@ -386,8 +380,14 @@
             here, there = mine * entering, theirs * leaving
             couple = couple + (scale_ref[a] * d) * (jnp.where(right, there, here) + jnp.where(right, here, there))
             wall = d * turn(own_ref[i], HALF) + image * entering
-            out_ref[i] = incoming + weight * jnp.where(outers[levels - 1], -wall, entering)
-    out_ref[2 * radix] = edge_ref[radix] + other_ref[radix] + jnp.where(subs < kept, couple, 0.0)
+            for ref, (incoming, weight) in zip((out_ref, mate_ref), sides):
+                for level in range(1, levels - 1):
+                    incoming = incoming + jnp.where(outers[level], 0.0, weight * received[level][i])
+                    weight = weight * jnp.where(outers[level], 1.0, spans[level])
+                ref[i] = incoming + weight * jnp.where(outers[levels - 1], -wall, entering)
+    energy = edge_ref[radix] + other_ref[radix] + jnp.where(subs < kept, couple, 0.0)
+    out_ref[2 * radix] = energy
+    mate_ref[2 * radix] = energy
 
 
 def response(groups, inner, entering_ref, decay_ref, scale_ref, lane_ref, twiddle_ref):
@@ -516,45 +516,42 @@
         name="forward",
     )(*map(inside, (*held, lane_transform(-1.0), twiddles(radix), decay, scale)))
 
-    def swapped(value, even, odd):
-        return lax.ppermute(value, "gz", [(i, i ^ (odd if i & 1 else even)) for i in range(slabs)])
-
-    received, level, after = [], 0, None
+    def swapped(value, bits):
+        return lax.ppermute(value, "gz", [(i, i ^ bits) for i in range(slabs)])
+
+    first, received, level = message, [], 0
     while level < levels - 1:
-        one_bit, next_bit = 1 << level, 2 << level
+        bit, cross = 1 << level, min(level, 1)
+        near = swapped(message, bit | cross)
+        received.append(near)
         if level == 0 or level == levels - 2:
-            received.append(swapped(message, one_bit, one_bit))
             message = pl.pallas_call(
                 functools.partial(join_kernel, level, cells, groups),
                 out_shape=held_array(*message.shape),
                 in_specs=[VMEM] * 4,
                 out_specs=VMEM,
                 name=f"join{level}",
-            )(*map(inside, (message, received[-1], decay, scale)))
+            )(*map(inside, (message, near, decay, scale)))
             level += 1
         else:
-            one = swapped(message, one_bit, next_bit)
-            after = one if after is None else after
-            two = swapped(message, next_bit, one_bit)
-            cross = swapped(message, one_bit | next_bit, one_bit | next_bit)
-            message, near, pair = pl.pallas_call(
+            message, pair = pl.pallas_call(
                 functools.partial(join_two_kernel, level, cells, groups),
-                out_shape=[held_array(*message.shape)] * 3,
+                out_shape=[held_array(*message.shape)] * 2,
                 in_specs=[VMEM] * 6,
-                out_specs=[VMEM] * 3,
+                out_specs=[VMEM] * 2,
                 name=f"join{level}",
-            )(*map(inside, (message, one, two, cross, decay, scale)))
-            received += [near, pair]
+            )(*map(inside, (message, near, swapped(message, 2 * bit | 1), swapped(message, 3 * bit | 1), decay, scale)))
+            received.append(pair)
             level += 2
     tables = (lane_transform(1.0), twiddles(radix))
     piece = held_array(parts * rows, inner, SUBS, LANES)
     pieces = pl.pallas_call(
         functools.partial(local_kernel, groups),
         out_shape=[piece] * groups,
-        in_specs=[VMEM] * 5,
+        in_specs=[VMEM] * 4,
         out_specs=[VMEM] * groups,
         name="local",
-    )(*map(inside, (local, scale, *tables, received[0] if after is None else after)))
+    )(*map(inside, (local, scale, *tables)))
     held = [lax.ppermute(x, "gy", d) for x, d in zip(pieces[1:], distances)]
 
     edge = pl.pallas_call(
@@ -564,15 +561,16 @@
         out_specs=VMEM,
         name="edge",
     )(*map(inside, (message, decay, scale)))
-    other = swapped(edge, 1 << level, 1 << level)
-    entering = pl.pallas_call(
+    other = swapped(edge, 1 << level | 1)
+    entering, mate = pl.pallas_call(
         functools.partial(entering_kernel, groups, slabs, cells),
-        out_shape=held_array(*message.shape),
-        in_specs=[VMEM] * (levels + 4),
-        out_specs=VMEM,
+        out_shape=[held_array(*message.shape)] * 2,
+        in_specs=[VMEM] * (levels + 5),
+        out_specs=[VMEM] * 2,
         name="entering",
-    )(*map(inside, (message, *received, edge, other, decay, scale)))
-    entered = [entering] + [lax.ppermute(entering, "gy", d) for d in distances]
+    )(*map(inside, (message, first, *received, edge, other, decay, scale)))
+    crossed = [[(i * slabs + z, j * slabs + (z ^ 1)) for i, j in d for z in range(slabs)] for d in distances]
+    entered = [entering] + [lax.ppermute(mate, ("gy", "gz"), d) for d in crossed]
     own = pl.pallas_call(
         functools.partial(own_kernel, groups),
         out_shape=piece,

time: 28.6 us -> 27.3 us (0.955)
  waiting for transfers between devices: 10.1 us -> 9.01 us
  starting transfers between devices: 12.6 us -> 12.2 us
    ppermute x6, waiting for transfers between devices: 7.32 us -> 6.25 us  [the longest x5 4.87 us: swapped(): return lax.ppermute(value, 'gz', [(i, i ^ bits) for i in range(slabs)])]
  transfers between devices with their start and end apart: 8 -> 8, of which waited for: 7 -> 6; matrix products, arithmetic and copies ran while one was open for 0% -> 0% of each run, Pallas kernels for 6% -> 6%
where the time goes in v4:
time: 27.3 us; the launch traced here: 27 us
  starting transfers between devices  12.2 us (45%)
  waiting for transfers between devices  9.01 us (33%)
  Pallas kernels  4.33 us (16%)
  between operations  1.4 us (5%)
    ppermute x5, starting transfers between devices, swapped(): return lax.ppermute(value, 'gz', [(i, i ^ bits) for i in range(slabs)])  5.99 us
    ppermute x5, waiting for transfers between devices, swapped(): return lax.ppermute(value, 'gz', [(i, i ^ bits) for i in range(slabs)])  4.87 us
    ppermute x1, starting transfers between devices, on_device(): lax.ppermute(x, 'gy', d)  3 us
    ppermute x1, waiting for transfers between devices, on_device(): lax.ppermute(x, 'gy', d)  2.76 us
    ppermute x1, starting transfers between devices, on_device(): held = [lax.ppermute(x, 'gy', d) for x, d in zip(pieces[1:], distances)]  1.63 us
    ppermute x1, starting transfers between devices, on_device(): lax.ppermute(mate, ('gy', 'gz'), d)  1.61 us
    ppermute x1, waiting for transfers between devices, on_device(): lax.ppermute(mate, ('gy', 'gz'), d)  1.37 us
    pallas_call x1, Pallas kernels, on_device(): pl.pallas_call(functools.partial(finish_kernel, groups), out_shape=[float...  1.28 us
  transfers between devices with their start and end apart: 8, of which 6 were waited for; matrix products, arithmetic and copies ran while one was open for 0% of the time, Pallas kernels for 6%

profile of v4, /device:TPU:0, one launch (start us, length us, event | category | flops | bytes accessed | tf_op | source)
XLA Modules:
  0.0 27.0 jit_solution(8393365465339342788)
XLA Ops:
  0.6 0.0 copy-start.1
  0.6 0.0 copy-start.4
  0.7 1.0 %pack.1 = (f32[8,512]{1,0:T(8,128)S(1)}, f32[2,4,4,8,128]{4,3,2,1,0:T(8,128)S(1)}, f32[2,4,4,8,128]{4,3,2,1,0:T(8,128)S(1)}) custom-call(f32[8,2,8,512]{3,2,1,0:T(8,128)} %residual_any.1, s32[8,512]{1,0:T(8,128)} %labels_any.1, f32[3]{0:T(128)} %diffusivity_any.1), custom_call_target="tpu_custom_call" | custom-call | tf_op jit(solution)/shard_map/pack/pallas_call | solution.py:483
  1.7 0.0 copy-start.3
  1.7 3.0 %collective-permute-start = (f32[2,4,4,8,128]{4,3,2,1,0:T(8,128)S(1)}, f32[2,4,4,8,128]{4,3,2,1,0:T(8,128)S(1)}, u32[]{:S(2)}, u32[]{:S(2)}) collective-permute-start(f32[2,4,4,8,128]{4,3,2,1,0:T(8,128)S(1)} %get-tuple-element.22), channel_id=1, source_target_pairs={{0,16},{16,0},{1,17},{17,1},{2,18},{18,2},{3,19},{19,3},{4,20},{20... | collective-permute-start | bytes 393224 | tf_op jit(solution)/shard_map/ppermute | solution.py:498
  4.7 0.0 copy-done.4
  4.7 0.7 %roots.1 = (f32[8,8,128]{2,1,0:T(8,128)S(1)}, f32[8,8,128]{2,1,0:T(8,128)S(1)}, f32[8,8,128]{2,1,0:T(8,128)S(1)}, f32[8,8,128]{2,1,0:T(8,128)S(1)}) custom-call(f32[8,128]{1,0:T(8,128)S(1)} %copy-done.4, f32[8]{0:T(128)} %eigen_ref.1), custom_call_target="tpu_custom_call" | custom-call | tf_op jit(solution)/shard_map/roots/pallas_call | solution.py:499
  5.5 2.8 %collective-permute-done.refs_1_ = f32[2,4,4,8,128]{4,3,2,1,0:T(8,128)S(1)} collective-permute-done((f32[2,4,4,8,128]{4,3,2,1,0:T(8,128)S(1)}, f32[2,4,4,8,128]{4,3,2,1,0:T(8,128)S(1)}, u32[]{:S(2)}, u32[]{:S(2)}) %collective-permute-start) | collective-permute-done | bytes 131104 | tf_op jit(solution)/shard_map/ppermute | solution.py:498
  8.2 0.0 copy-done.1
  8.2 0.0 copy-done.3
  8.2 0.4 %forward.1 = (f32[17,8,128]{2,1,0:T(8,128)S(1)}, f32[2,8,4,8,128]{4,3,2,1,0:T(8,128)S(1)}) custom-call(f32[2,4,4,8,128]{4,3,2,1,0:T(8,128)S(1)} %get-tuple-element.21.refs_0_, f32[2,4,4,8,128]{4,3,2,1,0:T(8,128)S(1)} %collective-permute-done.refs_1_, bf16[2,256,256]{2,1,0:T(8,128)(2,1)S(1)} %copy-done.1, f32[2,8,128]{2,1,0:T(8,128)S(1)} %copy-done.3, ...), custom_call_target="tpu_custom_call" | custom-call | tf_op jit(solution)/shard_map/forward/pallas_call | solution.py:508
  8.6 0.0 copy-start
  8.6 0.1 collective-permute-start.1
  8.7 1.2 %collective-permute-done.1.other_ref.refs_2_ = f32[17,8,128]{2,1,0:T(8,128)S(1)} collective-permute-done((f32[17,8,128]{2,1,0:T(8,128)S(1)}, f32[17,8,128]{2,1,0:T(8,128)S(1)}, u32[]{:S(2)}, u32[]{:S(2)}) %collective-permute-start.1) | collective-permute-done | bytes 69664 | tf_op jit(solution)/shard_map/ppermute | solution.py:520
  10.0 2.6 %collective-permute-start.4 = (f32[17,8,128]{2,1,0:T(8,128)S(1)}, f32[17,8,128]{2,1,0:T(8,128)S(1)}, u32[]{:S(2)}, u32[]{:S(2)}) collective-permute-start(f32[17,8,128]{2,1,0:T(8,128)S(1)} %join0.1.own_ref), channel_id=1, source_target_pairs={{0,7},{1,6},{2,5},{3,4},{4,3},{5,2},{6,1},{7,0},{8,15},{9,14},{10,... | collective-permute-start | bytes 208904 | tf_op jit(solution)/shard_map/ppermute | solution.py:520
  12.6 0.4 %collective-permute-start.3 = (f32[17,8,128]{2,1,0:T(8,128)S(1)}, f32[17,8,128]{2,1,0:T(8,128)S(1)}, u32[]{:S(2)}, u32[]{:S(2)}) collective-permute-start(f32[17,8,128]{2,1,0:T(8,128)S(1)} %join0.1.own_ref), channel_id=1, source_target_pairs={{0,5},{1,4},{2,7},{3,6},{4,1},{5,0},{6,3},{7,2},{8,13},{9,12},{10,... | collective-permute-start | bytes 208904 | tf_op jit(solution)/shard_map/ppermute | solution.py:520
  13.0 0.2 collective-permute-start.2
  13.2 0.0 copy-done
  13.2 0.3 %local.1 = (f32[8,4,8,128]{3,2,1,0:T(8,128)S(1)}, f32[8,4,8,128]{3,2,1,0:T(8,128)S(1)}) custom-call(f32[2,8,4,8,128]{4,3,2,1,0:T(8,128)S(1)} %get-tuple-element.30.local_ref, f32[8,8,128]{2,1,0:T(8,128)S(1)} %get-tuple-element.24.refs_5_.scale_ref.refs_8_, bf16[2,256,256]{2,1,0:T(8,128)(2,1)S(1)} %copy-done, f32[2,8,128]{2,1,0:T(8,128)S(1)} %copy-done.3), custom_call_target="tpu_custom_call" | custom-call | tf_op jit(solution)/shard_map/local/pallas_call | solution.py:548
  13.5 1.6 %collective-permute-start.7 = (f32[8,4,8,128]{3,2,1,0:T(8,128)S(1)}, f32[8,4,8,128]{3,2,1,0:T(8,128)S(1)}, u32[]{:S(2)}, u32[]{:S(2)}) collective-permute-start(f32[8,4,8,128]{3,2,1,0:T(8,128)S(1)} %get-tuple-element.32), channel_id=1, source_target_pairs={{0,16},{16,0},{1,17},{17,1},{2,18},{18,2},{3,19},{19,3},{4,20},{20... | collective-permute-start | bytes 393224 | tf_op jit(solution)/shard_map/ppermute | solution.py:555
  15.2 0.0 collective-permute-done.4.cross_ref
  15.2 1.7 %collective-permute-done.3.far_ref = f32[17,8,128]{2,1,0:T(8,128)S(1)} collective-permute-done((f32[17,8,128]{2,1,0:T(8,128)S(1)}, f32[17,8,128]{2,1,0:T(8,128)S(1)}, u32[]{:S(2)}, u32[]{:S(2)}) %collective-permute-start.3) | collective-permute-done | bytes 69664 | tf_op jit(solution)/shard_map/ppermute | solution.py:520
  16.9 0.2 collective-permute-done.2.near_ref.refs_3_
  17.1 0.1 join1.1
  17.3 2.7 %collective-permute-start.5 = (f32[9,8,128]{2,1,0:T(8,128)S(1)}, f32[9,8,128]{2,1,0:T(8,128)S(1)}, u32[]{:S(2)}, u32[]{:S(2)}) collective-permute-start(f32[9,8,128]{2,1,0:T(8,128)S(1)} %edge.1.refs_5_), channel_id=1, source_target_pairs={{0,9},{1,8},{2,11},{3,10},{4,13},{5,12},{6,15},{7,14},{8,1},{9,0},... | collective-permute-start | bytes 110600 | tf_op jit(solution)/shard_map/ppermute | solution.py:520
  20.0 1.6 %collective-permute-done.5.refs_6_ = f32[9,8,128]{2,1,0:T(8,128)S(1)} collective-permute-done((f32[9,8,128]{2,1,0:T(8,128)S(1)}, f32[9,8,128]{2,1,0:T(8,128)S(1)}, u32[]{:S(2)}, u32[]{:S(2)}) %collective-permute-start.5) | collective-permute-done | bytes 36896 | tf_op jit(solution)/shard_map/ppermute | solution.py:520
  21.6 0.1 entering.1
  21.7 1.6 %collective-permute-start.6 = (f32[17,8,128]{2,1,0:T(8,128)S(1)}, f32[17,8,128]{2,1,0:T(8,128)S(1)}, u32[]{:S(2)}, u32[]{:S(2)}) collective-permute-start(f32[17,8,128]{2,1,0:T(8,128)S(1)} %get-tuple-element.29), channel_id=1, source_target_pairs={{0,17},{1,16},{2,19},{3,18},{4,21},{5,20},{6,23},{7,22},{8,25},{9,... | collective-permute-start | bytes 208904 | tf_op jit(solution)/shard_map/ppermute | solution.py:573
  24.0 0.0 copy-start.2
  24.0 0.3 %own.1.refs_2_ = f32[8,4,8,128]{3,2,1,0:T(8,128)S(1)} custom-call(f32[17,8,128]{2,1,0:T(8,128)S(1)} %get-tuple-element.28.entering_ref.refs_0_, f32[8,8,128]{2,1,0:T(8,128)S(1)} %get-tuple-element.23.refs_4_.decay_ref.refs_7_, f32[8,8,128]{2,1,0:T(8,128)S(1)} %get-tuple-element.24.refs_5_.scale_ref.refs_8_, bf16[2,256,256]{2,1,0:T(8,128)(2,1)S(1)} %copy-done, ...), custom_call_target="tpu_custom_call" | custom-call | tf_op jit(solution)/shard_map/own/pallas_call | solution.py:574
  24.3 0.0 collective-permute-done.7.refs_3_
  24.3 1.4 %collective-permute-done.6.refs_1_ = f32[17,8,128]{2,1,0:T(8,128)S(1)} collective-permute-done((f32[17,8,128]{2,1,0:T(8,128)S(1)}, f32[17,8,128]{2,1,0:T(8,128)S(1)}, u32[]{:S(2)}, u32[]{:S(2)}) %collective-permute-start.6) | collective-permute-done | bytes 69664 | tf_op jit(solution)/shard_map/ppermute | solution.py:573
  25.7 0.0 copy-done.2
  25.7 1.3 %finish.1 = (f32[8,2,8,512]{3,2,1,0:T(8,128)}, f32[8,2,8,512]{3,2,1,0:T(8,128)}, f32[1,1]{1,0:T(1,128)}) custom-call(f32[17,8,128]{2,1,0:T(8,128)S(1)} %get-tuple-element.28.entering_ref.refs_0_, f32[17,8,128]{2,1,0:T(8,128)S(1)} %collective-permute-done.6.refs_1_, f32[8,4,8,128]{3,2,1,0:T(8,128)S(1)} %own.1.refs_2_, ...), custom_call_target="tpu_custom_call" | custom-call | tf_op jit(solution)/shard_map/finish/pallas_call | solution.py:582
  (2 shorter events, 0.1 us)
Async XLA Ops:
  0.6 7.6 %copy-start.1 = (bf16[2,256,256]{2,1,0:T(8,128)(2,1)S(1)}, bf16[2,256,256]{2,1,0:T(8,128)(2,1)}, u32[]{:S(2)}) copy-start(bf16[2,256,256]{2,1,0:T(8,128)(2,1)} %constant.9.clone.refs_2_) | copy-start | bytes 786436
  0.6 4.1 %copy-start.4 = (f32[8,128]{1,0:T(8,128)S(1)}, f32[8,128]{1,0:T(8,128)}, u32[]{:S(2)}) copy-start(f32[8,128]{1,0:T(8,128)} %constant.8.clone.y_eigen_ref) | copy-start | bytes 12292
  1.7 6.5 %copy-start.3 = (f32[2,8,128]{2,1,0:T(8,128)S(1)}, f32[2,8,128]{2,1,0:T(8,128)}, u32[]{:S(2)}) copy-start(f32[2,8,128]{2,1,0:T(8,128)} %constant.10.clone.refs_3_.twiddle_ref.refs_9_) | copy-start | bytes 24580
  1.7 6.5 %collective-permute-start = (f32[2,4,4,8,128]{4,3,2,1,0:T(8,128)S(1)}, f32[2,4,4,8,128]{4,3,2,1,0:T(8,128)S(1)}, u32[]{:S(2)}, u32[]{:S(2)}) collective-permute-start(f32[2,4,4,8,128]{4,3,2,1,0:T(8,128)S(1)} %get-tuple-element.22), channel_id=1, source_target_pairs={{0,16},{16,0},{1,17},{17,1},{2,18},{18,2},{3,19},{19,3},{4,20},{20... | collective-permute-start | bytes 393224 | tf_op jit(solution)/shard_map/ppermute | solution.py:498
  8.6 4.6 %copy-start = (bf16[2,256,256]{2,1,0:T(8,128)(2,1)S(1)}, bf16[2,256,256]{2,1,0:T(8,128)(2,1)}, u32[]{:S(2)}) copy-start(bf16[2,256,256]{2,1,0:T(8,128)(2,1)} %constant.11.clone.lane_ref.refs_8_) | copy-start | bytes 786436
  8.6 1.3 %collective-permute-start.1 = (f32[17,8,128]{2,1,0:T(8,128)S(1)}, f32[17,8,128]{2,1,0:T(8,128)S(1)}, u32[]{:S(2)}, u32[]{:S(2)}) collective-permute-start(f32[17,8,128]{2,1,0:T(8,128)S(1)} %get-tuple-element.25.own_ref.refs_1_), channel_id=1, source_target_pairs={{0,1},{1,0},{2,3},{3,2},{4,5},{5,4},{6,7},{7,6},{8,9},{9,8},{10,11... | collective-permute-start | bytes 208904 | tf_op jit(solution)/shard_map/ppermute | solution.py:520
  10.0 5.2 %collective-permute-start.4 = (f32[17,8,128]{2,1,0:T(8,128)S(1)}, f32[17,8,128]{2,1,0:T(8,128)S(1)}, u32[]{:S(2)}, u32[]{:S(2)}) collective-permute-start(f32[17,8,128]{2,1,0:T(8,128)S(1)} %join0.1.own_ref), channel_id=1, source_target_pairs={{0,7},{1,6},{2,5},{3,4},{4,3},{5,2},{6,1},{7,0},{8,15},{9,14},{10,... | collective-permute-start | bytes 208904 | tf_op jit(solution)/shard_map/ppermute | solution.py:520
  12.6 4.3 %collective-permute-start.3 = (f32[17,8,128]{2,1,0:T(8,128)S(1)}, f32[17,8,128]{2,1,0:T(8,128)S(1)}, u32[]{:S(2)}, u32[]{:S(2)}) collective-permute-start(f32[17,8,128]{2,1,0:T(8,128)S(1)} %join0.1.own_ref), channel_id=1, source_target_pairs={{0,5},{1,4},{2,7},{3,6},{4,1},{5,0},{6,3},{7,2},{8,13},{9,12},{10,... | collective-permute-start | bytes 208904 | tf_op jit(solution)/shard_map/ppermute | solution.py:520
  13.0 4.1 %collective-permute-start.2 = (f32[17,8,128]{2,1,0:T(8,128)S(1)}, f32[17,8,128]{2,1,0:T(8,128)S(1)}, u32[]{:S(2)}, u32[]{:S(2)}) collective-permute-start(f32[17,8,128]{2,1,0:T(8,128)S(1)} %join0.1.own_ref), channel_id=1, source_target_pairs={{0,3},{1,2},{2,1},{3,0},{4,7},{5,6},{6,5},{7,4},{8,11},{9,10},{10,... | collective-permute-start | bytes 208904 | tf_op jit(solution)/shard_map/ppermute | solution.py:520
  13.5 10.8 %collective-permute-start.7 = (f32[8,4,8,128]{3,2,1,0:T(8,128)S(1)}, f32[8,4,8,128]{3,2,1,0:T(8,128)S(1)}, u32[]{:S(2)}, u32[]{:S(2)}) collective-permute-start(f32[8,4,8,128]{3,2,1,0:T(8,128)S(1)} %get-tuple-element.32), channel_id=1, source_target_pairs={{0,16},{16,0},{1,17},{17,1},{2,18},{18,2},{3,19},{19,3},{4,20},{20... | collective-permute-start | bytes 393224 | tf_op jit(solution)/shard_map/ppermute | solution.py:555
  17.3 4.4 %collective-permute-start.5 = (f32[9,8,128]{2,1,0:T(8,128)S(1)}, f32[9,8,128]{2,1,0:T(8,128)S(1)}, u32[]{:S(2)}, u32[]{:S(2)}) collective-permute-start(f32[9,8,128]{2,1,0:T(8,128)S(1)} %edge.1.refs_5_), channel_id=1, source_target_pairs={{0,9},{1,8},{2,11},{3,10},{4,13},{5,12},{6,15},{7,14},{8,1},{9,0},... | collective-permute-start | bytes 110600 | tf_op jit(solution)/shard_map/ppermute | solution.py:520
  21.7 4.0 %collective-permute-start.6 = (f32[17,8,128]{2,1,0:T(8,128)S(1)}, f32[17,8,128]{2,1,0:T(8,128)S(1)}, u32[]{:S(2)}, u32[]{:S(2)}) collective-permute-start(f32[17,8,128]{2,1,0:T(8,128)S(1)} %get-tuple-element.29), channel_id=1, source_target_pairs={{0,17},{1,16},{2,19},{3,18},{4,21},{5,20},{6,23},{7,22},{8,25},{9,... | collective-permute-start | bytes 208904 | tf_op jit(solution)/shard_map/ppermute | solution.py:573
  24.0 1.7 %copy-start.2 = (f32[8,2,8,512]{3,2,1,0:T(8,128)S(1)}, f32[8,2,8,512]{3,2,1,0:T(8,128)}, u32[]{:S(2)}) copy-start(f32[8,2,8,512]{3,2,1,0:T(8,128)} %refs_11_.1) | copy-start | bytes 786436

commit v5 on v4

--- a/solution.py
+++ b/solution.py
@@ -289,13 +289,17 @@
     return [ref[i] for i in range(ref.shape[0])]
 
 
-def join_kernel(level, cells, groups, own_ref, other_ref, decay_ref, scale_ref, out_ref):
+def join_kernel(level, cells, groups, own_ref, other_ref, decay_ref, scale_ref, out_ref, *edge_refs):
     joined = join(level, cells, groups, rows_of(own_ref), rows_of(other_ref), decay_ref[...], scale_ref[...])
     for i, value in enumerate(joined):
         out_ref[i] = value
-
-
-def join_two_kernel(level, cells, groups, own_ref, near_ref, far_ref, cross_ref, decay_ref, scale_ref, out_ref, pair_ref):
+    for edge_ref in edge_refs:
+        edge_of(level + 1, cells, groups, joined, decay_ref, scale_ref, edge_ref)
+
+
+def join_two_kernel(
+    level, cells, groups, own_ref, near_ref, far_ref, cross_ref, decay_ref, scale_ref, out_ref, pair_ref, *edge_refs
+):
     decay, scale = decay_ref[...], scale_ref[...]
     own = join(level, cells, groups, rows_of(own_ref), rows_of(near_ref), decay, scale)
     other = join(level, cells, groups, rows_of(far_ref), rows_of(cross_ref), decay, scale)
@@ -303,9 +307,11 @@
     for i in range(len(joined)):
         out_ref[i] = joined[i]
         pair_ref[i] = other[i]
-
-
-def edge_kernel(level, cells, groups, own_ref, decay_ref, scale_ref, out_ref):
+    for edge_ref in edge_refs:
+        edge_of(level + 2, cells, groups, joined, decay_ref, scale_ref, edge_ref)
+
+
+def edge_of(level, cells, groups, moments, decay_ref, scale_ref, out_ref):
     radix = decay_ref.shape[0]
     kept = SUBS // groups
     subs = sub_ids((SUBS, LANES))
@@ -316,13 +322,13 @@
         image = power(d, (cells << level) + 1)
         both = []
         for part in range(2):
-            own = own_ref[part * radix + a]
+            own = moments[part * radix + a]
             near = jnp.where(outer, 0.0, own)
             walls = walls + (scale_ref[a] * d * d) * (near * near)
             sent = own - image * turn(own, HALF)
             both.append(jnp.where(outer, sent, turn(sent, HALF)))
         out_ref[a] = jnp.where(subs < HALF, both[0], both[1])
-    out_ref[radix] = own_ref[2 * radix] - jnp.where(lax.rem(subs, HALF) < kept, walls, 0.0)
+    out_ref[radix] = moments[2 * radix] - jnp.where(lax.rem(subs, HALF) < kept, walls, 0.0)
 
 
 def to_planes(re, im, lane_ref, twiddle_ref):
@@ -346,46 +352,60 @@
                 ref[part * rows + a] = value
 
 
-def entering_kernel(groups, slabs, cells, *refs):
+def both_parts(packed):
+    low = sub_ids((SUBS, LANES)) < HALF
+    turned = turn(packed, HALF)
+    return jnp.where(low, packed, turned), jnp.where(low, turned, packed)
+
+
+def near_side_kernel(slabs, cells, *refs):
     levels = slabs.bit_length() - 1
     own_ref, first_ref, received = refs[0], refs[1], refs[2 : levels + 1]
-    edge_ref, other_ref, decay_ref, scale_ref, out_ref, mate_ref = refs[levels + 1 :]
+    edge_ref, decay_ref, scale_ref, out_ref, mate_ref, factor_ref = refs[levels + 1 :]
     radix = decay_ref.shape[0]
-    kept = SUBS // groups
-    subs = sub_ids((SUBS, LANES))
-    low = subs < HALF
     outers = [facing(level)[0] for level in range(levels)]
-    right = facing(levels - 1)[1] == 1
-    couple = jnp.zeros((SUBS, LANES), jnp.float32)
     for a in range(radix):
         d = decay_ref[a]
         spans = [power(d, cells)]
         for level in range(1, levels + 1):
             spans.append(spans[-1] * spans[-1])
         far = spans[levels] * d
-        image = spans[levels - 1] * d
         rest = 1.0 / (1.0 - far * far)
-        edge, other = edge_ref[a], other_ref[a]
-        edge_turned, other_turned = turn(edge, HALF), turn(other, HALF)
+        facing_factor = jnp.where(outers[levels - 1], -spans[levels - 1] * d, 1.0) * rest
+        parts = both_parts(edge_ref[a])
         for part in range(2):
             i = part * radix + a
+            wall = jnp.where(outers[levels - 1], d * turn(own_ref[i], HALF), 0.0) + facing_factor * (far * parts[part])
             sides = [
                 (jnp.where(outers[0], 0.0, received[0][i]), jnp.where(outers[0], 1.0, spans[0])),
                 (jnp.where(outers[0], first_ref[i], 0.0), jnp.where(outers[0], spans[0], 1.0)),
             ]
-            mine = jnp.where(low, edge, edge_turned) if part == 0 else jnp.where(low, edge_turned, edge)
-            theirs = jnp.where(low, other, other_turned) if part == 0 else jnp.where(low, other_turned, other)
-            entering = rest * (theirs - far * mine)
-            leaving = rest * (mine - far * theirs)
-            here, there = mine * entering, theirs * leaving
-            couple = couple + (scale_ref[a] * d) * (jnp.where(right, there, here) + jnp.where(right, here, there))
-            wall = d * turn(own_ref[i], HALF) + image * entering
-            for ref, (incoming, weight) in zip((out_ref, mate_ref), sides):
+            for side, (ref, (incoming, weight)) in enumerate(zip((out_ref, mate_ref), sides)):
                 for level in range(1, levels - 1):
                     incoming = incoming + jnp.where(outers[level], 0.0, weight * received[level][i])
                     weight = weight * jnp.where(outers[level], 1.0, spans[level])
-                ref[i] = incoming + weight * jnp.where(outers[levels - 1], -wall, entering)
-    energy = edge_ref[radix] + other_ref[radix] + jnp.where(subs < kept, couple, 0.0)
+                ref[i] = incoming - weight * wall
+                factor_ref[side * radix + a] = weight * facing_factor
+        factor_ref[2 * radix + a] = scale_ref[a] * d * rest
+        factor_ref[3 * radix + a] = far
+    for ref in (out_ref, mate_ref):
+        ref[2 * radix] = edge_ref[radix]
+
+
+def entering_kernel(groups, slabs, edge_ref, other_ref, near_ref, near_mate_ref, factor_ref, out_ref, mate_ref):
+    radix = edge_ref.shape[0] - 1
+    right = facing(slabs.bit_length() - 2)[1] == 1
+    couple = jnp.zeros((SUBS, LANES), jnp.float32)
+    for a in range(radix):
+        for part, (mine, theirs) in enumerate(zip(both_parts(edge_ref[a]), both_parts(other_ref[a]))):
+            i = part * radix + a
+            out_ref[i] = near_ref[i] + factor_ref[a] * theirs
+            mate_ref[i] = near_mate_ref[i] + factor_ref[radix + a] * theirs
+            left_value, right_value = jnp.where(right, theirs, mine), jnp.where(right, mine, theirs)
+            squares = left_value * left_value + right_value * right_value
+            joined = 2.0 * (left_value * right_value) - factor_ref[3 * radix + a] * squares
+            couple = couple + factor_ref[2 * radix + a] * joined
+    energy = edge_ref[radix] + other_ref[radix] + jnp.where(sub_ids((SUBS, LANES)) < SUBS // groups, couple, 0.0)
     out_ref[2 * radix] = energy
     mate_ref[2 * radix] = energy
 
@@ -520,25 +540,28 @@
         return lax.ppermute(value, "gz", [(i, i ^ bits) for i in range(slabs)])
 
     first, received, level = message, [], 0
+    edge_shape = held_array(radix + 1, SUBS, LANES)
     while level < levels - 1:
         bit, cross = 1 << level, min(level, 1)
         near = swapped(message, bit | cross)
         received.append(near)
         if level == 0 or level == levels - 2:
-            message = pl.pallas_call(
+            last = [edge_shape] if level == levels - 2 else []
+            message, *edge = pl.pallas_call(
                 functools.partial(join_kernel, level, cells, groups),
-                out_shape=held_array(*message.shape),
+                out_shape=[held_array(*message.shape)] + last,
                 in_specs=[VMEM] * 4,
-                out_specs=VMEM,
+                out_specs=[VMEM] * (1 + len(last)),
                 name=f"join{level}",
             )(*map(inside, (message, near, decay, scale)))
             level += 1
         else:
-            message, pair = pl.pallas_call(
+            last = [edge_shape] if level == levels - 3 else []
+            message, pair, *edge = pl.pallas_call(
                 functools.partial(join_two_kernel, level, cells, groups),
-                out_shape=[held_array(*message.shape)] * 2,
+                out_shape=[held_array(*message.shape)] * 2 + last,
                 in_specs=[VMEM] * 6,
-                out_specs=[VMEM] * 2,
+                out_specs=[VMEM] * (2 + len(last)),
                 name=f"join{level}",
             )(*map(inside, (message, near, swapped(message, 2 * bit | 1), swapped(message, 3 * bit | 1), decay, scale)))
             received.append(pair)
@@ -554,21 +577,21 @@
     )(*map(inside, (local, scale, *tables)))
     held = [lax.ppermute(x, "gy", d) for x, d in zip(pieces[1:], distances)]
 
-    edge = pl.pallas_call(
-        functools.partial(edge_kernel, level, cells, groups),
-        out_shape=held_array(radix + 1, SUBS, LANES),
-        in_specs=[VMEM] * 3,
-        out_specs=VMEM,
-        name="edge",
-    )(*map(inside, (message, decay, scale)))
-    other = swapped(edge, 1 << level | 1)
+    other = swapped(edge[0], 1 << level | 1)
+    near_side = pl.pallas_call(
+        functools.partial(near_side_kernel, slabs, cells),
+        out_shape=[held_array(*message.shape)] * 2 + [held_array(4 * radix, SUBS, LANES)],
+        in_specs=[VMEM] * (levels + 4),
+        out_specs=[VMEM] * 3,
+        name="near_side",
+    )(*map(inside, (message, first, *received, edge[0], decay, scale)))
     entering, mate = pl.pallas_call(
-        functools.partial(entering_kernel, groups, slabs, cells),
+        functools.partial(entering_kernel, groups, slabs),
         out_shape=[held_array(*message.shape)] * 2,
-        in_specs=[VMEM] * (levels + 5),
+        in_specs=[VMEM] * 5,
         out_specs=[VMEM] * 2,
         name="entering",
-    )(*map(inside, (message, first, *received, edge, other, decay, scale)))
+    )(*map(inside, (edge[0], other, *near_side)))
     crossed = [[(i * slabs + z, j * slabs + (z ^ 1)) for i, j in d for z in range(slabs)] for d in distances]
     entered = [entering] + [lax.ppermute(mate, ("gy", "gz"), d) for d in crossed]
     own = pl.pallas_call(

time: 27.3 us -> 27.2 us (level)
  no operation moved by 1% of the time
where the time goes in v5:
time: 27.2 us; the launch traced here: 26.9 us
  starting transfers between devices  12.2 us (45%)
  waiting for transfers between devices  8.91 us (33%)
  Pallas kernels  4.34 us (16%)
  between operations  1.39 us (5%)
    ppermute x5, starting transfers between devices, swapped(): return lax.ppermute(value, 'gz', [(i, i ^ bits) for i in range(slabs)])  5.99 us
    ppermute x5, waiting for transfers between devices, swapped(): return lax.ppermute(value, 'gz', [(i, i ^ bits) for i in range(slabs)])  4.78 us
    ppermute x1, starting transfers between devices, on_device(): lax.ppermute(x, 'gy', d)  3 us
    ppermute x1, waiting for transfers between devices, on_device(): lax.ppermute(x, 'gy', d)  2.76 us
    ppermute x1, starting transfers between devices, on_device(): held = [lax.ppermute(x, 'gy', d) for x, d in zip(pieces[1:], distances)]  1.63 us
    ppermute x1, starting transfers between devices, on_device(): lax.ppermute(mate, ('gy', 'gz'), d)  1.61 us
    ppermute x1, waiting for transfers between devices, on_device(): lax.ppermute(mate, ('gy', 'gz'), d)  1.37 us
    pallas_call x1, Pallas kernels, on_device(): pl.pallas_call(functools.partial(finish_kernel, groups), out_shape=[float...  1.28 us
  transfers between devices with their start and end apart: 8, of which 6 were waited for; matrix products, arithmetic and copies ran while one was open for 0% of the time, Pallas kernels for 6%

profile of v5, /device:TPU:0, one launch (start us, length us, event | category | flops | bytes accessed | tf_op | source)
XLA Modules:
  0.0 26.9 jit_solution(15018511380989258963)
XLA Ops:
  0.6 0.0 copy-start.1
  0.6 0.0 copy-start.4
  0.7 1.0 %pack.1 = (f32[8,512]{1,0:T(8,128)S(1)}, f32[2,4,4,8,128]{4,3,2,1,0:T(8,128)S(1)}, f32[2,4,4,8,128]{4,3,2,1,0:T(8,128)S(1)}) custom-call(f32[8,2,8,512]{3,2,1,0:T(8,128)} %residual_any.1, s32[8,512]{1,0:T(8,128)} %labels_any.1, f32[3]{0:T(128)} %diffusivity_any.1), custom_call_target="tpu_custom_call" | custom-call | tf_op jit(solution)/shard_map/pack/pallas_call | solution.py:503
  1.7 0.0 copy-start.3
  1.7 3.0 %collective-permute-start = (f32[2,4,4,8,128]{4,3,2,1,0:T(8,128)S(1)}, f32[2,4,4,8,128]{4,3,2,1,0:T(8,128)S(1)}, u32[]{:S(2)}, u32[]{:S(2)}) collective-permute-start(f32[2,4,4,8,128]{4,3,2,1,0:T(8,128)S(1)} %get-tuple-element.26), channel_id=1, source_target_pairs={{0,16},{16,0},{1,17},{17,1},{2,18},{18,2},{3,19},{19,3},{4,20},{20... | collective-permute-start | bytes 393224 | tf_op jit(solution)/shard_map/ppermute | solution.py:518
  4.7 0.0 copy-done.4
  4.7 0.7 %roots.1 = (f32[8,8,128]{2,1,0:T(8,128)S(1)}, f32[8,8,128]{2,1,0:T(8,128)S(1)}, f32[8,8,128]{2,1,0:T(8,128)S(1)}, f32[8,8,128]{2,1,0:T(8,128)S(1)}) custom-call(f32[8,128]{1,0:T(8,128)S(1)} %copy-done.4, f32[8]{0:T(128)} %eigen_ref.1), custom_call_target="tpu_custom_call" | custom-call | tf_op jit(solution)/shard_map/roots/pallas_call | solution.py:519
  5.5 2.8 %collective-permute-done.refs_1_ = f32[2,4,4,8,128]{4,3,2,1,0:T(8,128)S(1)} collective-permute-done((f32[2,4,4,8,128]{4,3,2,1,0:T(8,128)S(1)}, f32[2,4,4,8,128]{4,3,2,1,0:T(8,128)S(1)}, u32[]{:S(2)}, u32[]{:S(2)}) %collective-permute-start) | collective-permute-done | bytes 131104 | tf_op jit(solution)/shard_map/ppermute | solution.py:518
  8.2 0.0 copy-done.1
  8.2 0.0 copy-done.3
  8.2 0.4 %forward.1 = (f32[17,8,128]{2,1,0:T(8,128)S(1)}, f32[2,8,4,8,128]{4,3,2,1,0:T(8,128)S(1)}) custom-call(f32[2,4,4,8,128]{4,3,2,1,0:T(8,128)S(1)} %get-tuple-element.25.refs_0_, f32[2,4,4,8,128]{4,3,2,1,0:T(8,128)S(1)} %collective-permute-done.refs_1_, bf16[2,256,256]{2,1,0:T(8,128)(2,1)S(1)} %copy-done.1, f32[2,8,128]{2,1,0:T(8,128)S(1)} %copy-done.3, ...), custom_call_target="tpu_custom_call" | custom-call | tf_op jit(solution)/shard_map/forward/pallas_call | solution.py:528
  8.6 0.0 copy-start
  8.6 0.1 collective-permute-start.1
  8.7 1.2 %collective-permute-done.1.other_ref.refs_2_ = f32[17,8,128]{2,1,0:T(8,128)S(1)} collective-permute-done((f32[17,8,128]{2,1,0:T(8,128)S(1)}, f32[17,8,128]{2,1,0:T(8,128)S(1)}, u32[]{:S(2)}, u32[]{:S(2)}) %collective-permute-start.1) | collective-permute-done | bytes 69664 | tf_op jit(solution)/shard_map/ppermute | solution.py:540
  10.0 2.6 %collective-permute-start.4 = (f32[17,8,128]{2,1,0:T(8,128)S(1)}, f32[17,8,128]{2,1,0:T(8,128)S(1)}, u32[]{:S(2)}, u32[]{:S(2)}) collective-permute-start(f32[17,8,128]{2,1,0:T(8,128)S(1)} %join0.1.own_ref), channel_id=1, source_target_pairs={{0,7},{1,6},{2,5},{3,4},{4,3},{5,2},{6,1},{7,0},{8,15},{9,14},{10,... | collective-permute-start | bytes 208904 | tf_op jit(solution)/shard_map/ppermute | solution.py:540
  12.6 0.4 %collective-permute-start.3 = (f32[17,8,128]{2,1,0:T(8,128)S(1)}, f32[17,8,128]{2,1,0:T(8,128)S(1)}, u32[]{:S(2)}, u32[]{:S(2)}) collective-permute-start(f32[17,8,128]{2,1,0:T(8,128)S(1)} %join0.1.own_ref), channel_id=1, source_target_pairs={{0,5},{1,4},{2,7},{3,6},{4,1},{5,0},{6,3},{7,2},{8,13},{9,12},{10,... | collective-permute-start | bytes 208904 | tf_op jit(solution)/shard_map/ppermute | solution.py:540
  13.0 0.2 collective-permute-start.2
  13.2 0.0 copy-done
  13.2 0.3 %local.1 = (f32[8,4,8,128]{3,2,1,0:T(8,128)S(1)}, f32[8,4,8,128]{3,2,1,0:T(8,128)S(1)}) custom-call(f32[2,8,4,8,128]{4,3,2,1,0:T(8,128)S(1)} %get-tuple-element.38.local_ref, f32[8,8,128]{2,1,0:T(8,128)S(1)} %get-tuple-element.28.refs_5_.scale_ref.refs_7_, bf16[2,256,256]{2,1,0:T(8,128)(2,1)S(1)} %copy-done, f32[2,8,128]{2,1,0:T(8,128)S(1)} %copy-done.3), custom_call_target="tpu_custom_call" | custom-call | tf_op jit(solution)/shard_map/local/pallas_call | solution.py:571
  13.5 1.6 %collective-permute-start.7 = (f32[8,4,8,128]{3,2,1,0:T(8,128)S(1)}, f32[8,4,8,128]{3,2,1,0:T(8,128)S(1)}, u32[]{:S(2)}, u32[]{:S(2)}) collective-permute-start(f32[8,4,8,128]{3,2,1,0:T(8,128)S(1)} %get-tuple-element.40), channel_id=1, source_target_pairs={{0,16},{16,0},{1,17},{17,1},{2,18},{18,2},{3,19},{19,3},{4,20},{20... | collective-permute-start | bytes 393224 | tf_op jit(solution)/shard_map/ppermute | solution.py:578
  15.2 0.0 collective-permute-done.4.cross_ref
  15.2 1.7 %collective-permute-done.3.far_ref = f32[17,8,128]{2,1,0:T(8,128)S(1)} collective-permute-done((f32[17,8,128]{2,1,0:T(8,128)S(1)}, f32[17,8,128]{2,1,0:T(8,128)S(1)}, u32[]{:S(2)}, u32[]{:S(2)}) %collective-permute-start.3) | collective-permute-done | bytes 69664 | tf_op jit(solution)/shard_map/ppermute | solution.py:540
  16.9 0.2 collective-permute-done.2.near_ref.refs_3_
  17.1 0.1 join1.1
  17.3 2.7 %collective-permute-start.5 = (f32[9,8,128]{2,1,0:T(8,128)S(1)}, f32[9,8,128]{2,1,0:T(8,128)S(1)}, u32[]{:S(2)}, u32[]{:S(2)}) collective-permute-start(f32[9,8,128]{2,1,0:T(8,128)S(1)} %get-tuple-element.30.refs_5_.edge_ref), channel_id=1, source_target_pairs={{0,9},{1,8},{2,11},{3,10},{4,13},{5,12},{6,15},{7,14},{8,1},{9,0},... | collective-permute-start | bytes 110600 | tf_op jit(solution)/shard_map/ppermute | solution.py:540
  20.0 0.1 near_side.1
  20.1 1.5 %collective-permute-done.5.other_ref = f32[9,8,128]{2,1,0:T(8,128)S(1)} collective-permute-done((f32[9,8,128]{2,1,0:T(8,128)S(1)}, f32[9,8,128]{2,1,0:T(8,128)S(1)}, u32[]{:S(2)}, u32[]{:S(2)}) %collective-permute-start.5) | collective-permute-done | bytes 36896 | tf_op jit(solution)/shard_map/ppermute | solution.py:540
  21.7 1.6 %collective-permute-start.6 = (f32[17,8,128]{2,1,0:T(8,128)S(1)}, f32[17,8,128]{2,1,0:T(8,128)S(1)}, u32[]{:S(2)}, u32[]{:S(2)}) collective-permute-start(f32[17,8,128]{2,1,0:T(8,128)S(1)} %get-tuple-element.37), channel_id=1, source_target_pairs={{0,17},{1,16},{2,19},{3,18},{4,21},{5,20},{6,23},{7,22},{8,25},{9,... | collective-permute-start | bytes 208904 | tf_op jit(solution)/shard_map/ppermute | solution.py:596
  23.9 0.0 copy-start.2
  23.9 0.3 %own.1.refs_2_ = f32[8,4,8,128]{3,2,1,0:T(8,128)S(1)} custom-call(f32[17,8,128]{2,1,0:T(8,128)S(1)} %get-tuple-element.36.entering_ref.refs_0_, f32[8,8,128]{2,1,0:T(8,128)S(1)} %get-tuple-element.27.refs_4_.decay_ref.refs_6_, f32[8,8,128]{2,1,0:T(8,128)S(1)} %get-tuple-element.28.refs_5_.scale_ref.refs_7_, bf16[2,256,256]{2,1,0:T(8,128)(2,1)S(1)} %copy-done, ...), custom_call_target="tpu_custom_call" | custom-call | tf_op jit(solution)/shard_map/own/pallas_call | solution.py:597
  24.2 0.0 collective-permute-done.7.refs_3_
  24.3 1.4 %collective-permute-done.6.refs_1_ = f32[17,8,128]{2,1,0:T(8,128)S(1)} collective-permute-done((f32[17,8,128]{2,1,0:T(8,128)S(1)}, f32[17,8,128]{2,1,0:T(8,128)S(1)}, u32[]{:S(2)}, u32[]{:S(2)}) %collective-permute-start.6) | collective-permute-done | bytes 69664 | tf_op jit(solution)/shard_map/ppermute | solution.py:596
  25.6 0.0 copy-done.2
  25.6 1.3 %finish.1 = (f32[8,2,8,512]{3,2,1,0:T(8,128)}, f32[8,2,8,512]{3,2,1,0:T(8,128)}, f32[1,1]{1,0:T(1,128)}) custom-call(f32[17,8,128]{2,1,0:T(8,128)S(1)} %get-tuple-element.36.entering_ref.refs_0_, f32[17,8,128]{2,1,0:T(8,128)S(1)} %collective-permute-done.6.refs_1_, f32[8,4,8,128]{3,2,1,0:T(8,128)S(1)} %own.1.refs_2_, ...), custom_call_target="tpu_custom_call" | custom-call | tf_op jit(solution)/shard_map/finish/pallas_call | solution.py:605
  (2 shorter events, 0.1 us)
Async XLA Ops:
  0.6 7.6 %copy-start.1 = (bf16[2,256,256]{2,1,0:T(8,128)(2,1)S(1)}, bf16[2,256,256]{2,1,0:T(8,128)(2,1)}, u32[]{:S(2)}) copy-start(bf16[2,256,256]{2,1,0:T(8,128)(2,1)} %constant.9.clone.refs_2_) | copy-start | bytes 786436
  0.6 4.1 %copy-start.4 = (f32[8,128]{1,0:T(8,128)S(1)}, f32[8,128]{1,0:T(8,128)}, u32[]{:S(2)}) copy-start(f32[8,128]{1,0:T(8,128)} %constant.8.clone.y_eigen_ref) | copy-start | bytes 12292
  1.7 6.5 %copy-start.3 = (f32[2,8,128]{2,1,0:T(8,128)S(1)}, f32[2,8,128]{2,1,0:T(8,128)}, u32[]{:S(2)}) copy-start(f32[2,8,128]{2,1,0:T(8,128)} %constant.10.clone.refs_3_.twiddle_ref.refs_9_) | copy-start | bytes 24580
  1.7 6.5 %collective-permute-start = (f32[2,4,4,8,128]{4,3,2,1,0:T(8,128)S(1)}, f32[2,4,4,8,128]{4,3,2,1,0:T(8,128)S(1)}, u32[]{:S(2)}, u32[]{:S(2)}) collective-permute-start(f32[2,4,4,8,128]{4,3,2,1,0:T(8,128)S(1)} %get-tuple-element.26), channel_id=1, source_target_pairs={{0,16},{16,0},{1,17},{17,1},{2,18},{18,2},{3,19},{19,3},{4,20},{20... | collective-permute-start | bytes 393224 | tf_op jit(solution)/shard_map/ppermute | solution.py:518
  8.6 4.6 %copy-start = (bf16[2,256,256]{2,1,0:T(8,128)(2,1)S(1)}, bf16[2,256,256]{2,1,0:T(8,128)(2,1)}, u32[]{:S(2)}) copy-start(bf16[2,256,256]{2,1,0:T(8,128)(2,1)} %constant.11.clone.lane_ref.refs_8_) | copy-start | bytes 786436
  8.6 1.3 %collective-permute-start.1 = (f32[17,8,128]{2,1,0:T(8,128)S(1)}, f32[17,8,128]{2,1,0:T(8,128)S(1)}, u32[]{:S(2)}, u32[]{:S(2)}) collective-permute-start(f32[17,8,128]{2,1,0:T(8,128)S(1)} %get-tuple-element.29.own_ref.refs_1_), channel_id=1, source_target_pairs={{0,1},{1,0},{2,3},{3,2},{4,5},{5,4},{6,7},{7,6},{8,9},{9,8},{10,11... | collective-permute-start | bytes 208904 | tf_op jit(solution)/shard_map/ppermute | solution.py:540
  10.0 5.2 %collective-permute-start.4 = (f32[17,8,128]{2,1,0:T(8,128)S(1)}, f32[17,8,128]{2,1,0:T(8,128)S(1)}, u32[]{:S(2)}, u32[]{:S(2)}) collective-permute-start(f32[17,8,128]{2,1,0:T(8,128)S(1)} %join0.1.own_ref), channel_id=1, source_target_pairs={{0,7},{1,6},{2,5},{3,4},{4,3},{5,2},{6,1},{7,0},{8,15},{9,14},{10,... | collective-permute-start | bytes 208904 | tf_op jit(solution)/shard_map/ppermute | solution.py:540
  12.6 4.3 %collective-permute-start.3 = (f32[17,8,128]{2,1,0:T(8,128)S(1)}, f32[17,8,128]{2,1,0:T(8,128)S(1)}, u32[]{:S(2)}, u32[]{:S(2)}) collective-permute-start(f32[17,8,128]{2,1,0:T(8,128)S(1)} %join0.1.own_ref), channel_id=1, source_target_pairs={{0,5},{1,4},{2,7},{3,6},{4,1},{5,0},{6,3},{7,2},{8,13},{9,12},{10,... | collective-permute-start | bytes 208904 | tf_op jit(solution)/shard_map/ppermute | solution.py:540
  13.0 4.1 %collective-permute-start.2 = (f32[17,8,128]{2,1,0:T(8,128)S(1)}, f32[17,8,128]{2,1,0:T(8,128)S(1)}, u32[]{:S(2)}, u32[]{:S(2)}) collective-permute-start(f32[17,8,128]{2,1,0:T(8,128)S(1)} %join0.1.own_ref), channel_id=1, source_target_pairs={{0,3},{1,2},{2,1},{3,0},{4,7},{5,6},{6,5},{7,4},{8,11},{9,10},{10,... | collective-permute-start | bytes 208904 | tf_op jit(solution)/shard_map/ppermute | solution.py:540
  13.5 10.7 %collective-permute-start.7 = (f32[8,4,8,128]{3,2,1,0:T(8,128)S(1)}, f32[8,4,8,128]{3,2,1,0:T(8,128)S(1)}, u32[]{:S(2)}, u32[]{:S(2)}) collective-permute-start(f32[8,4,8,128]{3,2,1,0:T(8,128)S(1)} %get-tuple-element.40), channel_id=1, source_target_pairs={{0,16},{16,0},{1,17},{17,1},{2,18},{18,2},{3,19},{19,3},{4,20},{20... | collective-permute-start | bytes 393224 | tf_op jit(solution)/shard_map/ppermute | solution.py:578
  17.3 4.4 %collective-permute-start.5 = (f32[9,8,128]{2,1,0:T(8,128)S(1)}, f32[9,8,128]{2,1,0:T(8,128)S(1)}, u32[]{:S(2)}, u32[]{:S(2)}) collective-permute-start(f32[9,8,128]{2,1,0:T(8,128)S(1)} %get-tuple-element.30.refs_5_.edge_ref), channel_id=1, source_target_pairs={{0,9},{1,8},{2,11},{3,10},{4,13},{5,12},{6,15},{7,14},{8,1},{9,0},... | collective-permute-start | bytes 110600 | tf_op jit(solution)/shard_map/ppermute | solution.py:540
  21.7 4.0 %collective-permute-start.6 = (f32[17,8,128]{2,1,0:T(8,128)S(1)}, f32[17,8,128]{2,1,0:T(8,128)S(1)}, u32[]{:S(2)}, u32[]{:S(2)}) collective-permute-start(f32[17,8,128]{2,1,0:T(8,128)S(1)} %get-tuple-element.37), channel_id=1, source_target_pairs={{0,17},{1,16},{2,19},{3,18},{4,21},{5,20},{6,23},{7,22},{8,25},{9,... | collective-permute-start | bytes 208904 | tf_op jit(solution)/shard_map/ppermute | solution.py:596
  23.9 1.7 %copy-start.2 = (f32[8,2,8,512]{3,2,1,0:T(8,128)S(1)}, f32[8,2,8,512]{3,2,1,0:T(8,128)}, u32[]{:S(2)}) copy-start(f32[8,2,8,512]{3,2,1,0:T(8,128)} %refs_11_.1) | copy-start | bytes 786436

commit v6 on v5

--- a/solution.py
+++ b/solution.py
@@ -197,6 +197,42 @@
         out_refs[2 * s + 1][...] = scale
 
 
+def slab_scan(cell, d, groups):
+    inner, kept = len(cell), SUBS // groups
+    group = sub_ids((SUBS, LANES)) // kept
+    ahead, behind = [cell[0]], [cell[-1]]
+    for i in range(1, inner):
+        ahead.append(cell[i] + d * ahead[-1])
+        behind.append(cell[inner - 1 - i] + d * behind[-1])
+    behind = behind[::-1]
+    value = [ahead[i] + behind[i] - cell[i] for i in range(inner)]
+    total = sum(cell[i] * value[i] for i in range(inner))
+    last, first = ahead[-1], behind[0]
+    from_low = jnp.zeros_like(last)
+    from_high = jnp.zeros_like(first)
+    low_weight, high_weight = jnp.ones_like(last), jnp.ones_like(first)
+    bit = 1
+    while bit < groups:
+        upper = (group & bit) != 0
+        step = bit * kept
+        if 2 * step == SUBS:
+            other_last, other_first = turn(last, step), turn(first, step)
+        else:
+            other_last = jnp.where(upper, turn(last, step), turn(last, -step))
+            other_first = jnp.where(upper, turn(first, step), turn(first, -step))
+        span = power(d, inner * bit)
+        joined = 2.0 * d * other_last * first
+        total = total + jnp.where(upper & ((group & (bit - 1)) == 0), joined, 0.0)
+        from_low = from_low + jnp.where(upper, low_weight * other_last, 0.0)
+        from_high = from_high + jnp.where(upper, 0.0, high_weight * other_first)
+        low_weight = low_weight * jnp.where(upper, span, 1.0)
+        high_weight = high_weight * jnp.where(upper, 1.0, span)
+        last = jnp.where(upper, last + span * other_last, other_last + span * last)
+        first = jnp.where(upper, other_first + span * first, first + span * other_first)
+        bit *= 2
+    return last, first, total, value, from_low, from_high
+
+
 def forward_kernel(groups, *refs):
     held = refs[:groups]
     lane_ref, twiddle_ref, decay_ref, scale_ref = refs[groups : groups + 4]
@@ -226,41 +262,10 @@
         for a in range(radix):
             d, g = decay[a], scale[a]
             cell = [field[a][i] for i in range(inner)]
-            ahead, behind = [cell[0]], [cell[-1]]
-            for i in range(1, inner):
-                ahead.append(cell[i] + d * ahead[-1])
-                behind.append(cell[inner - 1 - i] + d * behind[-1])
-            behind = behind[::-1]
-            value = [ahead[i] + behind[i] - cell[i] for i in range(inner)]
-            total = sum(cell[i] * value[i] for i in range(inner))
-            last, first = ahead[-1], behind[0]
-            from_low = jnp.zeros_like(last)
-            from_high = jnp.zeros_like(first)
-            low_weight, high_weight = jnp.ones_like(last), jnp.ones_like(first)
-            bit = 1
-            while bit < groups:
-                upper = (group & bit) != 0
-                step = bit * kept
-                if 2 * step == SUBS:
-                    other_last, other_first = turn(last, step), turn(first, step)
-                else:
-                    other_last = jnp.where(upper, turn(last, step), turn(last, -step))
-                    other_first = jnp.where(upper, turn(first, step), turn(first, -step))
-                span = power(d, inner * bit)
-                joined = 2.0 * d * other_last * first
-                total = total + jnp.where(upper & ((group & (bit - 1)) == 0), joined, 0.0)
-                from_low = from_low + jnp.where(upper, low_weight * other_last, 0.0)
-                from_high = from_high + jnp.where(upper, 0.0, high_weight * other_first)
-                low_weight = low_weight * jnp.where(upper, span, 1.0)
-                high_weight = high_weight * jnp.where(upper, 1.0, span)
-                last = jnp.where(upper, last + span * other_last, other_last + span * last)
-                first = jnp.where(upper, other_first + span * first, first + span * other_first)
-                bit *= 2
+            last, first, total, _, _, _ = slab_scan(cell, d, groups)
             energy = energy + g * total
             message_ref[part * radix + a] = jnp.where(subs < HALF, last, first)
-            for i in range(inner):
-                spread = power(d, i + 1) * from_low + power(d, inner - i) * from_high
-                local_ref[part, a, i] = value[i] + spread
+            local_ref[part, a] = field[a]
     message_ref[2 * radix] = energy
 
 
@@ -341,10 +346,17 @@
     return small_dft(turned_re, turned_im, 1.0)
 
 
-def local_kernel(groups, local_ref, scale_ref, lane_ref, twiddle_ref, *out_refs):
+def local_kernel(groups, local_ref, decay_ref, scale_ref, lane_ref, twiddle_ref, *out_refs):
     radix = scale_ref.shape[0]
     rows = radix // groups
-    fields = [[scale_ref[a] * local_ref[part, a] for a in range(radix)] for part in range(2)]
+    inner = local_ref.shape[2]
+    fields = ([], [])
+    for part in range(2):
+        for a in range(radix):
+            d = decay_ref[a]
+            _, _, _, value, from_low, from_high = slab_scan([local_ref[part, a, i] for i in range(inner)], d, groups)
+            whole = [value[i] + power(d, i + 1) * from_low + power(d, inner - i) * from_high for i in range(inner)]
+            fields[part].append(scale_ref[a] * jnp.stack(whole))
     for part, field in enumerate(to_planes(*fields, lane_ref, twiddle_ref)):
         for a in range(rows):
             pieces = [field[t * rows + a] for t in range(groups)]
@@ -571,10 +583,10 @@
     pieces = pl.pallas_call(
         functools.partial(local_kernel, groups),
         out_shape=[piece] * groups,
-        in_specs=[VMEM] * 4,
+        in_specs=[VMEM] * 5,
         out_specs=[VMEM] * groups,
         name="local",
-    )(*map(inside, (local, scale, *tables)))
+    )(*map(inside, (local, decay, scale, *tables)))
     held = [lax.ppermute(x, "gy", d) for x, d in zip(pieces[1:], distances)]
 
     other = swapped(edge[0], 1 << level | 1)

time: 27.2 us -> 27.2 us (level)
  no operation moved by 1% of the time
where the time goes in v6:
time: 27.2 us; the launch traced here: 26.9 us
  starting transfers between devices  12.2 us (45%)
  waiting for transfers between devices  8.89 us (33%)
  Pallas kernels  4.33 us (16%)
  between operations  1.39 us (5%)
    ppermute x5, starting transfers between devices, swapped(): return lax.ppermute(value, 'gz', [(i, i ^ bits) for i in range(slabs)])  5.99 us
    ppermute x5, waiting for transfers between devices, swapped(): return lax.ppermute(value, 'gz', [(i, i ^ bits) for i in range(slabs)])  4.75 us
    ppermute x1, starting transfers between devices, on_device(): lax.ppermute(x, 'gy', d)  3 us
    ppermute x1, waiting for transfers between devices, on_device(): lax.ppermute(x, 'gy', d)  2.76 us
    ppermute x1, starting transfers between devices, on_device(): held = [lax.ppermute(x, 'gy', d) for x, d in zip(pieces[1:], distances)]  1.63 us
    ppermute x1, starting transfers between devices, on_device(): lax.ppermute(mate, ('gy', 'gz'), d)  1.61 us
    ppermute x1, waiting for transfers between devices, on_device(): lax.ppermute(mate, ('gy', 'gz'), d)  1.37 us
    pallas_call x1, Pallas kernels, on_device(): pl.pallas_call(functools.partial(finish_kernel, groups), out_shape=[float...  1.28 us
  transfers between devices with their start and end apart: 8, of which 6 were waited for; matrix products, arithmetic and copies ran while one was open for 0% of the time, Pallas kernels for 6%

profile of v6, /device:TPU:0, one launch (start us, length us, event | category | flops | bytes accessed | tf_op | source)
XLA Modules:
  0.0 26.9 jit_solution(4447111967053586701)
XLA Ops:
  0.6 0.0 copy-start.1
  0.6 0.0 copy-start.4
  0.7 1.0 %pack.1 = (f32[8,512]{1,0:T(8,128)S(1)}, f32[2,4,4,8,128]{4,3,2,1,0:T(8,128)S(1)}, f32[2,4,4,8,128]{4,3,2,1,0:T(8,128)S(1)}) custom-call(f32[8,2,8,512]{3,2,1,0:T(8,128)} %residual_any.1, s32[8,512]{1,0:T(8,128)} %labels_any.1, f32[3]{0:T(128)} %diffusivity_any.1), custom_call_target="tpu_custom_call" | custom-call | tf_op jit(solution)/shard_map/pack/pallas_call | solution.py:515
  1.7 0.0 copy-start.3
  1.7 3.0 %collective-permute-start = (f32[2,4,4,8,128]{4,3,2,1,0:T(8,128)S(1)}, f32[2,4,4,8,128]{4,3,2,1,0:T(8,128)S(1)}, u32[]{:S(2)}, u32[]{:S(2)}) collective-permute-start(f32[2,4,4,8,128]{4,3,2,1,0:T(8,128)S(1)} %get-tuple-element.26), channel_id=1, source_target_pairs={{0,16},{16,0},{1,17},{17,1},{2,18},{18,2},{3,19},{19,3},{4,20},{20... | collective-permute-start | bytes 393224 | tf_op jit(solution)/shard_map/ppermute | solution.py:530
  4.7 0.0 copy-done.4
  4.7 0.7 %roots.1 = (f32[8,8,128]{2,1,0:T(8,128)S(1)}, f32[8,8,128]{2,1,0:T(8,128)S(1)}, f32[8,8,128]{2,1,0:T(8,128)S(1)}, f32[8,8,128]{2,1,0:T(8,128)S(1)}) custom-call(f32[8,128]{1,0:T(8,128)S(1)} %copy-done.4, f32[8]{0:T(128)} %eigen_ref.1), custom_call_target="tpu_custom_call" | custom-call | tf_op jit(solution)/shard_map/roots/pallas_call | solution.py:531
  5.5 2.8 %collective-permute-done.refs_1_ = f32[2,4,4,8,128]{4,3,2,1,0:T(8,128)S(1)} collective-permute-done((f32[2,4,4,8,128]{4,3,2,1,0:T(8,128)S(1)}, f32[2,4,4,8,128]{4,3,2,1,0:T(8,128)S(1)}, u32[]{:S(2)}, u32[]{:S(2)}) %collective-permute-start) | collective-permute-done | bytes 131104 | tf_op jit(solution)/shard_map/ppermute | solution.py:530
  8.2 0.0 copy-done.1
  8.2 0.0 copy-done.3
  8.2 0.3 %forward.1 = (f32[17,8,128]{2,1,0:T(8,128)S(1)}, f32[2,8,4,8,128]{4,3,2,1,0:T(8,128)S(1)}) custom-call(f32[2,4,4,8,128]{4,3,2,1,0:T(8,128)S(1)} %get-tuple-element.25.refs_0_, f32[2,4,4,8,128]{4,3,2,1,0:T(8,128)S(1)} %collective-permute-done.refs_1_, bf16[2,256,256]{2,1,0:T(8,128)(2,1)S(1)} %copy-done.1, f32[2,8,128]{2,1,0:T(8,128)S(1)} %copy-done.3, ...), custom_call_target="tpu_custom_call" | custom-call | tf_op jit(solution)/shard_map/forward/pallas_call | solution.py:540
  8.6 0.0 copy-start
  8.6 0.1 collective-permute-start.1
  8.7 1.2 %collective-permute-done.1.other_ref.refs_2_ = f32[17,8,128]{2,1,0:T(8,128)S(1)} collective-permute-done((f32[17,8,128]{2,1,0:T(8,128)S(1)}, f32[17,8,128]{2,1,0:T(8,128)S(1)}, u32[]{:S(2)}, u32[]{:S(2)}) %collective-permute-start.1) | collective-permute-done | bytes 69664 | tf_op jit(solution)/shard_map/ppermute | solution.py:552
  9.9 2.6 %collective-permute-start.4 = (f32[17,8,128]{2,1,0:T(8,128)S(1)}, f32[17,8,128]{2,1,0:T(8,128)S(1)}, u32[]{:S(2)}, u32[]{:S(2)}) collective-permute-start(f32[17,8,128]{2,1,0:T(8,128)S(1)} %join0.1.own_ref), channel_id=1, source_target_pairs={{0,7},{1,6},{2,5},{3,4},{4,3},{5,2},{6,1},{7,0},{8,15},{9,14},{10,... | collective-permute-start | bytes 208904 | tf_op jit(solution)/shard_map/ppermute | solution.py:552
  12.6 0.4 %collective-permute-start.3 = (f32[17,8,128]{2,1,0:T(8,128)S(1)}, f32[17,8,128]{2,1,0:T(8,128)S(1)}, u32[]{:S(2)}, u32[]{:S(2)}) collective-permute-start(f32[17,8,128]{2,1,0:T(8,128)S(1)} %join0.1.own_ref), channel_id=1, source_target_pairs={{0,5},{1,4},{2,7},{3,6},{4,1},{5,0},{6,3},{7,2},{8,13},{9,12},{10,... | collective-permute-start | bytes 208904 | tf_op jit(solution)/shard_map/ppermute | solution.py:552
  13.0 0.2 collective-permute-start.2
  13.2 0.0 copy-done
  13.2 0.3 %local.1 = (f32[8,4,8,128]{3,2,1,0:T(8,128)S(1)}, f32[8,4,8,128]{3,2,1,0:T(8,128)S(1)}) custom-call(f32[2,8,4,8,128]{4,3,2,1,0:T(8,128)S(1)} %get-tuple-element.38.local_ref, f32[8,8,128]{2,1,0:T(8,128)S(1)} %get-tuple-element.27.refs_4_.decay_ref.refs_6_, f32[8,8,128]{2,1,0:T(8,128)S(1)} %get-tuple-element.28.refs_5_.scale_ref.refs_7_, ...), custom_call_target="tpu_custom_call" | custom-call | tf_op jit(solution)/shard_map/local/pallas_call | solution.py:583
  13.5 1.6 %collective-permute-start.7 = (f32[8,4,8,128]{3,2,1,0:T(8,128)S(1)}, f32[8,4,8,128]{3,2,1,0:T(8,128)S(1)}, u32[]{:S(2)}, u32[]{:S(2)}) collective-permute-start(f32[8,4,8,128]{3,2,1,0:T(8,128)S(1)} %get-tuple-element.40), channel_id=1, source_target_pairs={{0,16},{16,0},{1,17},{17,1},{2,18},{18,2},{3,19},{19,3},{4,20},{20... | collective-permute-start | bytes 393224 | tf_op jit(solution)/shard_map/ppermute | solution.py:590
  15.1 0.0 collective-permute-done.4.cross_ref
  15.1 1.7 %collective-permute-done.3.far_ref = f32[17,8,128]{2,1,0:T(8,128)S(1)} collective-permute-done((f32[17,8,128]{2,1,0:T(8,128)S(1)}, f32[17,8,128]{2,1,0:T(8,128)S(1)}, u32[]{:S(2)}, u32[]{:S(2)}) %collective-permute-start.3) | collective-permute-done | bytes 69664 | tf_op jit(solution)/shard_map/ppermute | solution.py:552
  16.9 0.2 collective-permute-done.2.near_ref.refs_3_
  17.1 0.1 join1.1
  17.2 2.7 %collective-permute-start.5 = (f32[9,8,128]{2,1,0:T(8,128)S(1)}, f32[9,8,128]{2,1,0:T(8,128)S(1)}, u32[]{:S(2)}, u32[]{:S(2)}) collective-permute-start(f32[9,8,128]{2,1,0:T(8,128)S(1)} %get-tuple-element.30.refs_5_.edge_ref), channel_id=1, source_target_pairs={{0,9},{1,8},{2,11},{3,10},{4,13},{5,12},{6,15},{7,14},{8,1},{9,0},... | collective-permute-start | bytes 110600 | tf_op jit(solution)/shard_map/ppermute | solution.py:552
  19.9 0.1 near_side.1
  20.0 1.5 %collective-permute-done.5.other_ref = f32[9,8,128]{2,1,0:T(8,128)S(1)} collective-permute-done((f32[9,8,128]{2,1,0:T(8,128)S(1)}, f32[9,8,128]{2,1,0:T(8,128)S(1)}, u32[]{:S(2)}, u32[]{:S(2)}) %collective-permute-start.5) | collective-permute-done | bytes 36896 | tf_op jit(solution)/shard_map/ppermute | solution.py:552
  21.6 1.6 %collective-permute-start.6 = (f32[17,8,128]{2,1,0:T(8,128)S(1)}, f32[17,8,128]{2,1,0:T(8,128)S(1)}, u32[]{:S(2)}, u32[]{:S(2)}) collective-permute-start(f32[17,8,128]{2,1,0:T(8,128)S(1)} %get-tuple-element.37), channel_id=1, source_target_pairs={{0,17},{1,16},{2,19},{3,18},{4,21},{5,20},{6,23},{7,22},{8,25},{9,... | collective-permute-start | bytes 208904 | tf_op jit(solution)/shard_map/ppermute | solution.py:608
  23.9 0.0 copy-start.2
  23.9 0.3 %own.1.refs_2_ = f32[8,4,8,128]{3,2,1,0:T(8,128)S(1)} custom-call(f32[17,8,128]{2,1,0:T(8,128)S(1)} %get-tuple-element.36.entering_ref.refs_0_, f32[8,8,128]{2,1,0:T(8,128)S(1)} %get-tuple-element.27.refs_4_.decay_ref.refs_6_, f32[8,8,128]{2,1,0:T(8,128)S(1)} %get-tuple-element.28.refs_5_.scale_ref.refs_7_, bf16[2,256,256]{2,1,0:T(8,128)(2,1)S(1)} %copy-done, ...), custom_call_target="tpu_custom_call" | custom-call | tf_op jit(solution)/shard_map/own/pallas_call | solution.py:609
  24.2 0.0 collective-permute-done.7.refs_3_
  24.2 1.4 %collective-permute-done.6.refs_1_ = f32[17,8,128]{2,1,0:T(8,128)S(1)} collective-permute-done((f32[17,8,128]{2,1,0:T(8,128)S(1)}, f32[17,8,128]{2,1,0:T(8,128)S(1)}, u32[]{:S(2)}, u32[]{:S(2)}) %collective-permute-start.6) | collective-permute-done | bytes 69664 | tf_op jit(solution)/shard_map/ppermute | solution.py:608
  25.6 0.0 copy-done.2
  25.6 1.3 %finish.1 = (f32[8,2,8,512]{3,2,1,0:T(8,128)}, f32[8,2,8,512]{3,2,1,0:T(8,128)}, f32[1,1]{1,0:T(1,128)}) custom-call(f32[17,8,128]{2,1,0:T(8,128)S(1)} %get-tuple-element.36.entering_ref.refs_0_, f32[17,8,128]{2,1,0:T(8,128)S(1)} %collective-permute-done.6.refs_1_, f32[8,4,8,128]{3,2,1,0:T(8,128)S(1)} %own.1.refs_2_, ...), custom_call_target="tpu_custom_call" | custom-call | tf_op jit(solution)/shard_map/finish/pallas_call | solution.py:617
  (2 shorter events, 0.1 us)
Async XLA Ops:
  0.6 7.6 %copy-start.1 = (bf16[2,256,256]{2,1,0:T(8,128)(2,1)S(1)}, bf16[2,256,256]{2,1,0:T(8,128)(2,1)}, u32[]{:S(2)}) copy-start(bf16[2,256,256]{2,1,0:T(8,128)(2,1)} %constant.9.clone.refs_2_) | copy-start | bytes 786436
  0.6 4.1 %copy-start.4 = (f32[8,128]{1,0:T(8,128)S(1)}, f32[8,128]{1,0:T(8,128)}, u32[]{:S(2)}) copy-start(f32[8,128]{1,0:T(8,128)} %constant.8.clone.y_eigen_ref) | copy-start | bytes 12292
  1.7 6.5 %copy-start.3 = (f32[2,8,128]{2,1,0:T(8,128)S(1)}, f32[2,8,128]{2,1,0:T(8,128)}, u32[]{:S(2)}) copy-start(f32[2,8,128]{2,1,0:T(8,128)} %constant.10.clone.refs_3_.twiddle_ref.refs_9_) | copy-start | bytes 24580
  1.7 6.5 %collective-permute-start = (f32[2,4,4,8,128]{4,3,2,1,0:T(8,128)S(1)}, f32[2,4,4,8,128]{4,3,2,1,0:T(8,128)S(1)}, u32[]{:S(2)}, u32[]{:S(2)}) collective-permute-start(f32[2,4,4,8,128]{4,3,2,1,0:T(8,128)S(1)} %get-tuple-element.26), channel_id=1, source_target_pairs={{0,16},{16,0},{1,17},{17,1},{2,18},{18,2},{3,19},{19,3},{4,20},{20... | collective-permute-start | bytes 393224 | tf_op jit(solution)/shard_map/ppermute | solution.py:530
  8.6 4.6 %copy-start = (bf16[2,256,256]{2,1,0:T(8,128)(2,1)S(1)}, bf16[2,256,256]{2,1,0:T(8,128)(2,1)}, u32[]{:S(2)}) copy-start(bf16[2,256,256]{2,1,0:T(8,128)(2,1)} %constant.11.clone.lane_ref.refs_8_) | copy-start | bytes 786436
  8.6 1.3 %collective-permute-start.1 = (f32[17,8,128]{2,1,0:T(8,128)S(1)}, f32[17,8,128]{2,1,0:T(8,128)S(1)}, u32[]{:S(2)}, u32[]{:S(2)}) collective-permute-start(f32[17,8,128]{2,1,0:T(8,128)S(1)} %get-tuple-element.29.own_ref.refs_1_), channel_id=1, source_target_pairs={{0,1},{1,0},{2,3},{3,2},{4,5},{5,4},{6,7},{7,6},{8,9},{9,8},{10,11... | collective-permute-start | bytes 208904 | tf_op jit(solution)/shard_map/ppermute | solution.py:552
  9.9 5.2 %collective-permute-start.4 = (f32[17,8,128]{2,1,0:T(8,128)S(1)}, f32[17,8,128]{2,1,0:T(8,128)S(1)}, u32[]{:S(2)}, u32[]{:S(2)}) collective-permute-start(f32[17,8,128]{2,1,0:T(8,128)S(1)} %join0.1.own_ref), channel_id=1, source_target_pairs={{0,7},{1,6},{2,5},{3,4},{4,3},{5,2},{6,1},{7,0},{8,15},{9,14},{10,... | collective-permute-start | bytes 208904 | tf_op jit(solution)/shard_map/ppermute | solution.py:552
  12.6 4.3 %collective-permute-start.3 = (f32[17,8,128]{2,1,0:T(8,128)S(1)}, f32[17,8,128]{2,1,0:T(8,128)S(1)}, u32[]{:S(2)}, u32[]{:S(2)}) collective-permute-start(f32[17,8,128]{2,1,0:T(8,128)S(1)} %join0.1.own_ref), channel_id=1, source_target_pairs={{0,5},{1,4},{2,7},{3,6},{4,1},{5,0},{6,3},{7,2},{8,13},{9,12},{10,... | collective-permute-start | bytes 208904 | tf_op jit(solution)/shard_map/ppermute | solution.py:552
  13.0 4.1 %collective-permute-start.2 = (f32[17,8,128]{2,1,0:T(8,128)S(1)}, f32[17,8,128]{2,1,0:T(8,128)S(1)}, u32[]{:S(2)}, u32[]{:S(2)}) collective-permute-start(f32[17,8,128]{2,1,0:T(8,128)S(1)} %join0.1.own_ref), channel_id=1, source_target_pairs={{0,3},{1,2},{2,1},{3,0},{4,7},{5,6},{6,5},{7,4},{8,11},{9,10},{10,... | collective-permute-start | bytes 208904 | tf_op jit(solution)/shard_map/ppermute | solution.py:552
  13.5 10.7 %collective-permute-start.7 = (f32[8,4,8,128]{3,2,1,0:T(8,128)S(1)}, f32[8,4,8,128]{3,2,1,0:T(8,128)S(1)}, u32[]{:S(2)}, u32[]{:S(2)}) collective-permute-start(f32[8,4,8,128]{3,2,1,0:T(8,128)S(1)} %get-tuple-element.40), channel_id=1, source_target_pairs={{0,16},{16,0},{1,17},{17,1},{2,18},{18,2},{3,19},{19,3},{4,20},{20... | collective-permute-start | bytes 393224 | tf_op jit(solution)/shard_map/ppermute | solution.py:590
  17.2 4.4 %collective-permute-start.5 = (f32[9,8,128]{2,1,0:T(8,128)S(1)}, f32[9,8,128]{2,1,0:T(8,128)S(1)}, u32[]{:S(2)}, u32[]{:S(2)}) collective-permute-start(f32[9,8,128]{2,1,0:T(8,128)S(1)} %get-tuple-element.30.refs_5_.edge_ref), channel_id=1, source_target_pairs={{0,9},{1,8},{2,11},{3,10},{4,13},{5,12},{6,15},{7,14},{8,1},{9,0},... | collective-permute-start | bytes 110600 | tf_op jit(solution)/shard_map/ppermute | solution.py:552
  21.6 4.0 %collective-permute-start.6 = (f32[17,8,128]{2,1,0:T(8,128)S(1)}, f32[17,8,128]{2,1,0:T(8,128)S(1)}, u32[]{:S(2)}, u32[]{:S(2)}) collective-permute-start(f32[17,8,128]{2,1,0:T(8,128)S(1)} %get-tuple-element.37), channel_id=1, source_target_pairs={{0,17},{1,16},{2,19},{3,18},{4,21},{5,20},{6,23},{7,22},{8,25},{9,... | collective-permute-start | bytes 208904 | tf_op jit(solution)/shard_map/ppermute | solution.py:608
  23.9 1.7 %copy-start.2 = (f32[8,2,8,512]{3,2,1,0:T(8,128)S(1)}, f32[8,2,8,512]{3,2,1,0:T(8,128)}, u32[]{:S(2)}) copy-start(f32[8,2,8,512]{3,2,1,0:T(8,128)} %refs_11_.1) | copy-start | bytes 786436

commit v7 on v6

--- a/solution.py
+++ b/solution.py
@@ -336,8 +336,7 @@
     out_ref[radix] = moments[2 * radix] - jnp.where(lax.rem(subs, HALF) < kept, walls, 0.0)
 
 
-def to_planes(re, im, lane_ref, twiddle_ref):
-    re, im = lane_product(re, im, lane_ref)
+def to_planes(re, im, twiddle_ref):
     turned_re, turned_im = [], []
     for a in range(len(re)):
         c, s = twiddle_ref[0, a : a + 1, :], twiddle_ref[1, a : a + 1, :]
@@ -357,7 +356,7 @@
             _, _, _, value, from_low, from_high = slab_scan([local_ref[part, a, i] for i in range(inner)], d, groups)
             whole = [value[i] + power(d, i + 1) * from_low + power(d, inner - i) * from_high for i in range(inner)]
             fields[part].append(scale_ref[a] * jnp.stack(whole))
-    for part, field in enumerate(to_planes(*fields, lane_ref, twiddle_ref)):
+    for part, field in enumerate(to_planes(*lane_product(*fields, lane_ref), twiddle_ref)):
         for a in range(rows):
             pieces = [field[t * rows + a] for t in range(groups)]
             for ref, value in zip(out_refs, for_targets(pieces, lax.axis_index("gy"))):
@@ -422,9 +421,8 @@
     mate_ref[2 * radix] = energy
 
 
-def response(groups, inner, entering_ref, decay_ref, scale_ref, lane_ref, twiddle_ref):
+def response(groups, inner, entering_ref, decay_ref, scale_ref, lane_ref):
     radix = decay_ref.shape[0]
-    rows = radix // groups
     low = sub_ids((SUBS, LANES)) < HALF
     decay = decay_ref[...]
     ahead, behind = group_powers(decay, inner, groups, SUBS // groups)
@@ -438,14 +436,19 @@
             fields[part].append(
                 jnp.stack([power(d, z + 1) * from_low + power(d, inner - z) * from_high for z in range(inner)])
             )
-    planes = to_planes(*fields, lane_ref, twiddle_ref)
+    return lane_product(*fields, lane_ref)
+
+
+def own_planes(groups, re, im, twiddle_ref):
+    rows = len(re) // groups
     me = lax.axis_index("gy")
+    planes = to_planes(re, im, twiddle_ref)
     return [[for_targets([field[t * rows + a] for t in range(groups)], me)[0] for a in range(rows)] for field in planes]
 
 
 def own_kernel(groups, entering_ref, decay_ref, scale_ref, lane_ref, twiddle_ref, local_ref, out_ref):
     rows, inner = local_ref.shape[0] // 2, local_ref.shape[1]
-    field = response(groups, inner, entering_ref, decay_ref, scale_ref, lane_ref, twiddle_ref)
+    field = own_planes(groups, *response(groups, inner, entering_ref, decay_ref, scale_ref, lane_ref), twiddle_ref)
     for part in range(2):
         for a in range(rows):
             out_ref[part * rows + a] = field[part][a] + local_ref[part * rows + a]
@@ -466,15 +469,18 @@
     copies = [pltpu.make_async_copy(total_buffer, total_ref, total_sem)]
     copies[0].start()
     ratio = total / rz_prev_ref[0]
-    held = [[[parts[0][part * rows + a] for a in range(rows)] for part in range(2)]]
-    for s in range(1, groups):
-        field = response(groups, inner, entering[s], roots[2 * s], roots[2 * s + 1], lane_ref, twiddle_ref)
-        held.append([[field[part][a] + parts[s][part * rows + a] for a in range(rows)] for part in range(2)])
+    responses = [
+        response(groups, inner, entering[s], roots[2 * s], roots[2 * s + 1], lane_ref) for s in range(1, groups)
+    ]
     for zp in range(inner):
+        held = [[[parts[0][part * rows + a, zp] for a in range(rows)] for part in range(2)]]
+        for s, (re, im) in enumerate(responses, 1):
+            field = own_planes(groups, [v[zp] for v in re], [v[zp] for v in im], twiddle_ref)
+            held.append([[field[part][a] + parts[s][part * rows + a, zp] for a in range(rows)] for part in range(2)])
         for part in range(2):
             for a in range(rows):
                 lanes = slice(a * LANES, (a + 1) * LANES)
-                sources = by_source([fields[part][a][zp] for fields in held], me)
+                sources = by_source([fields[part][a] for fields in held], me)
                 for zg in range(groups):
                     z = zg * inner + zp
                     value = turn(sources[0], -zg * kept)

time: 27.2 us -> 27.2 us (level)
  no operation moved by 1% of the time
where the time goes in v7:
time: 27.2 us; the launch traced here: 26.9 us
  starting transfers between devices  12.2 us (45%)
  waiting for transfers between devices  8.89 us (33%)
  Pallas kernels  4.32 us (16%)
  between operations  1.39 us (5%)
    ppermute x5, starting transfers between devices, swapped(): return lax.ppermute(value, 'gz', [(i, i ^ bits) for i in range(slabs)])  5.99 us
    ppermute x5, waiting for transfers between devices, swapped(): return lax.ppermute(value, 'gz', [(i, i ^ bits) for i in range(slabs)])  4.75 us
    ppermute x1, starting transfers between devices, on_device(): lax.ppermute(x, 'gy', d)  3 us
    ppermute x1, waiting for transfers between devices, on_device(): lax.ppermute(x, 'gy', d)  2.76 us
    ppermute x1, starting transfers between devices, on_device(): held = [lax.ppermute(x, 'gy', d) for x, d in zip(pieces[1:], distances)]  1.63 us
    ppermute x1, starting transfers between devices, on_device(): lax.ppermute(mate, ('gy', 'gz'), d)  1.61 us
    ppermute x1, waiting for transfers between devices, on_device(): lax.ppermute(mate, ('gy', 'gz'), d)  1.37 us
    pallas_call x1, Pallas kernels, on_device(): pl.pallas_call(functools.partial(finish_kernel, groups), out_shape=[float...  1.27 us
  transfers between devices with their start and end apart: 8, of which 6 were waited for; matrix products, arithmetic and copies ran while one was open for 0% of the time, Pallas kernels for 6%

profile of v7, /device:TPU:0, one launch (start us, length us, event | category | flops | bytes accessed | tf_op | source)
XLA Modules:
  0.0 26.9 jit_solution(14589342043806734412)
XLA Ops:
  0.6 0.0 copy-start.1
  0.6 0.0 copy-start.4
  0.7 1.0 %pack.1 = (f32[8,512]{1,0:T(8,128)S(1)}, f32[2,4,4,8,128]{4,3,2,1,0:T(8,128)S(1)}, f32[2,4,4,8,128]{4,3,2,1,0:T(8,128)S(1)}) custom-call(f32[8,2,8,512]{3,2,1,0:T(8,128)} %residual_any.1, s32[8,512]{1,0:T(8,128)} %labels_any.1, f32[3]{0:T(128)} %diffusivity_any.1), custom_call_target="tpu_custom_call" | custom-call | tf_op jit(solution)/shard_map/pack/pallas_call | solution.py:521
  1.7 0.0 copy-start.3
  1.7 3.0 %collective-permute-start = (f32[2,4,4,8,128]{4,3,2,1,0:T(8,128)S(1)}, f32[2,4,4,8,128]{4,3,2,1,0:T(8,128)S(1)}, u32[]{:S(2)}, u32[]{:S(2)}) collective-permute-start(f32[2,4,4,8,128]{4,3,2,1,0:T(8,128)S(1)} %get-tuple-element.26), channel_id=1, source_target_pairs={{0,16},{16,0},{1,17},{17,1},{2,18},{18,2},{3,19},{19,3},{4,20},{20... | collective-permute-start | bytes 393224 | tf_op jit(solution)/shard_map/ppermute | solution.py:536
  4.7 0.0 copy-done.4
  4.7 0.7 %roots.1 = (f32[8,8,128]{2,1,0:T(8,128)S(1)}, f32[8,8,128]{2,1,0:T(8,128)S(1)}, f32[8,8,128]{2,1,0:T(8,128)S(1)}, f32[8,8,128]{2,1,0:T(8,128)S(1)}) custom-call(f32[8,128]{1,0:T(8,128)S(1)} %copy-done.4, f32[8]{0:T(128)} %eigen_ref.1), custom_call_target="tpu_custom_call" | custom-call | tf_op jit(solution)/shard_map/roots/pallas_call | solution.py:537
  5.5 2.8 %collective-permute-done.refs_1_ = f32[2,4,4,8,128]{4,3,2,1,0:T(8,128)S(1)} collective-permute-done((f32[2,4,4,8,128]{4,3,2,1,0:T(8,128)S(1)}, f32[2,4,4,8,128]{4,3,2,1,0:T(8,128)S(1)}, u32[]{:S(2)}, u32[]{:S(2)}) %collective-permute-start) | collective-permute-done | bytes 131104 | tf_op jit(solution)/shard_map/ppermute | solution.py:536
  8.2 0.0 copy-done.1
  8.2 0.0 copy-done.3
  8.2 0.3 %forward.1 = (f32[17,8,128]{2,1,0:T(8,128)S(1)}, f32[2,8,4,8,128]{4,3,2,1,0:T(8,128)S(1)}) custom-call(f32[2,4,4,8,128]{4,3,2,1,0:T(8,128)S(1)} %get-tuple-element.25.refs_0_, f32[2,4,4,8,128]{4,3,2,1,0:T(8,128)S(1)} %collective-permute-done.refs_1_, bf16[2,256,256]{2,1,0:T(8,128)(2,1)S(1)} %copy-done.1, f32[2,8,128]{2,1,0:T(8,128)S(1)} %copy-done.3, ...), custom_call_target="tpu_custom_call" | custom-call | tf_op jit(solution)/shard_map/forward/pallas_call | solution.py:546
  8.6 0.0 copy-start
  8.6 0.1 collective-permute-start.1
  8.7 1.2 %collective-permute-done.1.other_ref.refs_2_ = f32[17,8,128]{2,1,0:T(8,128)S(1)} collective-permute-done((f32[17,8,128]{2,1,0:T(8,128)S(1)}, f32[17,8,128]{2,1,0:T(8,128)S(1)}, u32[]{:S(2)}, u32[]{:S(2)}) %collective-permute-start.1) | collective-permute-done | bytes 69664 | tf_op jit(solution)/shard_map/ppermute | solution.py:558
  9.9 2.6 %collective-permute-start.4 = (f32[17,8,128]{2,1,0:T(8,128)S(1)}, f32[17,8,128]{2,1,0:T(8,128)S(1)}, u32[]{:S(2)}, u32[]{:S(2)}) collective-permute-start(f32[17,8,128]{2,1,0:T(8,128)S(1)} %join0.1.own_ref), channel_id=1, source_target_pairs={{0,7},{1,6},{2,5},{3,4},{4,3},{5,2},{6,1},{7,0},{8,15},{9,14},{10,... | collective-permute-start | bytes 208904 | tf_op jit(solution)/shard_map/ppermute | solution.py:558
  12.6 0.4 %collective-permute-start.3 = (f32[17,8,128]{2,1,0:T(8,128)S(1)}, f32[17,8,128]{2,1,0:T(8,128)S(1)}, u32[]{:S(2)}, u32[]{:S(2)}) collective-permute-start(f32[17,8,128]{2,1,0:T(8,128)S(1)} %join0.1.own_ref), channel_id=1, source_target_pairs={{0,5},{1,4},{2,7},{3,6},{4,1},{5,0},{6,3},{7,2},{8,13},{9,12},{10,... | collective-permute-start | bytes 208904 | tf_op jit(solution)/shard_map/ppermute | solution.py:558
  13.0 0.2 collective-permute-start.2
  13.2 0.0 copy-done
  13.2 0.3 %local.1 = (f32[8,4,8,128]{3,2,1,0:T(8,128)S(1)}, f32[8,4,8,128]{3,2,1,0:T(8,128)S(1)}) custom-call(f32[2,8,4,8,128]{4,3,2,1,0:T(8,128)S(1)} %get-tuple-element.38.local_ref, f32[8,8,128]{2,1,0:T(8,128)S(1)} %get-tuple-element.27.refs_4_.decay_ref.refs_6_, f32[8,8,128]{2,1,0:T(8,128)S(1)} %get-tuple-element.28.refs_5_.scale_ref.refs_7_, ...), custom_call_target="tpu_custom_call" | custom-call | tf_op jit(solution)/shard_map/local/pallas_call | solution.py:589
  13.5 1.6 %collective-permute-start.7 = (f32[8,4,8,128]{3,2,1,0:T(8,128)S(1)}, f32[8,4,8,128]{3,2,1,0:T(8,128)S(1)}, u32[]{:S(2)}, u32[]{:S(2)}) collective-permute-start(f32[8,4,8,128]{3,2,1,0:T(8,128)S(1)} %get-tuple-element.40), channel_id=1, source_target_pairs={{0,16},{16,0},{1,17},{17,1},{2,18},{18,2},{3,19},{19,3},{4,20},{20... | collective-permute-start | bytes 393224 | tf_op jit(solution)/shard_map/ppermute | solution.py:596
  15.1 0.0 collective-permute-done.4.cross_ref
  15.1 1.7 %collective-permute-done.3.far_ref = f32[17,8,128]{2,1,0:T(8,128)S(1)} collective-permute-done((f32[17,8,128]{2,1,0:T(8,128)S(1)}, f32[17,8,128]{2,1,0:T(8,128)S(1)}, u32[]{:S(2)}, u32[]{:S(2)}) %collective-permute-start.3) | collective-permute-done | bytes 69664 | tf_op jit(solution)/shard_map/ppermute | solution.py:558
  16.9 0.2 collective-permute-done.2.near_ref.refs_3_
  17.1 0.1 join1.1
  17.2 2.7 %collective-permute-start.5 = (f32[9,8,128]{2,1,0:T(8,128)S(1)}, f32[9,8,128]{2,1,0:T(8,128)S(1)}, u32[]{:S(2)}, u32[]{:S(2)}) collective-permute-start(f32[9,8,128]{2,1,0:T(8,128)S(1)} %get-tuple-element.30.refs_5_.edge_ref), channel_id=1, source_target_pairs={{0,9},{1,8},{2,11},{3,10},{4,13},{5,12},{6,15},{7,14},{8,1},{9,0},... | collective-permute-start | bytes 110600 | tf_op jit(solution)/shard_map/ppermute | solution.py:558
  19.9 0.1 near_side.1
  20.0 1.5 %collective-permute-done.5.other_ref = f32[9,8,128]{2,1,0:T(8,128)S(1)} collective-permute-done((f32[9,8,128]{2,1,0:T(8,128)S(1)}, f32[9,8,128]{2,1,0:T(8,128)S(1)}, u32[]{:S(2)}, u32[]{:S(2)}) %collective-permute-start.5) | collective-permute-done | bytes 36896 | tf_op jit(solution)/shard_map/ppermute | solution.py:558
  21.6 1.6 %collective-permute-start.6 = (f32[17,8,128]{2,1,0:T(8,128)S(1)}, f32[17,8,128]{2,1,0:T(8,128)S(1)}, u32[]{:S(2)}, u32[]{:S(2)}) collective-permute-start(f32[17,8,128]{2,1,0:T(8,128)S(1)} %get-tuple-element.37), channel_id=1, source_target_pairs={{0,17},{1,16},{2,19},{3,18},{4,21},{5,20},{6,23},{7,22},{8,25},{9,... | collective-permute-start | bytes 208904 | tf_op jit(solution)/shard_map/ppermute | solution.py:614
  23.9 0.0 copy-start.2
  23.9 0.3 %own.1.refs_2_ = f32[8,4,8,128]{3,2,1,0:T(8,128)S(1)} custom-call(f32[17,8,128]{2,1,0:T(8,128)S(1)} %get-tuple-element.36.entering_ref.refs_0_, f32[8,8,128]{2,1,0:T(8,128)S(1)} %get-tuple-element.27.refs_4_.decay_ref.refs_6_, f32[8,8,128]{2,1,0:T(8,128)S(1)} %get-tuple-element.28.refs_5_.scale_ref.refs_7_, bf16[2,256,256]{2,1,0:T(8,128)(2,1)S(1)} %copy-done, ...), custom_call_target="tpu_custom_call" | custom-call | tf_op jit(solution)/shard_map/own/pallas_call | solution.py:615
  24.2 0.0 collective-permute-done.7.refs_3_
  24.2 1.4 %collective-permute-done.6.refs_1_ = f32[17,8,128]{2,1,0:T(8,128)S(1)} collective-permute-done((f32[17,8,128]{2,1,0:T(8,128)S(1)}, f32[17,8,128]{2,1,0:T(8,128)S(1)}, u32[]{:S(2)}, u32[]{:S(2)}) %collective-permute-start.6) | collective-permute-done | bytes 69664 | tf_op jit(solution)/shard_map/ppermute | solution.py:614
  25.6 0.0 copy-done.2
  25.6 1.3 %finish.1 = (f32[8,2,8,512]{3,2,1,0:T(8,128)}, f32[8,2,8,512]{3,2,1,0:T(8,128)}, f32[1,1]{1,0:T(1,128)}) custom-call(f32[17,8,128]{2,1,0:T(8,128)S(1)} %get-tuple-element.36.entering_ref.refs_0_, f32[17,8,128]{2,1,0:T(8,128)S(1)} %collective-permute-done.6.refs_1_, f32[8,4,8,128]{3,2,1,0:T(8,128)S(1)} %own.1.refs_2_, ...), custom_call_target="tpu_custom_call" | custom-call | tf_op jit(solution)/shard_map/finish/pallas_call | solution.py:623
  (2 shorter events, 0.1 us)
Async XLA Ops:
  0.6 7.6 %copy-start.1 = (bf16[2,256,256]{2,1,0:T(8,128)(2,1)S(1)}, bf16[2,256,256]{2,1,0:T(8,128)(2,1)}, u32[]{:S(2)}) copy-start(bf16[2,256,256]{2,1,0:T(8,128)(2,1)} %constant.9.clone.refs_2_) | copy-start | bytes 786436
  0.6 4.1 %copy-start.4 = (f32[8,128]{1,0:T(8,128)S(1)}, f32[8,128]{1,0:T(8,128)}, u32[]{:S(2)}) copy-start(f32[8,128]{1,0:T(8,128)} %constant.8.clone.y_eigen_ref) | copy-start | bytes 12292
  1.7 6.5 %copy-start.3 = (f32[2,8,128]{2,1,0:T(8,128)S(1)}, f32[2,8,128]{2,1,0:T(8,128)}, u32[]{:S(2)}) copy-start(f32[2,8,128]{2,1,0:T(8,128)} %constant.10.clone.refs_3_.twiddle_ref.refs_9_) | copy-start | bytes 24580
  1.7 6.5 %collective-permute-start = (f32[2,4,4,8,128]{4,3,2,1,0:T(8,128)S(1)}, f32[2,4,4,8,128]{4,3,2,1,0:T(8,128)S(1)}, u32[]{:S(2)}, u32[]{:S(2)}) collective-permute-start(f32[2,4,4,8,128]{4,3,2,1,0:T(8,128)S(1)} %get-tuple-element.26), channel_id=1, source_target_pairs={{0,16},{16,0},{1,17},{17,1},{2,18},{18,2},{3,19},{19,3},{4,20},{20... | collective-permute-start | bytes 393224 | tf_op jit(solution)/shard_map/ppermute | solution.py:536
  8.6 4.6 %copy-start = (bf16[2,256,256]{2,1,0:T(8,128)(2,1)S(1)}, bf16[2,256,256]{2,1,0:T(8,128)(2,1)}, u32[]{:S(2)}) copy-start(bf16[2,256,256]{2,1,0:T(8,128)(2,1)} %constant.11.clone.lane_ref.refs_8_) | copy-start | bytes 786436
  8.6 1.3 %collective-permute-start.1 = (f32[17,8,128]{2,1,0:T(8,128)S(1)}, f32[17,8,128]{2,1,0:T(8,128)S(1)}, u32[]{:S(2)}, u32[]{:S(2)}) collective-permute-start(f32[17,8,128]{2,1,0:T(8,128)S(1)} %get-tuple-element.29.own_ref.refs_1_), channel_id=1, source_target_pairs={{0,1},{1,0},{2,3},{3,2},{4,5},{5,4},{6,7},{7,6},{8,9},{9,8},{10,11... | collective-permute-start | bytes 208904 | tf_op jit(solution)/shard_map/ppermute | solution.py:558
  9.9 5.2 %collective-permute-start.4 = (f32[17,8,128]{2,1,0:T(8,128)S(1)}, f32[17,8,128]{2,1,0:T(8,128)S(1)}, u32[]{:S(2)}, u32[]{:S(2)}) collective-permute-start(f32[17,8,128]{2,1,0:T(8,128)S(1)} %join0.1.own_ref), channel_id=1, source_target_pairs={{0,7},{1,6},{2,5},{3,4},{4,3},{5,2},{6,1},{7,0},{8,15},{9,14},{10,... | collective-permute-start | bytes 208904 | tf_op jit(solution)/shard_map/ppermute | solution.py:558
  12.6 4.3 %collective-permute-start.3 = (f32[17,8,128]{2,1,0:T(8,128)S(1)}, f32[17,8,128]{2,1,0:T(8,128)S(1)}, u32[]{:S(2)}, u32[]{:S(2)}) collective-permute-start(f32[17,8,128]{2,1,0:T(8,128)S(1)} %join0.1.own_ref), channel_id=1, source_target_pairs={{0,5},{1,4},{2,7},{3,6},{4,1},{5,0},{6,3},{7,2},{8,13},{9,12},{10,... | collective-permute-start | bytes 208904 | tf_op jit(solution)/shard_map/ppermute | solution.py:558
  13.0 4.1 %collective-permute-start.2 = (f32[17,8,128]{2,1,0:T(8,128)S(1)}, f32[17,8,128]{2,1,0:T(8,128)S(1)}, u32[]{:S(2)}, u32[]{:S(2)}) collective-permute-start(f32[17,8,128]{2,1,0:T(8,128)S(1)} %join0.1.own_ref), channel_id=1, source_target_pairs={{0,3},{1,2},{2,1},{3,0},{4,7},{5,6},{6,5},{7,4},{8,11},{9,10},{10,... | collective-permute-start | bytes 208904 | tf_op jit(solution)/shard_map/ppermute | solution.py:558
  13.5 10.7 %collective-permute-start.7 = (f32[8,4,8,128]{3,2,1,0:T(8,128)S(1)}, f32[8,4,8,128]{3,2,1,0:T(8,128)S(1)}, u32[]{:S(2)}, u32[]{:S(2)}) collective-permute-start(f32[8,4,8,128]{3,2,1,0:T(8,128)S(1)} %get-tuple-element.40), channel_id=1, source_target_pairs={{0,16},{16,0},{1,17},{17,1},{2,18},{18,2},{3,19},{19,3},{4,20},{20... | collective-permute-start | bytes 393224 | tf_op jit(solution)/shard_map/ppermute | solution.py:596
  17.2 4.4 %collective-permute-start.5 = (f32[9,8,128]{2,1,0:T(8,128)S(1)}, f32[9,8,128]{2,1,0:T(8,128)S(1)}, u32[]{:S(2)}, u32[]{:S(2)}) collective-permute-start(f32[9,8,128]{2,1,0:T(8,128)S(1)} %get-tuple-element.30.refs_5_.edge_ref), channel_id=1, source_target_pairs={{0,9},{1,8},{2,11},{3,10},{4,13},{5,12},{6,15},{7,14},{8,1},{9,0},... | collective-permute-start | bytes 110600 | tf_op jit(solution)/shard_map/ppermute | solution.py:558
  21.6 4.0 %collective-permute-start.6 = (f32[17,8,128]{2,1,0:T(8,128)S(1)}, f32[17,8,128]{2,1,0:T(8,128)S(1)}, u32[]{:S(2)}, u32[]{:S(2)}) collective-permute-start(f32[17,8,128]{2,1,0:T(8,128)S(1)} %get-tuple-element.37), channel_id=1, source_target_pairs={{0,17},{1,16},{2,19},{3,18},{4,21},{5,20},{6,23},{7,22},{8,25},{9,... | collective-permute-start | bytes 208904 | tf_op jit(solution)/shard_map/ppermute | solution.py:614
  23.9 1.7 %copy-start.2 = (f32[8,2,8,512]{3,2,1,0:T(8,128)S(1)}, f32[8,2,8,512]{3,2,1,0:T(8,128)}, u32[]{:S(2)}) copy-start(f32[8,2,8,512]{3,2,1,0:T(8,128)} %refs_11_.1) | copy-start | bytes 786436
